TPU v7x, 128 devices: a whole 4x4x4 slice. The times are simulated.
128 devices in a mesh: machine: 32 (over x, z, core), local: 4 (over y).
Axes of the slice: x: 4, y: 4, z: 4, core: 2. Of those that a mesh axis runs over, the one named last changes fastest.
Arguments:
- features: bfloat16 [262144, 768], P(('machine', 'local')), may hold values from -6 to 6
- w_self: bfloat16 [768, 256], replicated, may hold values from -0.21875 to 0.21875
- w_neigh: bfloat16 [768, 256], replicated, may hold values from -0.875 to 0.875
- mirror_master_part: int32 [65536, 1], P(('machine', 'local')), may hold values from 0 to 127; in each aligned block of 512 rows (0 to 511, 512 to 1023, ...) at most 8 rows name the same one
- mirror_row: int32 [65536], P(('machine', 'local')), may hold values from 0 to 2047
- tile_count: int32 [2560], P(('machine', 'local')), may hold values from 1 to 16, as said below
- tile_column: int32 [2560, 16], P(('machine', 'local')), may hold values from 0 to 19
- tile_weight: bfloat16 [2560, 16, 128, 128], P(('machine', 'local')), may hold values from 0 to 1, as said below
- cotangent: bfloat16 [262144, 256], P(('machine', 'local')), may hold values from -0.01171875 to 0.01171875
Outputs:
- mixed: bfloat16 [262144, 256], P(('machine', 'local'))
- grad_features: bfloat16 [262144, 768], P(('machine', 'local'))
- grad_self: float32 [768, 256], replicated
- grad_neigh: float32 [768, 256], replicated
Inputs may be any that keep to these rules, and one draw needn't show every extreme that they name: `mirror_master_part`: among the 512 mirrors of one partition at most 8 have their master on any one partition, and in every draw some partition reaches 8. `tile_count`: every partition has a row block with 16 tiles. `tile_weight`: edge weights are nonnegative.
All inputs are finite; a program needn't handle non-finite values.
Results may differ from a plain program's by a relative error of at most 0.0053.
Values may be sent and summed in bfloat16 or wider, within the bound.
No kernel may reach another device: no remote copies, remote signals or barrier semaphores. Data moves between devices by JAX's collectives and lax.ppermute only.
A program may use at most 192 MiB of HBM per device.

v0:
```python
import jax
import jax.numpy as jnp
from jax import lax
from jax.sharding import PartitionSpec as P


def activate(value):
    return jax.nn.gelu(value, approximate=True)


def carry_values(buffer, partition_list, capacity):
    width = buffer.shape[1]
    moved = lax.all_to_all(
        buffer.reshape(partition_list, capacity, width),
        ("machine", "local"),
        split_axis=0,
        concat_axis=0,
        tiled=True,
    )
    return moved.reshape(buffer.shape)


def return_sums(rows, degree, partition_list, capacity):
    width = rows.shape[1]
    moved_rows, moved_degree = (
        lax.all_to_all(
            rows.reshape(partition_list, capacity, width),
            ("machine", "local"),
            split_axis=0,
            concat_axis=0,
            tiled=True,
        ),
        lax.all_to_all(
            degree.reshape(partition_list, capacity),
            ("machine", "local"),
            split_axis=0,
            concat_axis=0,
            tiled=True,
        ),
    )
    return (moved_rows.reshape(rows.shape), moved_degree.reshape(degree.shape))


def return_grads(rows, partition_list, capacity):
    width = rows.shape[1]
    moved = lax.all_to_all(
        rows.reshape(partition_list, capacity, width),
        ("machine", "local"),
        split_axis=0,
        concat_axis=0,
        tiled=True,
    )
    return moved.reshape(rows.shape)


def masked_tiles(tile_weight, tile_count):
    tiles_max = tile_weight.shape[1]
    used = (jnp.arange(tiles_max, dtype=jnp.int32)[None, :] < tile_count[:, None]).astype(
        tile_weight.dtype
    )
    return tile_weight * used[:, :, None, None]


def aggregate_tiles(tiles, tile_column, slab):
    row_blocks = tiles.shape[0]
    edge = tiles.shape[2]
    width = slab.shape[1]
    blocks = slab.reshape(row_blocks, edge, width)
    picked = blocks[tile_column]
    partial_value = jnp.einsum("btij,btjf->bif", tiles, picked, preferred_element_type=jnp.float32)
    degree = jnp.sum(tiles, axis=(1, 3), dtype=jnp.float32)
    return (partial_value.reshape(row_blocks * edge, width), degree.reshape(row_blocks * edge))


def spread_tiles(tiles, tile_column, d_slab):
    row_blocks = tiles.shape[0]
    edge = tiles.shape[2]
    width = d_slab.shape[1]
    rows_here = d_slab.reshape(row_blocks, edge, width)
    contrib = jnp.einsum("btij,bif->btjf", tiles, rows_here, preferred_element_type=jnp.float32)
    placing = (
        tile_column[:, :, None] == jnp.arange(row_blocks, dtype=jnp.int32)[None, None, :]
    ).astype(jnp.float32)
    grads = jnp.einsum("btc,btjf->cjf", placing, contrib, precision=lax.Precision.HIGHEST)
    return grads.reshape(row_blocks * edge, width)


def on_device(
    features,
    w_self,
    w_neigh,
    mirror_master_part,
    mirror_row,
    tile_count,
    tile_column,
    tile_weight,
    cotangent,
):
    masters = features.shape[0]
    mirrors = mirror_row.shape[0]
    width = w_neigh.shape[1]
    partition_list = lax.axis_size("machine") * lax.axis_size("local")
    capacity = 2 * mirrors // partition_list
    peer = mirror_master_part[:, 0]
    member = (peer[:, None] == jnp.arange(partition_list, dtype=jnp.int32)[None, :]).astype(
        jnp.int32
    )
    ranking = jnp.sum(member * (jnp.cumsum(member, axis=0) - 1), axis=1)
    places = peer * capacity + ranking
    wanted = jnp.zeros((partition_list * capacity,), jnp.int32).at[places].set(mirror_row)
    present = jnp.zeros((partition_list * capacity,), jnp.int32).at[places].set(1)
    asked, alive = (
        lax.all_to_all(
            wanted.reshape(partition_list, capacity),
            ("machine", "local"),
            split_axis=0,
            concat_axis=0,
            tiled=True,
        ),
        lax.all_to_all(
            present.reshape(partition_list, capacity),
            ("machine", "local"),
            split_axis=0,
            concat_axis=0,
            tiled=True,
        ),
    )
    asked = asked.reshape(-1)
    alive = alive.reshape(-1).astype(jnp.float32)
    tiles = masked_tiles(tile_weight, tile_count)
    projected = jnp.dot(features, w_neigh, preferred_element_type=jnp.float32).astype(jnp.bfloat16)
    arrived = carry_values(projected[asked], partition_list, capacity)
    slab = jnp.concatenate([projected, arrived[places]], axis=0)
    partial_value, degree_part = aggregate_tiles(tiles, tile_column, slab)
    send_rows = (
        jnp.zeros((partition_list * capacity, width), jnp.float32)
        .at[places]
        .set(partial_value[masters:])
    )
    send_degree = (
        jnp.zeros((partition_list * capacity,), jnp.float32).at[places].set(degree_part[masters:])
    )
    back_rows, back_degree = return_sums(send_rows, send_degree, partition_list, capacity)
    aggregate = partial_value[:masters].at[asked].add(back_rows * alive[:, None])
    degree = degree_part[:masters].at[asked].add(back_degree * alive)
    scale = 1.0 / (1.0 + degree)
    pre = jnp.dot(features, w_self, preferred_element_type=jnp.float32) + aggregate * scale[:, None]
    result, pullback = jax.vjp(activate, pre)
    mixed = result.astype(jnp.bfloat16)
    d_pre = pullback(cotangent.astype(jnp.float32))[0]
    d_pre_low = d_pre.astype(jnp.bfloat16)
    d_aggregate = (d_pre * scale[:, None]).astype(jnp.bfloat16)
    d_arrived = carry_values(d_aggregate[asked], partition_list, capacity)
    d_slab = jnp.concatenate([d_aggregate, d_arrived[places]], axis=0)
    d_partial = spread_tiles(tiles, tile_column, d_slab)
    send_grads = (
        jnp.zeros((partition_list * capacity, width), jnp.float32)
        .at[places]
        .set(d_partial[masters:])
    )
    back_grads = return_grads(send_grads, partition_list, capacity)
    d_projected = (
        d_partial[:masters].at[asked].add(back_grads * alive[:, None]).astype(jnp.bfloat16)
    )
    grad_features = (
        jnp.dot(d_pre_low, w_self.T, preferred_element_type=jnp.float32)
        + jnp.dot(d_projected, w_neigh.T, preferred_element_type=jnp.float32)
    ).astype(jnp.bfloat16)
    local_self = lax.dot_general(
        features, d_pre_low, (((0,), (0,)), ((), ())), preferred_element_type=jnp.float32
    )
    local_neigh = lax.dot_general(
        features, d_projected, (((0,), (0,)), ((), ())), preferred_element_type=jnp.float32
    )
    grad_self, grad_neigh = lax.psum((local_self, local_neigh), ("machine", "local"))
    return (mixed, grad_features, grad_self, grad_neigh)


def solution(mesh):
    placed = (
        P(("machine", "local"), None),
        P(),
        P(),
        P(("machine", "local"), None),
        P(("machine", "local")),
        P(("machine", "local")),
        P(("machine", "local"), None),
        P(("machine", "local"), None, None, None),
        P(("machine", "local"), None),
    )
    return jax.shard_map(
        on_device,
        mesh=mesh,
        in_specs=placed,
        out_specs=(P(("machine", "local"), None), P(("machine", "local"), None), P(), P()),
        check_vma=False,
    )
```

profile of v0, /device:TPU:1, one launch (start us, length us, event | category | flops | bytes accessed | tf_op | source)
XLA Modules:
  0.0 465.2 jit_solution(14525108013919602223)
XLA Ops:
  10.1 2.6 scatter_custom_fusion
  13.4 11.5 %all-to-all-start = ((s32[128,1,8]{2,1,0:T(1,128)}), s32[128,1,8]{2,1,0:T(1,128)S(1)}, u32[]{:S(2)}, u32[]{:S(2)}) async-start(s32[128,1,8]{2,1,0:T(1,128)} %bitcast.7), calls=%async_computation | async-start | bytes 131072 | tf_op jit(solution)/shard_map/all_to_all | solution.py:113
  25.6 6.5 %convert_reduce_fusion = f32[20,128]{1,0:T(8,128)S(1)} fusion(bf16[20,16,128,128]{3,2,1,0:T(8,128)(2,1)} %param.16, bf16[20,16]{1,0:T(8,128)(2,1)S(1)} %fusion.43), kind=kLoop, calls=%fused_computation.15 | loop fusion | flops 15726080 | bytes 10496640 | tf_op jit(solution)/shard_map/reduce_sum | solution.py:71
  36.2 6.0 %gather_fusion = bf16[1024,256]{1,0:T(8,128)(2,1)} fusion(bf16[2048,256]{1,0:T(8,128)(2,1)} %convolution_convert_fusion, s32[1024]{0:T(1024)S(1)} %broadcast_clamp_fusion), kind=kCustom, calls=%fused_computation | custom fusion | bytes 1052672 | tf_op jit(solution)/shard_map/gather | solution.py:132
  42.2 9.6 %all-to-all-start.1 = ((bf16[128,8,256]{2,1,0:T(8,128)(2,1)}), bf16[128,8,256]{2,1,0:T(8,128)(2,1)}, u32[]{:S(2)}, u32[]{:S(2)}) async-start(bf16[128,8,256]{2,1,0:T(8,128)(2,1)} %bitcast.74), calls=%async_computation.1 | async-start | bytes 1048576 | tf_op jit(solution)/shard_map/all_to_all | solution.py:13
  58.3 7.2 %all-to-all-done.1 = bf16[128,8,256]{2,1,0:T(8,128)(2,1)} async-done(((bf16[128,8,256]{2,1,0:T(8,128)(2,1)}), bf16[128,8,256]{2,1,0:T(8,128)(2,1)}, u32[]{:S(2)}, u32[]{:S(2)}) %all-to-all-start.1) | async-done | bytes 524320 | tf_op jit(solution)/shard_map/all_to_all | solution.py:13
  65.6 3.9 all-to-all-start.3
  69.5 2.7 gather_fusion.1
  74.6 12.6 %gather_fusion.2 = bf16[320,128,256]{2,1,0:T(8,128)(2,1)} fusion(bf16[20,128,256]{2,1,0:T(8,128)(2,1)} %bitcast.66, s32[1024]{0:T(1024)S(1)} %pad_clamp_fusion), kind=kCustom, calls=%fused_computation.2 | custom fusion | bytes 41944320 | tf_op jit(solution)/shard_map/gather | solution.py:69
  87.2 9.9 %all-to-all-start.4 = ((f32[128,1,8]{2,1,0:T(1,128)}), f32[128,1,8]{2,1,0:T(1,128)S(1)}, u32[]{:S(2)}, u32[]{:S(2)}) async-start(f32[128,1,8]{2,1,0:T(1,128)} %bitcast.22), calls=%async_computation.4 | async-start | bytes 131072 | tf_op jit(solution)/shard_map/all_to_all | solution.py:33
  97.1 14.9 %fusion.20 = f32[20,128,256]{2,1,0:T(8,128)} fusion(bf16[20,16,128,256]{3,2,1,0:T(8,128)(2,1)} %bitcast.67, bf16[20,16,128,128]{3,2,1,0:T(8,128)(2,1)} %param.16, bf16[20,16]{1,0:T(8,128)(2,1)S(1)} %fusion.43), kind=kOutput, calls=%fused_computation.41 | convolution fusion | flops 2689597440 | bytes 34079360 | tf_op jit(solution)/shard_map/btij,btjf->bif/dot_general | solution.py:70
  113.8 3.7 scatter_custom_fusion.1
  117.5 10.2 %all-to-all-start.2 = ((f32[128,8,256]{2,1,0:T(8,128)}), f32[128,8,256]{2,1,0:T(8,128)}, u32[]{:S(2)}, u32[]{:S(2)}) async-start(f32[128,8,256]{2,1,0:T(8,128)} %bitcast.71), calls=%async_computation.2 | async-start | bytes 2097152 | tf_op jit(solution)/shard_map/all_to_all | solution.py:26
  129.5 7.3 %scatter_fusion = f32[2048]{0:T(1024)S(1)} fusion(f32[2048]{0:T(1024)S(1)} %fusion.44, s32[1024]{0:T(1024)S(1)} %bitcast.79, f32[1024]{0:T(1024)S(1)} %mul.100), kind=kCustom, calls=%fused_computation.10 | custom fusion | flops 1024 | bytes 16384 | tf_op jit(solution)/shard_map/scatter-add | solution.py:145
  136.8 3.1 slice.64
  139.9 7.2 %all-to-all-done.2 = f32[128,8,256]{2,1,0:T(8,128)} async-done(((f32[128,8,256]{2,1,0:T(8,128)}), f32[128,8,256]{2,1,0:T(8,128)}, u32[]{:S(2)}, u32[]{:S(2)}) %all-to-all-start.2) | async-done | bytes 1048608 | tf_op jit(solution)/shard_map/all_to_all | solution.py:26
  147.2 9.9 %scatter_custom_fusion.3 = f32[2048,256]{1,0:T(8,128)} fusion(f32[2048,256]{1,0:T(8,128)} %bitcast.73, s32[1024]{0:T(1024)S(1)} %bitcast.80, f32[128,8,256]{2,1,0:T(8,128)} %all-to-all-done.2, f32[1024]{0:T(1024)S(1)} %convert_element_type.51), kind=kCustom, calls=%fused_computation.49 | custom fusion | flops 524288 | bytes 3149824 | tf_op jit(solution)/shard_map/scatter-add | solution.py:144
  157.1 5.3 %multiply_convert_fusion = (bf16[2048,256]{1,0:T(8,128)(2,1)}, bf16[2048,256]{1,0:T(8,128)(2,1)}, f32[2048,256]{1,0:T(8,128)}) fusion(f32[2048]{0:T(1024)S(1)} %broadcast_divide_fusion, bf16[2048,256]{1,0:T(8,128)(2,1)} %param.17, f32[2048,256]{1,0:T(8,128)} %scatter_custom_fusion.3, bf16[2048,768]{1,0:T(8,128)(2,1)S(1)} %copy-done, bf16[768,256]{1,0:T(8,128)(2,1)} %param.10), kind=kOutput, calls=%fused_computation.38 | convolution fusion | flops 818937856 | bytes 10887168 | tf_op jit(solution)/shard_map/dot_general | solution.py:147
  162.4 6.0 %gather_fusion.3 = bf16[1024,256]{1,0:T(8,128)(2,1)} fusion(bf16[2048,256]{1,0:T(8,128)(2,1)} %get-tuple-element.18, s32[1024]{0:T(1024)S(1)} %broadcast_clamp_fusion), kind=kCustom, calls=%fused_computation.3 | custom fusion | bytes 1052672 | tf_op jit(solution)/shard_map/gather | solution.py:153
  168.4 18.9 %all_to_all.47 = bf16[128,8,256]{2,1,0:T(8,128)(2,1)} all-to-all(bf16[128,8,256]{2,1,0:T(8,128)(2,1)} %bitcast.75), channel_id=1, replica_groups=mesh['machine'=32,'local'=4] {'machine','local'}, dimensions={0} | all-to-all | bytes 1048576 | tf_op jit(solution)/shard_map/all_to_all | solution.py:13
  187.3 2.7 gather_fusion.4
  191.3 19.8 %fusion.2 = f32[20,16,128,256]{3,2,1,0:T(8,128)} fusion(bf16[20,128,256,1]{2,1,3,0:T(8,128)(2,1)S(1)} %bitcast.70, bf16[20,16,128,128]{3,2,1,0:T(8,128)(2,1)} %param.16, bf16[20,16]{1,0:T(8,128)(2,1)S(1)} %fusion.43), kind=kOutput, calls=%fused_computation.16 | convolution fusion | flops 2689597440 | bytes 53740160 | tf_op jit(solution)/shard_map/btij,bif->btjf/dot_general | solution.py:80
  211.0 53.6 %fusion.17 = f32[20,128,256]{2,0,1:T(8,128)S(1)} fusion(f32[20,16,128,256]{3,2,1,0:T(8,128)} %fusion.2, s32[20,16]{0,1:T(8,128)S(1)} %copy-done.5), kind=kOutput, calls=%fused_computation.40 | convolution fusion | flops 2516588800 | bytes 44565760 | tf_op jit(solution)/shard_map/btc,btjf->cjf/dot_general | solution.py:84
  267.3 3.8 scatter_custom_fusion.6
  271.1 4.7 %all-to-all-start.6 = ((f32[128,8,256]{2,1,0:T(8,128)}), f32[128,8,256]{2,1,0:T(8,128)}, u32[]{:S(2)}, u32[]{:S(2)}) async-start(f32[128,8,256]{2,1,0:T(8,128)} %bitcast.72), calls=%async_computation.6 | async-start | bytes 2097152 | tf_op jit(solution)/shard_map/all_to_all | solution.py:46
  275.9 4.6 convolution_bitcast_fusion.1
  284.6 10.8 %all-to-all-done.6 = f32[128,8,256]{2,1,0:T(8,128)} async-done(((f32[128,8,256]{2,1,0:T(8,128)}), f32[128,8,256]{2,1,0:T(8,128)}, u32[]{:S(2)}, u32[]{:S(2)}) %all-to-all-start.6) | async-done | bytes 1048608 | tf_op jit(solution)/shard_map/all_to_all | solution.py:46
  295.4 10.1 %scatter_custom_fusion.7 = f32[2048,256]{1,0:T(8,128)} fusion(f32[2048,256]{1,0:T(8,128)} %bitcast.68, s32[1024]{0:T(1024)S(1)} %bitcast.81, f32[128,8,256]{2,1,0:T(8,128)} %all-to-all-done.6, f32[1024]{0:T(1024)S(1)} %convert_element_type.51), kind=kCustom, calls=%fused_computation.47 | custom fusion | flops 524288 | bytes 3149824 | tf_op jit(solution)/shard_map/scatter-add | solution.py:163
  305.5 3.5 convolution_bitcast_fusion
  309.1 4.2 fusion.28
  313.4 2.7 add_convert_fusion
  316.1 137.2 %all-reduce.3.cloned.1.call-done = (f32[768,256]{0,1:T(8,128)}, f32[768,256]{0,1:T(8,128)}) async-done(((f32[768,256]{0,1:T(8,128)}, f32[768,256]{0,1:T(8,128)}), (f32[768,256]{0,1:T(8,128)}, f32[768,256]{0,1:T(8,128)})) %all-reduce.3.cloned.1.call-update) | async-done | bytes 1572880 | tf_op jit(solution)/shard_map/psum | solution.py:175
  (65 shorter events, 33.5 us)
Async XLA Ops:
  7.2 25.0 %copy-start = (bf16[2048,768]{1,0:T(8,128)(2,1)S(1)}, bf16[2048,768]{1,0:T(8,128)(2,1)}, u32[]{:S(2)}) copy-start(bf16[2048,768]{1,0:T(8,128)(2,1)} %param.9) | copy-start | bytes 9437188
  13.4 21.3 %all-to-all-start = ((s32[128,1,8]{2,1,0:T(1,128)}), s32[128,1,8]{2,1,0:T(1,128)S(1)}, u32[]{:S(2)}, u32[]{:S(2)}) async-start(s32[128,1,8]{2,1,0:T(1,128)} %bitcast.7), calls=%async_computation | async-start | bytes 131072 | tf_op jit(solution)/shard_map/all_to_all | solution.py:113
  25.6 6.5 %copy-start.3 = (bf16[768,256]{1,0:T(8,128)(2,1)S(1)}, bf16[768,256]{1,0:T(8,128)(2,1)}, u32[]{:S(2)}) copy-start(bf16[768,256]{1,0:T(8,128)(2,1)} %param.11) | copy-start | bytes 1179652
  36.2 15.6 %copy-start.5 = (s32[20,16]{0,1:T(8,128)S(1)}, s32[20,16]{0,1:T(8,128)}, u32[]{:S(2)}) copy-start(s32[20,16]{0,1:T(8,128)} %param.15) | copy-start | bytes 3844
  42.2 23.4 %all-to-all-start.1 = ((bf16[128,8,256]{2,1,0:T(8,128)(2,1)}), bf16[128,8,256]{2,1,0:T(8,128)(2,1)}, u32[]{:S(2)}, u32[]{:S(2)}) async-start(bf16[128,8,256]{2,1,0:T(8,128)(2,1)} %bitcast.74), calls=%async_computation.1 | async-start | bytes 1048576 | tf_op jit(solution)/shard_map/all_to_all | solution.py:13
  65.6 21.6 %all-to-all-start.3 = ((s32[128,1,8]{2,1,0:T(1,128)}), s32[128,1,8]{2,1,0:T(1,128)S(1)}, u32[]{:S(2)}, u32[]{:S(2)}) async-start(s32[128,1,8]{2,1,0:T(1,128)} %bitcast.19), calls=%async_computation.3 | async-start | bytes 131072 | tf_op jit(solution)/shard_map/all_to_all | solution.py:120
  87.2 30.4 %all-to-all-start.4 = ((f32[128,1,8]{2,1,0:T(1,128)}), f32[128,1,8]{2,1,0:T(1,128)S(1)}, u32[]{:S(2)}, u32[]{:S(2)}) async-start(f32[128,1,8]{2,1,0:T(1,128)} %bitcast.22), calls=%async_computation.4 | async-start | bytes 131072 | tf_op jit(solution)/shard_map/all_to_all | solution.py:33
  117.5 29.6 %all-to-all-start.2 = ((f32[128,8,256]{2,1,0:T(8,128)}), f32[128,8,256]{2,1,0:T(8,128)}, u32[]{:S(2)}, u32[]{:S(2)}) async-start(f32[128,8,256]{2,1,0:T(8,128)} %bitcast.71), calls=%async_computation.2 | async-start | bytes 2097152 | tf_op jit(solution)/shard_map/all_to_all | solution.py:26
  264.7 1.7 copy-start.2
  271.1 24.3 %all-to-all-start.6 = ((f32[128,8,256]{2,1,0:T(8,128)}), f32[128,8,256]{2,1,0:T(8,128)}, u32[]{:S(2)}, u32[]{:S(2)}) async-start(f32[128,8,256]{2,1,0:T(8,128)} %bitcast.72), calls=%async_computation.6 | async-start | bytes 2097152 | tf_op jit(solution)/shard_map/all_to_all | solution.py:46
  275.8 177.5 %all-reduce.3.cloned.1.call-start = ((), (), s32[]{:S(2)}) async-start(), calls=%async_computation.7 | async-start | bytes 3145728 | tf_op jit(solution)/shard_map/psum | solution.py:175
  280.4 1.6 slice-start
  305.5 3.6 copy-start.6
  309.1 4.3 copy-start.1
  309.1 4.3 copy-start.4
Sparse Core Ops, SparseCore 0:
  309.2 144.0 all-reduce.2
where the time goes:
time: 474 us; the launch traced here: 465 us
  waiting for transfers between devices  163 us (34%)
  matrix products  111 us (23%)
  local copies, waits for them, and re-layouts  65.8 us (14%)
  starting transfers between devices  50 us (11%)
  other arithmetic  42 us (9%)
  blocking collectives  18.9 us (4%)
  between operations  14.8 us (3%)
    psum x1, waiting for transfers between devices, on_device(): lax.psum((local_self, local_neigh), ('machine', 'local'))  137 us
    dot_general x1, matrix products, spread_tiles(): jnp.einsum('btc,btjf->cjf', placing, contrib, precision=lax.Precision.HIG...  53.6 us
    dot_general x1, matrix products, spread_tiles(): jnp.einsum('btij,bif->btjf', tiles, rows_here, preferred_element_type=jnp...  19.8 us
    all_to_all x1, blocking collectives, carry_values(): lax.all_to_all(buffer.reshape(partition_list, capacity, width), ('machine...  18.9 us
    dot_general x1, matrix products, aggregate_tiles(): jnp.einsum('btij,btjf->bif', tiles, picked, preferred_element_type=jnp.fl...  14.9 us
    gather x1, local copies, waits for them, and re-layouts, aggregate_tiles(): picked = blocks[tile_column]  12.6 us
    all_to_all x1, starting transfers between devices, on_device(): lax.all_to_all(wanted.reshape(partition_list, capacity), ('machine', 'loc...  11.5 us
    all_to_all x1, waiting for transfers between devices, return_grads(): lax.all_to_all(rows.reshape(partition_list, capacity, width), ('machine',...  10.8 us
  transfers between devices with their start and end apart: 7, of which 5 were waited for; matrix products, arithmetic and copies ran while one was open for 17% of the time, Pallas kernels for 0%

commit v1 on v0

v1 whole, which is shorter than its diff:
```python
import jax
import jax.numpy as jnp
from jax import lax
from jax.experimental import pallas as pl
from jax.experimental.pallas import tpu as pltpu
from jax.sharding import PartitionSpec as P

F32 = jnp.float32
BF16 = jnp.bfloat16
I32 = jnp.int32
EDGE = 128
SLOTS = 8
VMEM_BYTES = 60 * 1024 * 1024
EXACT = lax.Precision.HIGHEST
ROOT = 0.7978845608028654
CUBIC = 0.044715


def dot(a, b, ca=1, cb=0, precision=None):
    return lax.dot_general(
        a, b, (((ca,), (cb,)), ((), ())), precision=precision, preferred_element_type=F32
    )


def iota(shape, dim):
    return lax.broadcasted_iota(I32, shape, dim)


def pick_rows(rows, base, row):
    return jnp.where(iota((rows, row.shape[1]), 0) + base == row, 1.0, 0.0).astype(BF16)


def pick_columns(column, base, columns):
    lane = iota(column.shape, 1) + base
    parts = [
        jnp.where(column == lane + EDGE * g, 1.0, 0.0).astype(BF16) for g in range(columns // EDGE)
    ]
    return jnp.concatenate(parts, axis=1)


def params():
    return pltpu.CompilerParams(vmem_limit_bytes=VMEM_BYTES)


def whole(*shape):
    return pl.BlockSpec(shape, lambda *_: (0,) * len(shape))


def cost(flops, nbytes):
    return pl.CostEstimate(flops=int(flops), bytes_accessed=int(nbytes), transcendentals=0)


def place_kernel(count, peer, row, tiles, ask, slot_row, slot_column, held, sem):
    first = count.shape[0] - held.shape[0]
    copy = pltpu.make_async_copy(tiles.at[pl.ds(first, held.shape[0])], held, sem)
    copy.start()
    mirrors = peer.shape[1]
    parts = ask.shape[0]
    member = iota((parts, mirrors), 0) == peer[...]
    earlier = jnp.where(
        iota((mirrors, mirrors), 0) < iota((mirrors, mirrors), 1), 1.0, 0.0
    ).astype(BF16)
    before = dot(jnp.where(member, 1.0, 0.0).astype(BF16), earlier)
    rank = jnp.sum(jnp.where(member, before, 0.0), axis=0, keepdims=True).astype(I32)
    slot = peer[...] * SLOTS + rank
    slot_row[...] = slot
    slot_column[...] = jnp.transpose(
        jnp.broadcast_to(slot.astype(F32), (EDGE, mirrors))
    ).astype(I32)
    lanes = iota((EDGE, mirrors), 0)
    rows = jnp.where(member, (row[...] + 1).astype(F32), 0.0)
    asked = dot(rows, jnp.where(lanes == rank, 1.0, 0.0), 1, 1, EXACT)
    copy.wait()
    degrees = []
    for b in range(held.shape[0]):
        used = iota((16, held.shape[1] * EDGE), 1) < count[first + b] * EDGE
        flat = jnp.concatenate([held[b, t] for t in range(held.shape[1])], axis=1)
        degrees.append(dot(jnp.where(used, 1.0, 0.0).astype(BF16), flat, 1, 1)[0:1])
    degree = jnp.where(member, jnp.concatenate(degrees, axis=1), 0.0)
    ask[...] = asked + dot(degree, jnp.where(lanes == rank + SLOTS, 1.0, 0.0), 1, 1, EXACT)


def place(tile_count, peer, row, tiles, parts):
    mirrors = row.shape[0]
    blocks = mirrors // EDGE
    smem = pl.BlockSpec(memory_space=pltpu.SMEM)
    return pl.pallas_call(
        place_kernel,
        grid=(1,),
        in_specs=[
            smem,
            whole(1, mirrors),
            whole(1, mirrors),
            pl.BlockSpec(memory_space=pl.ANY),
        ],
        out_specs=[whole(parts, EDGE), whole(1, mirrors), whole(mirrors, EDGE)],
        out_shape=[
            jax.ShapeDtypeStruct((parts, EDGE), F32),
            jax.ShapeDtypeStruct((1, mirrors), I32),
            jax.ShapeDtypeStruct((mirrors, EDGE), I32),
        ],
        scratch_shapes=[
            pltpu.VMEM((blocks, *tiles.shape[1:]), BF16),
            pltpu.SemaphoreType.DMA,
        ],
        compiler_params=params(),
        cost_estimate=cost(1e9, 2 << 20),
    )(tile_count, peer.reshape(1, mirrors), row.reshape(1, mirrors), tiles)


def fetch_kernel(arrived, values, rows, asked_row, degree_row, asked_column):
    slots = rows.shape[0]
    parts = arrived.shape[0]
    spread = jnp.where(iota((slots, parts), 0) // SLOTS == iota((slots, parts), 1), 1.0, 0.0)
    every = dot(spread, arrived[...], 1, 0, EXACT)
    lane, own = iota((slots, EDGE), 1), iota((slots, EDGE), 0) % SLOTS
    asked = jnp.sum(jnp.where(lane == own, every, 0.0), axis=1, keepdims=True) - 1.0
    asked = jnp.broadcast_to(asked, (slots, EDGE))
    asked_column[...] = asked.astype(I32)
    asked_row[...] = jnp.transpose(asked)[0:8].astype(I32)
    degree = jnp.sum(jnp.where(lane == own + SLOTS, every, 0.0), axis=1, keepdims=True)
    degree_row[...] = jnp.transpose(jnp.broadcast_to(degree, (slots, EDGE)))[0:8]
    step = 256

    def body(g, carry):
        at = pl.ds(pl.multiple_of(g * step, step), step)
        rows[at, :] = dot(pick_columns(asked_column[at, :], 0, values.shape[0]), values[...]).astype(BF16)
        return carry

    lax.fori_loop(0, slots // step, body, 0)


def fetch(arrived, values, slots):
    parts, width = arrived.shape[0], values.shape[1]
    return pl.pallas_call(
        fetch_kernel,
        grid=(1,),
        in_specs=[whole(parts, EDGE), whole(*values.shape)],
        out_specs=[whole(slots, width), whole(8, slots), whole(8, slots), whole(slots, EDGE)],
        out_shape=[
            jax.ShapeDtypeStruct((slots, width), BF16),
            jax.ShapeDtypeStruct((8, slots), I32),
            jax.ShapeDtypeStruct((8, slots), F32),
            jax.ShapeDtypeStruct((slots, EDGE), I32),
        ],
        compiler_params=params(),
        cost_estimate=cost(2e9, 2 << 20),
    )(arrived, values)


def near_kernel(count, column, tiles, values, partial, degree, slab):
    b = pl.program_id(0)
    blocks = values.shape[0] // EDGE
    width = values.shape[1]

    @pl.when(b == 0)
    def _():
        slab[: values.shape[0], :width] = values[...]
        slab[: values.shape[0], width:] = jnp.ones((values.shape[0], EDGE), BF16)
        slab[values.shape[0] :, :] = jnp.zeros((2 * EDGE, width + EDGE), BF16)
        slab[values.shape[0] + EDGE :, width:] = jnp.ones((EDGE, EDGE), BF16)

    n = count[b]

    def body(i, total):
        right = []
        for k in range(4):
            t = 4 * i + k
            c = column[b, t]
            c = jnp.where(t < n, jnp.where(c < blocks, c, blocks + 1), blocks)
            right.append(slab[pl.ds(pl.multiple_of(c * EDGE, EDGE), EDGE), :])
        left = jnp.concatenate([tiles[0, 4 * i + k] for k in range(4)], axis=1)
        return total + dot(left, jnp.concatenate(right, axis=0))

    total = lax.fori_loop(0, (n + 3) // 4, body, jnp.zeros((EDGE, width + EDGE), F32))
    partial[...] = total[:, :width]
    degree[...] = total[:, width:]


def near(tile_count, tile_column, tiles, values):
    row_blocks, most = tiles.shape[:2]
    rows, width = values.shape
    return pl.pallas_call(
        near_kernel,
        grid_spec=pltpu.PrefetchScalarGridSpec(
            num_scalar_prefetch=2,
            grid=(row_blocks,),
            in_specs=[
                pl.BlockSpec((1, most, EDGE, EDGE), lambda b, *_: (b, 0, 0, 0)),
                whole(rows, width),
            ],
            out_specs=[
                pl.BlockSpec((EDGE, width), lambda b, *_: (b, 0)),
                pl.BlockSpec((EDGE, EDGE), lambda b, *_: (b, 0)),
            ],
            scratch_shapes=[pltpu.VMEM((rows + 2 * EDGE, width + EDGE), BF16)],
        ),
        out_shape=[
            jax.ShapeDtypeStruct((row_blocks * EDGE, width), F32),
            jax.ShapeDtypeStruct((row_blocks * EDGE, EDGE), F32),
        ],
        compiler_params=params(),
        cost_estimate=cost(6e9, 16 << 20),
    )(tile_count, tile_column, tiles, values)


def mirror_out_kernel(
    count, column, arrived, slot_column, slot_row, partial, tiles, send, slab, held, total, sem
):
    blocks = held.shape[0]
    first = count.shape[0] - blocks
    copy = pltpu.make_async_copy(tiles.at[pl.ds(first, blocks)], held, sem)
    copy.start()
    slab[...] = dot(pick_columns(slot_column[...], 0, arrived.shape[0]), arrived[...]).astype(BF16)
    total[...] = partial[...]
    copy.wait()
    for b in range(blocks):
        n = count[first + b]

        def body(t, carry):
            c = column[first + b, t]

            @pl.when(c >= first)
            def _():
                at = pl.ds(pl.multiple_of((c - first) * EDGE, EDGE), EDGE)
                total[b * EDGE : (b + 1) * EDGE, :] += dot(held[b, t], slab[at, :])

            return carry

        lax.fori_loop(0, n, body, 0)
    send[...] = dot(pick_rows(send.shape[0], 0, slot_row[...]), total[...].astype(BF16)).astype(BF16)


def mirror_out(tile_count, tile_column, arrived, slot_column, slot_row, partial, tiles):
    slots, width = arrived.shape
    mirrors = slot_row.shape[1]
    last = partial.shape[0] // mirrors - 1
    smem = pl.BlockSpec(memory_space=pltpu.SMEM)
    return pl.pallas_call(
        mirror_out_kernel,
        grid=(1,),
        in_specs=[
            smem,
            smem,
            whole(slots, width),
            whole(mirrors, EDGE),
            whole(1, mirrors),
            pl.BlockSpec((mirrors, width), lambda *_: (last, 0)),
            pl.BlockSpec(memory_space=pl.ANY),
        ],
        out_specs=[whole(slots, width), whole(mirrors, width)],
        out_shape=[
            jax.ShapeDtypeStruct((slots, width), BF16),
            jax.ShapeDtypeStruct((mirrors, width), BF16),
        ],
        scratch_shapes=[
            pltpu.VMEM((mirrors // EDGE, *tiles.shape[1:]), BF16),
            pltpu.VMEM((mirrors, width), F32),
            pltpu.SemaphoreType.DMA,
        ],
        compiler_params=params(),
        cost_estimate=cost(2e9, 4 << 20),
    )(tile_count, tile_column, arrived, slot_column, slot_row, partial, tiles)


def far_kernel(
    count, column, tiles, mirrors, partial, degree, own, asked_row, degree_row, base, scale, slab
):
    b = pl.program_id(0)
    blocks = mirrors.shape[0] // EDGE
    first = count.shape[0] - blocks

    @pl.when(b == 0)
    def _():
        slab[: mirrors.shape[0], :] = mirrors[...]
        slab[mirrors.shape[0] :, :] = jnp.zeros((EDGE, mirrors.shape[1]), BF16)

    n = count[b]

    def body(i, total):
        right = []
        for k in range(4):
            t = 4 * i + k
            c = column[b, t]
            c = jnp.where((t < n) & (c >= first), c - first, blocks)
            right.append(slab[pl.ds(pl.multiple_of(c * EDGE, EDGE), EDGE), :])
        left = jnp.concatenate([tiles[0, 4 * i + k] for k in range(4)], axis=1)
        return total + dot(left, jnp.concatenate(right, axis=0))

    total = lax.fori_loop(0, (n + 3) // 4, body, partial[...])
    hit = iota((EDGE, asked_row.shape[1]), 0) + b * EDGE == asked_row[0:1]
    more = jnp.sum(jnp.where(hit, degree_row[0:1], 0.0), axis=1, keepdims=True)
    factor = 1.0 / (1.0 + (degree[...] + more))
    scale[...] = factor
    base[...] = own[...] + total * jnp.concatenate([factor, factor], axis=1)


def far(tile_count, tile_column, tiles, mirrors, partial, degree, own, asked_row, degree_row):
    most = tiles.shape[1]
    masters, width = own.shape
    return pl.pallas_call(
        far_kernel,
        grid_spec=pltpu.PrefetchScalarGridSpec(
            num_scalar_prefetch=2,
            grid=(masters // EDGE,),
            in_specs=[
                pl.BlockSpec((1, most, EDGE, EDGE), lambda b, *_: (b, 0, 0, 0)),
                whole(*mirrors.shape),
                pl.BlockSpec((EDGE, width), lambda b, *_: (b, 0)),
                pl.BlockSpec((EDGE, EDGE), lambda b, *_: (b, 0)),
                pl.BlockSpec((EDGE, width), lambda b, *_: (b, 0)),
                whole(*asked_row.shape),
                whole(*degree_row.shape),
            ],
            out_specs=[
                pl.BlockSpec((EDGE, width), lambda b, *_: (b, 0)),
                pl.BlockSpec((EDGE, EDGE), lambda b, *_: (b, 0)),
            ],
            scratch_shapes=[pltpu.VMEM((mirrors.shape[0] + EDGE, width), BF16)],
        ),
        out_shape=[
            jax.ShapeDtypeStruct((masters, width), F32),
            jax.ShapeDtypeStruct((masters, EDGE), F32),
        ],
        compiler_params=params(),
        cost_estimate=cost(6e9, 16 << 20),
    )(tile_count, tile_column, tiles, mirrors, partial, degree, own, asked_row, degree_row)


def turn_kernel(base, scale, cotangent, back, asked_row, asked_column, mixed, low, spread, send, total):
    g = pl.program_id(0)
    rows = base.shape[0]
    both = jnp.concatenate([scale[...], scale[...]], axis=1)
    added = dot(pick_rows(rows, g * rows, asked_row[0:1]), back[...])
    u = base[...] + added * both
    square = u * u
    bend = jnp.tanh(ROOT * (u + CUBIC * square * u))
    half = 0.5 * (1.0 + bend)
    mixed[...] = (u * half).astype(BF16)
    slope = half + 0.5 * u * (1.0 - bend * bend) * (ROOT * (1.0 + 3.0 * CUBIC * square))
    d_pre = cotangent[...].astype(F32) * slope
    low[...] = d_pre.astype(BF16)
    d_aggregate = (d_pre * both).astype(BF16)
    spread[...] = d_aggregate
    part = dot(pick_columns(asked_column[...], g * rows, rows), d_aggregate)

    @pl.when(g == 0)
    def _():
        total[...] = part

    @pl.when(g > 0)
    def _():
        total[...] += part

    @pl.when(g == pl.num_programs(0) - 1)
    def _():
        send[...] = total[...].astype(BF16)


def turn(base, scale, cotangent, back, asked_row, asked_column):
    masters, width = base.shape
    slots = back.shape[0]
    rows = 256
    block = pl.BlockSpec((rows, width), lambda g: (g, 0))
    return pl.pallas_call(
        turn_kernel,
        grid=(masters // rows,),
        in_specs=[
            block,
            pl.BlockSpec((rows, EDGE), lambda g: (g, 0)),
            block,
            whole(slots, width),
            whole(*asked_row.shape),
            whole(*asked_column.shape),
        ],
        out_specs=[block, block, block, whole(slots, width)],
        out_shape=[jax.ShapeDtypeStruct((masters, width), BF16)] * 3
        + [jax.ShapeDtypeStruct((slots, width), BF16)],
        scratch_shapes=[pltpu.VMEM((slots, width), F32)],
        compiler_params=params(),
        cost_estimate=cost(3e9, 8 << 20),
    )(base, scale, cotangent, back, asked_row, asked_column)


def add_back(n, count_from, column, b, tiles, values, total, low, high):
    def body(i, carry):
        right = jnp.concatenate([tiles[0, 2 * i], tiles[0, 2 * i + 1]], axis=1)
        product = dot(values, right)
        for k in range(2):
            t = 2 * i + k
            c = column[b, t]
            c = jnp.where((t < n) & (c >= low) & (c < high), c - low, high - low)
            total[c] += product[:, k * EDGE : (k + 1) * EDGE]
        return carry

    lax.fori_loop(count_from, (n + 1) // 2, body, 0)


def back_near_kernel(count, column, tiles, values, total):
    b = pl.program_id(0)

    @pl.when(b == 0)
    def _():
        total[...] = jnp.zeros(total.shape, F32)

    turned = jnp.transpose(values[...].astype(F32)).astype(BF16)
    add_back(count[b], 0, column, b, tiles, turned, total, 0, total.shape[0] - 1)


def back_near(tile_count, tile_column, tiles, values):
    row_blocks, most = tiles.shape[:2]
    masters, width = values.shape
    return pl.pallas_call(
        back_near_kernel,
        grid_spec=pltpu.PrefetchScalarGridSpec(
            num_scalar_prefetch=2,
            grid=(masters // EDGE,),
            in_specs=[
                pl.BlockSpec((1, most, EDGE, EDGE), lambda b, *_: (b, 0, 0, 0)),
                pl.BlockSpec((EDGE, width), lambda b, *_: (b, 0)),
            ],
            out_specs=whole(row_blocks + 1, width, EDGE),
        ),
        out_shape=jax.ShapeDtypeStruct((row_blocks + 1, width, EDGE), F32),
        compiler_params=params(),
        cost_estimate=cost(6e9, 16 << 20),
    )(tile_count, tile_column, tiles, values)


def mirror_back_kernel(
    count, column, arrived, slot_column, slot_row, partial, tiles, send, turned, held, total, rows, sem
):
    blocks = held.shape[0]
    first = count.shape[0] - blocks
    copy = pltpu.make_async_copy(tiles.at[pl.ds(first, blocks)], held, sem)
    copy.start()
    slab = dot(pick_columns(slot_column[...], 0, arrived.shape[0]), arrived[...])
    for b in range(blocks):
        turned[b] = jnp.transpose(slab[b * EDGE : (b + 1) * EDGE]).astype(BF16)
    total[...] = partial[...]
    copy.wait()
    for b in range(blocks):
        n = count[first + b]

        def body(t, carry):
            c = column[first + b, t]

            @pl.when(c >= first)
            def _():
                total[c - first] += dot(turned[b], held[b, t])

            return carry

        lax.fori_loop(0, n, body, 0)
    for c in range(blocks):
        rows[c * EDGE : (c + 1) * EDGE, :] = jnp.transpose(total[c]).astype(BF16)
    send[...] = dot(pick_rows(send.shape[0], 0, slot_row[...]), rows[...]).astype(BF16)


def mirror_back(tile_count, tile_column, arrived, slot_column, slot_row, partial, tiles):
    slots, width = arrived.shape
    mirrors = slot_row.shape[1]
    blocks = mirrors // EDGE
    at = tiles.shape[0] // blocks - 1
    smem = pl.BlockSpec(memory_space=pltpu.SMEM)
    return pl.pallas_call(
        mirror_back_kernel,
        grid=(1,),
        in_specs=[
            smem,
            smem,
            whole(slots, width),
            whole(mirrors, EDGE),
            whole(1, mirrors),
            pl.BlockSpec((blocks, width, EDGE), lambda *_: (at, 0, 0)),
            pl.BlockSpec(memory_space=pl.ANY),
        ],
        out_specs=[whole(slots, width), whole(blocks, width, EDGE)],
        out_shape=[
            jax.ShapeDtypeStruct((slots, width), BF16),
            jax.ShapeDtypeStruct((blocks, width, EDGE), BF16),
        ],
        scratch_shapes=[
            pltpu.VMEM((blocks, *tiles.shape[1:]), BF16),
            pltpu.VMEM((blocks, width, EDGE), F32),
            pltpu.VMEM((mirrors, width), BF16),
            pltpu.SemaphoreType.DMA,
        ],
        compiler_params=params(),
        cost_estimate=cost(2e9, 4 << 20),
    )(tile_count, tile_column, arrived, slot_column, slot_row, partial, tiles)


def back_far_kernel(count, column, tiles, turned, partial, total):
    b = pl.program_id(0)
    masters = total.shape[0] - 1

    @pl.when(b == 0)
    def _():
        total[:masters] = partial[...]
        total[masters] = jnp.zeros(total.shape[1:], F32)

    at = masters + b
    add_back(count[at], 0, column, at, tiles, turned[0], total, 0, masters)


def back_far(tile_count, tile_column, tiles, turned, partial):
    row_blocks, most = tiles.shape[:2]
    blocks, width = turned.shape[:2]
    masters = row_blocks - blocks
    return pl.pallas_call(
        back_far_kernel,
        grid_spec=pltpu.PrefetchScalarGridSpec(
            num_scalar_prefetch=2,
            grid=(blocks,),
            in_specs=[
                pl.BlockSpec((1, most, EDGE, EDGE), lambda b, *_: (masters + b, 0, 0, 0)),
                pl.BlockSpec((1, width, EDGE), lambda b, *_: (b, 0, 0)),
                whole(masters, width, EDGE),
            ],
            out_specs=whole(masters + 1, width, EDGE),
        ),
        out_shape=jax.ShapeDtypeStruct((masters + 1, width, EDGE), F32),
        compiler_params=params(),
        cost_estimate=cost(3e9, 8 << 20),
    )(tile_count, tile_column, tiles, turned, partial)


def finish_kernel(partial, back, asked_column, features, grad_self, turned, grads, flipped, total):
    g = pl.program_id(0)
    columns = turned.shape[1]
    width = turned.shape[0]
    inputs = features.shape[1]

    @pl.when(g == 0)
    def _():
        flipped[...] = jnp.transpose(back[...].astype(F32)).astype(BF16)
        total[...] = jnp.zeros(total.shape, F32)

    own = jnp.concatenate([partial[0], partial[1]], axis=1)
    value = own + dot(flipped[...], pick_columns(asked_column[...], g * columns, columns))
    value = value.astype(BF16)
    turned[...] = value
    total[...] += dot(value, features[...])

    @pl.when(g == pl.num_programs(0) - 1)
    def _():
        for h in range(width // EDGE):
            part = pl.ds(h * EDGE, EDGE)
            grads[pl.ds(h * inputs, inputs), :] = grad_self[:, h * EDGE : (h + 1) * EDGE]
            grads[pl.ds((width // EDGE + h) * inputs, inputs), :] = jnp.transpose(
                total[part, :]
            ).astype(BF16)


def finish(partial, back, asked_column, features, grad_self):
    slots, width = back.shape
    masters, inputs = features.shape
    columns = 2 * EDGE
    lines = 2 * inputs * width // EDGE
    return pl.pallas_call(
        finish_kernel,
        grid=(masters // columns,),
        in_specs=[
            pl.BlockSpec((2, width, EDGE), lambda g: (g, 0, 0)),
            whole(slots, width),
            whole(slots, EDGE),
            pl.BlockSpec((columns, inputs), lambda g: (g, 0)),
            whole(inputs, width),
        ],
        out_specs=[pl.BlockSpec((width, columns), lambda g: (0, g)), whole(lines, EDGE)],
        out_shape=[
            jax.ShapeDtypeStruct((width, masters), BF16),
            jax.ShapeDtypeStruct((lines, EDGE), BF16),
        ],
        scratch_shapes=[pltpu.VMEM((width, slots), BF16), pltpu.VMEM((width, inputs), F32)],
        compiler_params=params(),
        cost_estimate=cost(3e9, 8 << 20),
    )(partial, back, asked_column, features, grad_self)


def share_kernel(parts, out):
    share = jnp.sum(parts[...].astype(F32), axis=0, keepdims=True).astype(BF16)
    out[...] = jnp.broadcast_to(share, out.shape)


def share_out(parts):
    return pl.pallas_call(
        share_kernel,
        out_shape=jax.ShapeDtypeStruct(parts.shape, BF16),
        compiler_params=params(),
        cost_estimate=cost(1e6, 2 << 20),
    )(parts)


def unpack_kernel(lines, first, second):
    inputs = first.shape[0]
    for at, out in enumerate((first, second)):
        halves = [
            lines[(2 * at + h) * inputs : (2 * at + h + 1) * inputs, :].astype(F32) for h in range(2)
        ]
        out[...] = jnp.concatenate(halves, axis=1)


def unpack(lines, inputs, width):
    return pl.pallas_call(
        unpack_kernel,
        out_shape=[jax.ShapeDtypeStruct((inputs, width), F32)] * 2,
        compiler_params=params(),
        cost_estimate=cost(1e6, 2 << 20),
    )(lines)


def exchange(buffer, parts):
    moved = lax.all_to_all(
        buffer.reshape(parts, buffer.shape[0] // parts, buffer.shape[1]),
        ("machine", "local"),
        split_axis=0,
        concat_axis=0,
        tiled=True,
    )
    return moved.reshape(buffer.shape)


def on_device(
    features,
    w_self,
    w_neigh,
    mirror_master_part,
    mirror_row,
    tile_count,
    tile_column,
    tile_weight,
    cotangent,
):
    inputs, width = w_neigh.shape
    parts = lax.axis_size("machine") * lax.axis_size("local")
    slots = SLOTS * parts
    peer = mirror_master_part[:, 0]
    ask, slot_row, slot_column = place(tile_count, peer, mirror_row, tile_weight, parts)
    asked = exchange(ask, parts)
    projected = jnp.dot(features, w_neigh, preferred_element_type=F32).astype(BF16)
    own = jnp.dot(features, w_self, preferred_element_type=F32)
    rows, asked_row, degree_row, asked_column = fetch(asked, projected, slots)
    rows, projected = lax.optimization_barrier((rows, projected))
    arrived = exchange(rows, parts)
    partial, degree = near(tile_count, tile_column, tile_weight, projected)
    send, slab = mirror_out(
        tile_count, tile_column, arrived, slot_column, slot_row, partial, tile_weight
    )
    back = exchange(send, parts)
    base, scale = far(
        tile_count, tile_column, tile_weight, slab, partial, degree, own, asked_row, degree_row
    )
    mixed, low, spread, send = turn(base, scale, cotangent, back, asked_row, asked_column)
    arrived = exchange(send, parts)
    partial = back_near(tile_count, tile_column, tile_weight, spread)
    grad_self = lax.dot_general(
        features, low, (((0,), (0,)), ((), ())), preferred_element_type=F32
    ).astype(BF16)
    send, turned = mirror_back(
        tile_count, tile_column, arrived, slot_column, slot_row, partial, tile_weight
    )
    back = exchange(send, parts)
    partial = back_far(tile_count, tile_column, tile_weight, turned, partial)
    d_projected, grads = finish(partial, back, asked_column, features, grad_self)
    shares = exchange(grads, parts).reshape(parts, -1, EDGE)
    grad_features = (
        lax.dot_general(low, w_self, (((1,), (1,)), ((), ())), preferred_element_type=F32)
        + lax.dot_general(d_projected, w_neigh, (((0,), (1,)), ((), ())), preferred_element_type=F32)
    ).astype(BF16)
    sums = exchange(share_out(shares).reshape(grads.shape), parts)
    grad_self, grad_neigh = unpack(sums, inputs, width)
    return (mixed, grad_features, grad_self, grad_neigh)


def solution(mesh):
    placed = (
        P(("machine", "local"), None),
        P(),
        P(),
        P(("machine", "local"), None),
        P(("machine", "local")),
        P(("machine", "local")),
        P(("machine", "local"), None),
        P(("machine", "local"), None, None, None),
        P(("machine", "local"), None),
    )
    return jax.shard_map(
        on_device,
        mesh=mesh,
        in_specs=placed,
        out_specs=(P(("machine", "local"), None), P(("machine", "local"), None), P(), P()),
        check_vma=False,
    )
```

time: 474 us -> 230 us (0.49); the launches traced: 465 us -> 230 us
  waiting for transfers between devices: 163 us -> 21.8 us
  Pallas kernels: 0 us -> 107 us
  matrix products: 111 us -> 11.3 us
  local copies, waits for them, and re-layouts: 65.8 us -> 1.87 us
  other arithmetic: 42 us -> 0 us
  between operations: 14.8 us -> 0.79 us
  starting transfers between devices: 50 us -> 62.5 us
  blocking collectives: 18.9 us -> 24.6 us
    psum x1 -> x0, waiting for transfers between devices: 137 us -> none  [on_device(): lax.psum((local_self, local_neigh), ('machine', 'local'))]
    pallas_call x0 -> x12, Pallas kernels: none -> 107 us  [the longest x1 18.9 us: near(): pl.pallas_call(near_kernel, grid_spec=pltpu.PrefetchScalarGridSpec(num_sc...]
    dot_general x9 -> x5, matrix products: 111 us -> 11.3 us  [the longest x1 3.31 us: on_device(): lax.dot_general(features, low, (((0,), (0,)), ((), ())), preferred_elemen...]
    gather x5 -> x0, local copies, waits for them, and re-layouts: 29.9 us -> none  [the longest x1 12.6 us: aggregate_tiles(): picked = blocks[tile_column]]
    scatter-add x3 -> x0, other arithmetic: 27.4 us -> none  [the longest x1 10.1 us: on_device(): d_partial[:masters].at[asked].add(back_grads * alive[:, None])]
    scatter x5 -> x0, local copies, waits for them, and re-layouts: 15 us -> none  [the longest x1 3.78 us: on_device(): send_grads = jnp.zeros((partition_list * capacity, width), jnp.float32).a...]
    all_to_all x6, starting transfers between devices: 49.9 us -> 62.5 us  [exchange(): lax.all_to_all(buffer.reshape(parts, buffer.shape[0] // parts, buffer.sha...]
    slice x8 -> x0, local copies, waits for them, and re-layouts: 10.1 us -> none  [the longest x3 4.13 us: on_device(): d_partial[:masters].at[asked].add(back_grads * alive[:, None])]
  transfers between devices with their start and end apart: 7 -> 6, of which waited for: 5 -> 3; matrix products, arithmetic and copies ran while one was open for 17% -> 5% of each run, Pallas kernels for 0% -> 26%
where the time goes in v1:
time: 230 us
  Pallas kernels  107 us (47%)
  starting transfers between devices  62.5 us (27%)
  blocking collectives  24.6 us (11%)
  waiting for transfers between devices  21.8 us (9%)
  matrix products  11.3 us (5%)
    all_to_all x6, starting transfers between devices, exchange(): lax.all_to_all(buffer.reshape(parts, buffer.shape[0] // parts, buffer.sha...  62.5 us
    all_to_all x1, blocking collectives, exchange(): lax.all_to_all(buffer.reshape(parts, buffer.shape[0] // parts, buffer.sha...  24.6 us
    all_to_all x6, waiting for transfers between devices, exchange(): lax.all_to_all(buffer.reshape(parts, buffer.shape[0] // parts, buffer.sha...  21.8 us
    pallas_call x1, Pallas kernels, near(): pl.pallas_call(near_kernel, grid_spec=pltpu.PrefetchScalarGridSpec(num_sc...  18.9 us
    pallas_call x1, Pallas kernels, back_near(): pl.pallas_call(back_near_kernel, grid_spec=pltpu.PrefetchScalarGridSpec(n...  18.5 us
    pallas_call x1, Pallas kernels, far(): pl.pallas_call(far_kernel, grid_spec=pltpu.PrefetchScalarGridSpec(num_sca...  16.8 us
    pallas_call x1, Pallas kernels, turn(): pl.pallas_call(turn_kernel, grid=(masters // rows,), in_specs=[block, pl....  11.5 us
    pallas_call x1, Pallas kernels, finish(): pl.pallas_call(finish_kernel, grid=(masters // columns,), in_specs=[pl.Bl...  9.71 us
  transfers between devices with their start and end apart: 6, of which 3 were waited for; matrix products, arithmetic and copies ran while one was open for 5% of the time, Pallas kernels for 26%

profile of v1, /device:TPU:1, one launch (start us, length us, event | category | flops | bytes accessed | tf_op | source)
XLA Modules:
  0.0 229.6 jit_solution(6825001180895551539)
XLA Ops:
  0.6 0.0 copy-start
  0.7 5.1 %shard_map.120 = (f32[128,128]{1,0:T(8,128)}, s32[1,512]{1,0:T(1,128)}, s32[512,128]{1,0:T(8,128)}) custom-call(s32[20]{0:T(128)} %count.13, s32[1,512]{1,0:T(1,128)} %bitcast.35, s32[1,512]{1,0:T(1,128)} %bitcast.36, bf16[20,16,128,128]{3,2,1,0:T(8,128)(2,1)} %tiles.13), custom_call_target="tpu_custom_call" | custom-call | flops 1000000000 | bytes 2097152 | tf_op jit(solution)/shard_map/pallas_call | solution.py:87
  5.7 12.0 %all-to-all-start = ((f32[128,1,128]{2,1,0:T(1,128)}), f32[128,1,128]{2,1,0:T(1,128)}, u32[]{:S(2)}, u32[]{:S(2)}) async-start(f32[128,1,128]{2,1,0:T(1,128)} %bitcast.34), calls=%async_computation | async-start | bytes 131072 | tf_op jit(solution)/shard_map/all_to_all | solution.py:615
  17.7 2.3 %fusion.1.own = f32[2048,256]{1,0:T(8,128)} fusion(bf16[2048,768]{1,0:T(8,128)(2,1)S(1)} %copy-done.1, bf16[768,256]{1,0:T(8,128)(2,1)S(1)} %copy-done), kind=kOutput, calls=%fused_computation.4 | convolution fusion | flops 805306368 | bytes 5636096 | tf_op jit(solution)/shard_map/dot_general | solution.py:643
  20.1 2.0 convolution_convert_fusion.values
  22.0 0.7 copy.23.column
  22.7 4.8 %all-to-all-done = f32[128,1,128]{2,1,0:T(1,128)} async-done(((f32[128,1,128]{2,1,0:T(1,128)}), f32[128,1,128]{2,1,0:T(1,128)}, u32[]{:S(2)}, u32[]{:S(2)}) %all-to-all-start) | async-done | bytes 65568 | tf_op jit(solution)/shard_map/all_to_all | solution.py:615
  27.5 4.9 %shard_map.121 = (bf16[1024,256]{1,0:T(8,128)(2,1)}, s32[8,1024]{1,0:T(8,128)}, f32[8,1024]{1,0:T(8,128)}, s32[1024,128]{1,0:T(8,128)}) custom-call(f32[128,128]{1,0:T(8,128)} %bitcast.4.arrived, bf16[2048,256]{1,0:T(8,128)(2,1)} %convolution_convert_fusion.values), custom_call_target="tpu_custom_call" | custom-call | flops 2000000000 | bytes 2097152 | tf_op jit(solution)/shard_map/pallas_call | solution.py:135
  32.4 5.5 %all-to-all-start.1 = ((bf16[128,8,256]{2,1,0:T(8,128)(2,1)}), bf16[128,8,256]{2,1,0:T(8,128)(2,1)}, u32[]{:S(2)}, u32[]{:S(2)}) async-start(bf16[128,8,256]{2,1,0:T(8,128)(2,1)} %bitcast.31), calls=%async_computation.1 | async-start | bytes 1048576 | tf_op jit(solution)/shard_map/all_to_all | solution.py:615
  37.9 18.9 %shard_map.122 = (f32[2560,256]{1,0:T(8,128)}, f32[2560,128]{1,0:T(8,128)}) custom-call(s32[20]{0:T(128)} %count.13, s32[20,16]{1,0:T(8,128)} %copy.23.column, bf16[20,16,128,128]{3,2,1,0:T(8,128)(2,1)} %tiles.13, bf16[2048,256]{1,0:T(8,128)(2,1)} %convolution_convert_fusion.values), custom_call_target="tpu_custom_call" | custom-call | flops 6000000000 | bytes 16777216 | tf_op jit(solution)/shard_map/pallas_call | solution.py:183
  56.8 5.1 %shard_map.123 = (bf16[1024,256]{1,0:T(8,128)(2,1)}, bf16[512,256]{1,0:T(8,128)(2,1)}) custom-call(s32[20]{0:T(128)} %count.13, s32[20,16]{1,0:T(8,128)} %copy.23.column, bf16[1024,256]{1,0:T(8,128)(2,1)} %bitcast.6.arrived, s32[512,128]{1,0:T(8,128)} %get-tuple-element.32.slot_column, s32[1,512]{1,0:T(1,128)} %get-tuple-element.33.slot_row, ...), custom_call_target="tpu_custom_call" | custom-call | flops 2000000000 | bytes 4194304 | tf_op jit(solution)/shard_map/pallas_call | solution.py:239
  61.9 13.8 %all-to-all-start.2 = ((bf16[128,8,256]{2,1,0:T(8,128)(2,1)}), bf16[128,8,256]{2,1,0:T(8,128)(2,1)}, u32[]{:S(2)}, u32[]{:S(2)}) async-start(bf16[128,8,256]{2,1,0:T(8,128)(2,1)} %bitcast.30), calls=%async_computation.2 | async-start | bytes 1048576 | tf_op jit(solution)/shard_map/all_to_all | solution.py:615
  75.7 16.8 %shard_map.124 = (f32[2048,256]{1,0:T(8,128)}, f32[2048,128]{1,0:T(8,128)}) custom-call(s32[20]{0:T(128)} %count.13, s32[20,16]{1,0:T(8,128)} %copy.23.column, bf16[20,16,128,128]{3,2,1,0:T(8,128)(2,1)} %tiles.13, bf16[512,256]{1,0:T(8,128)(2,1)} %get-tuple-element.36.mirrors, f32[2560,256]{1,0:T(8,128)} %get-tuple-element.35.partial, ...), custom_call_target="tpu_custom_call" | custom-call | flops 6000000000 | bytes 16777216 | tf_op jit(solution)/shard_map/pallas_call | solution.py:301
  92.4 11.5 %shard_map.125 = (bf16[2048,256]{1,0:T(8,128)(2,1)}, bf16[2048,256]{1,0:T(8,128)(2,1)}, bf16[2048,256]{1,0:T(8,128)(2,1)}, bf16[1024,256]{1,0:T(8,128)(2,1)}) custom-call(f32[2048,256]{1,0:T(8,128)} %get-tuple-element.40.base, f32[2048,128]{1,0:T(8,128)} %get-tuple-element.41.scale, bf16[2048,256]{1,0:T(8,128)(2,1)} %cotangent.1, ...), custom_call_target="tpu_custom_call" | custom-call | flops 3000000000 | bytes 8388608 | tf_op jit(solution)/shard_map/pallas_call | solution.py:365
  103.9 12.0 %all-to-all-start.3 = ((bf16[128,8,256]{2,1,0:T(8,128)(2,1)}), bf16[128,8,256]{2,1,0:T(8,128)(2,1)}, u32[]{:S(2)}, u32[]{:S(2)}) async-start(bf16[128,8,256]{2,1,0:T(8,128)(2,1)} %bitcast.32), calls=%async_computation.3 | async-start | bytes 1048576 | tf_op jit(solution)/shard_map/all_to_all | solution.py:615
  115.9 18.5 %shard_map.126.partial = f32[21,256,128]{2,1,0:T(8,128)} custom-call(s32[20]{0:T(128)} %count.13, s32[20,16]{1,0:T(8,128)} %copy.23.column, bf16[20,16,128,128]{3,2,1,0:T(8,128)(2,1)} %tiles.13, bf16[2048,256]{1,0:T(8,128)(2,1)} %get-tuple-element.47.values), custom_call_target="tpu_custom_call" | custom-call | flops 6000000000 | bytes 16777216 | tf_op jit(solution)/shard_map/pallas_call | solution.py:413
  134.4 5.2 %shard_map.127 = (bf16[1024,256]{1,0:T(8,128)(2,1)}, bf16[4,256,128]{2,1,0:T(8,128)(2,1)}) custom-call(s32[20]{0:T(128)} %count.13, s32[20,16]{1,0:T(8,128)} %copy.23.column, bf16[1024,256]{1,0:T(8,128)(2,1)} %bitcast.10.arrived, s32[512,128]{1,0:T(8,128)} %get-tuple-element.32.slot_column, s32[1,512]{1,0:T(1,128)} %get-tuple-element.33.slot_row, ...), custom_call_target="tpu_custom_call" | custom-call | flops 2000000000 | bytes 4194304 | tf_op jit(solution)/shard_map/pallas_call | solution.py:466
  139.6 15.7 %all-to-all-start.4 = ((bf16[128,8,256]{2,1,0:T(8,128)(2,1)}), bf16[128,8,256]{2,1,0:T(8,128)(2,1)}, u32[]{:S(2)}, u32[]{:S(2)}) async-start(bf16[128,8,256]{2,1,0:T(8,128)(2,1)} %bitcast.33), calls=%async_computation.4 | async-start | bytes 1048576 | tf_op jit(solution)/shard_map/all_to_all | solution.py:615
  155.3 3.3 %fusion.grad_self = bf16[768,256]{1,0:T(8,128)(2,1)} fusion(bf16[2048,256]{1,0:T(8,128)(2,1)} %get-tuple-element.45, bf16[2048,768]{1,0:T(8,128)(2,1)S(1)} %copy-done.1), kind=kOutput, calls=%fused_computation.3 | convolution fusion | flops 805502976 | bytes 4587520 | tf_op jit(solution)/shard_map/dot_general | solution.py:658
  158.6 6.4 %shard_map.128.partial = f32[17,256,128]{2,1,0:T(8,128)} custom-call(s32[20]{0:T(128)} %count.13, s32[20,16]{1,0:T(8,128)} %copy.23.column, bf16[20,16,128,128]{3,2,1,0:T(8,128)(2,1)} %tiles.13, bf16[4,256,128]{2,1,0:T(8,128)(2,1)} %get-tuple-element.48.turned, f32[21,256,128]{2,1,0:T(8,128)} %shard_map.126.partial), custom_call_target="tpu_custom_call" | custom-call | flops 3000000000 | bytes 8388608 | tf_op jit(solution)/shard_map/pallas_call | solution.py:511
  165.0 4.0 %all-to-all-done.4 = bf16[128,8,256]{2,1,0:T(8,128)(2,1)} async-done(((bf16[128,8,256]{2,1,0:T(8,128)(2,1)}), bf16[128,8,256]{2,1,0:T(8,128)(2,1)}, u32[]{:S(2)}, u32[]{:S(2)}) %all-to-all-start.4) | async-done | bytes 524320 | tf_op jit(solution)/shard_map/all_to_all | solution.py:615
  169.1 9.7 %shard_map.129 = (bf16[256,2048]{1,0:T(8,128)(2,1)}, bf16[3072,128]{1,0:T(8,128)(2,1)}) custom-call(f32[17,256,128]{2,1,0:T(8,128)} %shard_map.128.partial, bf16[1024,256]{1,0:T(8,128)(2,1)} %bitcast.12.back, s32[1024,128]{1,0:T(8,128)} %get-tuple-element.43.asked_column, bf16[2048,768]{1,0:T(8,128)(2,1)} %features.1, bf16[768,256]{1,0:T(8,128)(2,1)} %fusion.grad_self), custom_call_target="tpu_custom_call" | custom-call | flops 3000000000 | bytes 8388608 | tf_op jit(solution)/shard_map/pallas_call | solution.py:561
  178.8 24.6 %all_to_all.35.parts = bf16[128,24,128]{2,1,0:T(8,128)(2,1)} all-to-all(bf16[128,24,128]{2,1,0:T(8,128)(2,1)} %bitcast.29), channel_id=1, replica_groups=mesh['machine'=32,'local'=4] {'machine','local'}, dimensions={0} | all-to-all | bytes 1572864 | tf_op jit(solution)/shard_map/all_to_all | solution.py:615
  203.4 2.2 shard_map.130
  205.6 3.7 %all-to-all-start.6 = ((bf16[128,24,128]{2,1,0:T(8,128)(2,1)}), bf16[128,24,128]{2,1,0:T(8,128)(2,1)S(1)}, u32[]{:S(2)}, u32[]{:S(2)}) async-start(bf16[128,24,128]{2,1,0:T(8,128)(2,1)} %shard_map.130), calls=%async_computation.6 | async-start | bytes 1572864 | tf_op jit(solution)/shard_map/all_to_all | solution.py:615
  209.3 1.0 fusion.2
  210.3 0.2 copy-done.4
  210.5 0.1 copy-done.6
  210.6 2.7 %add_convert_fusion = bf16[2048,768]{1,0:T(8,128)(2,1)} fusion(f32[2048,768]{1,0:T(8,128)S(1)} %fusion.2, bf16[256,2048]{1,0:T(8,128)(2,1)S(1)} %copy-done.4, bf16[768,256]{1,0:T(8,128)(2,1)S(1)} %copy-done.6), kind=kOutput, calls=%fused_computation | convolution fusion | flops 808452096 | bytes 10878976 | tf_op jit(solution)/shard_map/dot_general | solution.py:670
  213.3 13.0 %all-to-all-done.6 = bf16[128,24,128]{2,1,0:T(8,128)(2,1)S(1)} async-done(((bf16[128,24,128]{2,1,0:T(8,128)(2,1)}), bf16[128,24,128]{2,1,0:T(8,128)(2,1)S(1)}, u32[]{:S(2)}, u32[]{:S(2)}) %all-to-all-start.6) | async-done | bytes 786464 | tf_op jit(solution)/shard_map/all_to_all | solution.py:615
  226.4 0.9 copy-done.2
  227.3 2.3 %shard_map.131 = (f32[768,256]{1,0:T(8,128)}, f32[768,256]{1,0:T(8,128)}) custom-call(bf16[3072,128]{1,0:T(8,128)(2,1)} %bitcast.28), custom_call_target="tpu_custom_call" | custom-call | flops 1000000 | bytes 2097152 | tf_op jit(solution)/shard_map/pallas_call | solution.py:606
  (15 shorter events, 0.0 us)
Async XLA Ops:
  0.6 17.1 %copy-start = (bf16[768,256]{1,0:T(8,128)(2,1)S(1)}, bf16[768,256]{1,0:T(8,128)(2,1)}, u32[]{:S(2)}) copy-start(bf16[768,256]{1,0:T(8,128)(2,1)} %param.10) | copy-start | bytes 1179652
  0.6 17.1 %copy-start.1 = (bf16[2048,768]{1,0:T(8,128)(2,1)S(1)}, bf16[2048,768]{1,0:T(8,128)(2,1)}, u32[]{:S(2)}) copy-start(bf16[2048,768]{1,0:T(8,128)(2,1)} %features.1) | copy-start | bytes 9437188
  5.7 21.7 %all-to-all-start = ((f32[128,1,128]{2,1,0:T(1,128)}), f32[128,1,128]{2,1,0:T(1,128)}, u32[]{:S(2)}, u32[]{:S(2)}) async-start(f32[128,1,128]{2,1,0:T(1,128)} %bitcast.34), calls=%async_computation | async-start | bytes 131072 | tf_op jit(solution)/shard_map/all_to_all | solution.py:615
  17.7 2.3 %copy-start.5 = (bf16[768,256]{1,0:T(8,128)(2,1)S(1)}, bf16[768,256]{1,0:T(8,128)(2,1)}, u32[]{:S(2)}) copy-start(bf16[768,256]{1,0:T(8,128)(2,1)} %param.11) | copy-start | bytes 1179652
  20.1 2.0 copy-start.7
  32.4 24.3 %all-to-all-start.1 = ((bf16[128,8,256]{2,1,0:T(8,128)(2,1)}), bf16[128,8,256]{2,1,0:T(8,128)(2,1)}, u32[]{:S(2)}, u32[]{:S(2)}) async-start(bf16[128,8,256]{2,1,0:T(8,128)(2,1)} %bitcast.31), calls=%async_computation.1 | async-start | bytes 1048576 | tf_op jit(solution)/shard_map/all_to_all | solution.py:615
  61.9 30.6 %all-to-all-start.2 = ((bf16[128,8,256]{2,1,0:T(8,128)(2,1)}), bf16[128,8,256]{2,1,0:T(8,128)(2,1)}, u32[]{:S(2)}, u32[]{:S(2)}) async-start(bf16[128,8,256]{2,1,0:T(8,128)(2,1)} %bitcast.30), calls=%async_computation.2 | async-start | bytes 1048576 | tf_op jit(solution)/shard_map/all_to_all | solution.py:615
  103.9 30.5 %all-to-all-start.3 = ((bf16[128,8,256]{2,1,0:T(8,128)(2,1)}), bf16[128,8,256]{2,1,0:T(8,128)(2,1)}, u32[]{:S(2)}, u32[]{:S(2)}) async-start(bf16[128,8,256]{2,1,0:T(8,128)(2,1)} %bitcast.32), calls=%async_computation.3 | async-start | bytes 1048576 | tf_op jit(solution)/shard_map/all_to_all | solution.py:615
  139.6 29.4 %all-to-all-start.4 = ((bf16[128,8,256]{2,1,0:T(8,128)(2,1)}), bf16[128,8,256]{2,1,0:T(8,128)(2,1)}, u32[]{:S(2)}, u32[]{:S(2)}) async-start(bf16[128,8,256]{2,1,0:T(8,128)(2,1)} %bitcast.33), calls=%async_computation.4 | async-start | bytes 1048576 | tf_op jit(solution)/shard_map/all_to_all | solution.py:615
  178.8 30.5 %copy-start.3 = (bf16[2048,256]{1,0:T(8,128)(2,1)S(1)}, bf16[2048,256]{1,0:T(8,128)(2,1)}, u32[]{:S(2)}) copy-start(bf16[2048,256]{1,0:T(8,128)(2,1)} %get-tuple-element.45) | copy-start | bytes 3145732
  205.6 20.7 %all-to-all-start.6 = ((bf16[128,24,128]{2,1,0:T(8,128)(2,1)}), bf16[128,24,128]{2,1,0:T(8,128)(2,1)S(1)}, u32[]{:S(2)}, u32[]{:S(2)}) async-start(bf16[128,24,128]{2,1,0:T(8,128)(2,1)} %shard_map.130), calls=%async_computation.6 | async-start | bytes 1572864 | tf_op jit(solution)/shard_map/all_to_all | solution.py:615
  209.3 1.2 copy-start.4
  209.3 1.3 copy-start.6
  226.4 0.9 copy-start.2

commit v2 on v0

v2 whole, which is shorter than its diff:
```python
import jax
import jax.numpy as jnp
from jax import lax
from jax.experimental import pallas as pl
from jax.experimental.pallas import tpu as pltpu
from jax.sharding import PartitionSpec as P

F32 = jnp.float32
BF16 = jnp.bfloat16
I32 = jnp.int32
EDGE = 128
SLOTS = 8
MIB = 1024 * 1024
VMEM_BYTES = 60 * MIB
GROUP = 4
ROOT = 0.7978845608028654
CUBIC = 0.044715
EVERY = ("chip", "core", "local")


def dot(a, b, ca=1, cb=0):
    return lax.dot_general(a, b, (((ca,), (cb,)), ((), ())), preferred_element_type=F32)


def iota(shape, dim):
    return lax.broadcasted_iota(I32, shape, dim)


def pick_rows(rows, base, row):
    return jnp.where(iota((rows, row.shape[1]), 0) + base == row, 1.0, 0.0).astype(BF16)


def pick_columns(column, base, columns):
    lane = iota(column.shape, 1) + base
    parts = [
        jnp.where(column == lane + EDGE * g, 1.0, 0.0).astype(BF16) for g in range(columns // EDGE)
    ]
    return jnp.concatenate(parts, axis=1)


def block(b, size=EDGE):
    return pl.ds(pl.multiple_of(b * size, size), size)


def struct(*shape, dtype=BF16):
    return jax.ShapeDtypeStruct(shape, dtype)


class Moved:
    def __init__(self, far, held, sems, pieces, inward):
        self.far, self.held, self.sems, self.pieces, self.inward = far, held, sems, pieces, inward
        self.size = far.shape[0] // pieces
        self.started, self.waited = False, False

    def rows(self, p):
        return slice(p * self.size, (p + 1) * self.size)

    def copy(self, p):
        at = pl.ds(p * self.size, self.size)
        ends = self.far.at[at], self.held.at[at]
        return pltpu.make_async_copy(*(ends if self.inward else ends[::-1]), self.sems.at[p])

    def start(self, p=0):
        self.started = True
        self.copy(p).start()

    def wait(self, p=0):
        self.copy(p).wait()

    def all(self):
        if not self.waited:
            for p in range(self.pieces):
                self.wait(p)
        self.waited = True
        return self.held


def run(kernel, scalars, ins, outs, scratch=(), flops=1e9):
    ins, outs = list(ins), list(outs)
    n, m = len(ins), len(outs)
    own = [k for k in range(n + m) if k >= n or ins[k][1]]

    def body(*refs):
        scalar_refs, refs = refs[: len(scalars)], refs[len(scalars) :]
        far, refs = list(refs[: n + m]), refs[n + m :]
        held, sems, rest = refs[: len(own)], refs[len(own) : 2 * len(own)], refs[2 * len(own) :]
        for at, k in enumerate(own):
            far[k] = Moved(far[k], held[at], sems[at], (ins + outs)[k][1], k < n)
            if k < n and ins[k][1] == 1:
                far[k].start()
        kernel(scalar_refs, far[:n], far[n:], *rest)
        for out in far[n:]:
            if not out.started:
                for p in range(out.pieces):
                    out.start(p)
        for out in far[n:]:
            out.all()

    def place_of(k):
        shape = ins[k][0] if k < n else outs[k - n][0]
        spare = 0 if k < n else outs[k - n][2]
        return pltpu.VMEM((shape.shape[0] + spare, *shape.shape[1:]), shape.dtype)

    smem, any_space = pl.BlockSpec(memory_space=pltpu.SMEM), pl.BlockSpec(memory_space=pl.ANY)
    return pl.pallas_call(
        body,
        in_specs=[smem] * len(scalars) + [any_space] * n,
        out_specs=[any_space] * m,
        out_shape=[out[0] for out in outs],
        scratch_shapes=[place_of(k) for k in own]
        + [pltpu.SemaphoreType.DMA(((ins + outs)[k][1],)) for k in own]
        + list(scratch),
        compiler_params=params(),
        cost_estimate=cost(flops),
    )(*scalars, *[x for x, _ in ins])


def params():
    return pltpu.CompilerParams(vmem_limit_bytes=VMEM_BYTES)


def cost(flops):
    return pl.CostEstimate(flops=int(flops), bytes_accessed=4 * MIB, transcendentals=0)


def groups(tiles):
    return tiles.shape[0] // GROUP


def thirds(value):
    first = value.astype(BF16).astype(F32)
    second = (value - first).astype(BF16).astype(F32)
    return first, second, value - first - second


def used_ones(n, most):
    return jnp.concatenate(
        [jnp.full((EDGE, EDGE), jnp.where(t < n, 1.0, 0.0), F32).astype(BF16) for t in range(most)],
        axis=0,
    )


def place_kernel(scalars, ins, outs):
    (count,) = scalars
    peer, row, tiles = ins
    ask, slot_row, slot_column = outs
    mirrors = peer.held.shape[1]
    parts = ask.held.shape[0]
    blocks, most = mirrors // EDGE, tiles.held.shape[1]
    first = count.shape[0] - blocks
    last = tiles.pieces - 1
    tiles.start(last)
    peer = peer.all()[...]
    member = iota((parts, mirrors), 0) == peer
    chosen = jnp.where(member, 1.0, 0.0).astype(BF16)
    earlier = jnp.where(
        iota((mirrors, mirrors), 0) < iota((mirrors, mirrors), 1), 1.0, 0.0
    ).astype(BF16)
    before = dot(chosen, earlier)
    rank = jnp.sum(jnp.where(member, before, 0.0), axis=0, keepdims=True).astype(I32)
    slot = peer * SLOTS + rank
    slot_row.held[...] = slot
    slot_column.held[...] = jnp.transpose(
        jnp.broadcast_to(slot.astype(F32), (EDGE, mirrors))
    ).astype(I32)
    slot_row.start()
    slot_column.start()
    lane = iota((EDGE, mirrors), 0) - rank
    named = row.all()[...] + 1
    degrees = []
    tiles.wait(last)
    for b in range(first, first + blocks):
        flat = jnp.concatenate([tiles.held[b, t] for t in range(most)], axis=1)
        degrees.append(jnp.transpose(dot(flat, used_ones(count[b], most)))[0:1])
    fields = (named // EDGE).astype(F32), (named % EDGE).astype(F32)
    fields += thirds(jnp.concatenate(degrees, axis=1))
    lines = jnp.zeros((EDGE, mirrors), F32)
    for k, field in enumerate(fields):
        lines = jnp.where(lane == SLOTS * k, field, lines)
    ask.held[...] = dot(chosen, lines.astype(BF16), 1, 1)


def place(tile_count, peer, row, tiles, parts):
    mirrors = row.shape[0]
    return run(
        place_kernel,
        (tile_count,),
        ((peer.reshape(1, mirrors), 1), (row.reshape(1, mirrors), 1), (tiles, groups(tiles))),
        (
            (struct(parts, EDGE, dtype=F32), 1, 0),
            (struct(1, mirrors, dtype=I32), 1, 0),
            (struct(mirrors, EDGE, dtype=I32), 1, 0),
        ),
    )


def slot_lines(arrived, slots):
    parts = arrived.shape[0]
    spread = jnp.where(iota((slots, parts), 0) // SLOTS == iota((slots, parts), 1), 1.0, 0.0)
    return dot(spread.astype(BF16), arrived[...].astype(BF16))


def gather(values, asked_column, rows):
    step = 512
    for g in range(rows.shape[0] // step):
        at = slice(g * step, (g + 1) * step)
        rows[at, :] = dot(pick_columns(asked_column[at, :], 0, values.shape[0]), values[...]).astype(BF16)


def fetch_kernel(scalars, ins, outs):
    arrived, values = ins
    rows, asked_column = outs
    slots = rows.held.shape[0]
    every = slot_lines(arrived.all(), slots)
    lane = iota((slots, EDGE), 1) - iota((slots, EDGE), 0) % SLOTS
    asked = jnp.where(lane == 0, every * EDGE, jnp.where(lane == SLOTS, every, 0.0))
    asked = jnp.sum(asked, axis=1, keepdims=True) - 1.0
    asked_column.held[...] = jnp.broadcast_to(asked, (slots, EDGE)).astype(I32)
    asked_column.start()
    gather(values.all(), asked_column.held, rows.held)


def fetch(arrived, values, slots):
    return run(
        fetch_kernel,
        (),
        ((arrived, 1), (values, 1)),
        ((struct(slots, values.shape[1]), 1, 0), (struct(slots, EDGE, dtype=I32), 1, 0)),
        flops=2e9,
    )


def near_kernel(scalars, ins, outs, slab):
    count, column = scalars
    values, arrived, asked_column, tiles = ins
    partial, asked_row, degree_row = outs
    most = tiles.held.shape[1]
    for g in range(tiles.pieces):
        tiles.start(g)
    rows, width = values.held.shape
    blocks = rows // EDGE
    slab[rows:, :] = jnp.zeros((EDGE, width), BF16)
    slab[:rows, :] = values.all()[...]
    for g in range(tiles.pieces):
        tiles.wait(g)
        for b in range(g * GROUP, (g + 1) * GROUP):
            right = []
            for t in range(most):
                c = column[b, t]
                c = jnp.where((t < count[b]) & (c < blocks), c, blocks)
                right.append(slab[block(c), :])
            left = jnp.concatenate([tiles.held[b, t] for t in range(most)], axis=1)
            partial.held[b * EDGE : (b + 1) * EDGE, :] = dot(left, jnp.concatenate(right, axis=0))
        partial.start(g)
    slots = asked_column.held.shape[0]
    asked_row.held[...] = jnp.transpose(asked_column.all()[...].astype(F32))[0:8].astype(I32)
    lane = iota((slots, EDGE), 1) - iota((slots, EDGE), 0) % SLOTS
    mine = (lane == 2 * SLOTS) | (lane == 3 * SLOTS) | (lane == 4 * SLOTS)
    sums = jnp.sum(jnp.where(mine, slot_lines(arrived.all(), slots), 0.0), axis=1, keepdims=True)
    degree_row.held[...] = jnp.transpose(jnp.broadcast_to(sums, (slots, EDGE)))[0:8]


def near(tile_count, tile_column, arrived, asked_column, values, tiles):
    rows, width = values.shape
    slots, row_blocks = asked_column.shape[0], tiles.shape[0]
    return run(
        near_kernel,
        (tile_count, tile_column),
        ((values, 1), (arrived, 1), (asked_column, 1), (tiles, groups(tiles))),
        (
            (struct(row_blocks * EDGE, width, dtype=F32), groups(tiles), 0),
            (struct(8, slots, dtype=I32), 1, 0),
            (struct(8, slots, dtype=F32), 1, 0),
        ),
        (pltpu.VMEM((rows + EDGE, width), BF16),),
        flops=5e9,
    )


def far_product(n, column, b, tiles, padded, first):
    blocks = padded.shape[0] // EDGE - 1
    right = []
    for t in range(tiles.shape[1]):
        c = column[b, t]
        c = jnp.where((t < n) & (c >= first), c - first, blocks)
        right.append(padded[block(c), :])
    left = jnp.concatenate([tiles[b, t] for t in range(tiles.shape[1])], axis=1)
    return dot(left, jnp.concatenate(right, axis=0))


def mirror_out_kernel(scalars, ins, outs, total):
    count, column = scalars
    arrived, slot_column, partial, tiles, slot_row = ins
    send, padded = outs
    mirrors = total.shape[0]
    blocks = mirrors // EDGE
    first = tiles.held.shape[0] - blocks
    last = tiles.pieces - 1
    tiles.start(last)
    partial.start(last)
    pick = pick_columns(slot_column.all()[...], 0, arrived.held.shape[0])
    padded.held[:mirrors, :] = dot(pick, arrived.all()[...]).astype(BF16)
    padded.held[mirrors:, :] = jnp.zeros((EDGE, padded.held.shape[1]), BF16)
    padded.start()
    partial.wait(last)
    tiles.wait(last)
    for b in range(first, first + blocks):
        more = far_product(count[b], column, b, tiles.held, padded.held, first)
        total[(b - first) * EDGE : (b - first + 1) * EDGE, :] = (
            partial.held[b * EDGE : (b + 1) * EDGE, :] + more
        ).astype(BF16)
    slots = send.held.shape[0]
    send.held[...] = dot(pick_rows(slots, 0, slot_row.all()[...]), total[...]).astype(BF16)


def mirror_out(tile_count, tile_column, arrived, slot_column, slot_row, partial, tiles):
    slots, width = arrived.shape
    mirrors = slot_row.shape[1]
    return run(
        mirror_out_kernel,
        (tile_count, tile_column),
        (
            (arrived, 1),
            (slot_column, 1),
            (partial, groups(tiles)),
            (tiles, groups(tiles)),
            (slot_row, 1),
        ),
        ((struct(slots, width), 1, 0), (struct(mirrors + EDGE, width), 1, 0)),
        (pltpu.VMEM((mirrors, width), BF16),),
        flops=2e9,
    )


def far_kernel(scalars, ins, outs):
    count, column = scalars
    padded, asked_row, degree_row, tiles, partial, own = ins
    base, scale = outs
    for g in range(own.pieces):
        for source in (tiles, partial, own):
            source.start(g)
    row_blocks, most = base.held.shape[0] // EDGE, tiles.held.shape[1]
    padded, asked, degrees = padded.all(), asked_row.all()[0:1], degree_row.all()[0:1]
    for g in range(own.pieces):
        for source in (tiles, partial, own):
            source.wait(g)
        for b in range(g * GROUP, (g + 1) * GROUP):
            at = slice(b * EDGE, (b + 1) * EDGE)
            total = partial.held[at, :] + far_product(
                count[b], column, b, tiles.held, padded, row_blocks
            )
            weights = jnp.zeros((EDGE, EDGE), F32)
            for t in range(most):
                used = jnp.where(t < count[b], 1.0, 0.0)
                weights += tiles.held[b, t].astype(F32) * used
            hit = iota((EDGE, asked.shape[1]), 0) + b * EDGE == asked
            given = jnp.where(hit, degrees, 0.0)
            for k in range(asked.shape[1] // EDGE):
                weights += given[:, k * EDGE : (k + 1) * EDGE]
            degree = jnp.sum(weights, axis=1, keepdims=True)
            factor = jnp.broadcast_to(1.0 / (1.0 + degree), (EDGE, EDGE))
            scale.held[at, :] = factor
            base.held[at, :] = own.held[at, :] + total * jnp.concatenate([factor, factor], axis=1)
        base.start(g)
    scale.start()


def far(tile_count, tile_column, tiles, padded, partial, own, asked_row, degree_row):
    masters, width = own.shape
    n = masters // EDGE // GROUP
    return run(
        far_kernel,
        (tile_count, tile_column),
        (
            (padded, 1),
            (asked_row, 1),
            (degree_row, 1),
            (tiles, groups(tiles)),
            (partial, groups(tiles)),
            (own, n),
        ),
        ((struct(masters, width, dtype=F32), n, 0), (struct(masters, EDGE, dtype=F32), 1, 0)),
        flops=5e9,
    )


def turn_kernel(scalars, ins, outs):
    asked_row, back, base, scale, cotangent, asked_column = ins
    mixed, low, spread, send = outs
    for p in range(base.pieces):
        for source in (base, scale, cotangent):
            source.start(p)
    asked, back = asked_row.all()[0:1], back.all()
    step = 512
    for g in range(base.held.shape[0] // step):
        if g * step % base.size == 0:
            for source in (base, scale, cotangent):
                source.wait(g * step // base.size)
        at = slice(g * step, (g + 1) * step)
        both = jnp.concatenate([scale.held[at, :], scale.held[at, :]], axis=1)
        added = dot(pick_rows(step, g * step, asked), back[...])
        u = base.held[at, :] + added * both
        square = u * u
        bend = jnp.tanh(u * (ROOT + (ROOT * CUBIC) * square))
        half = 0.5 + 0.5 * bend
        mixed.held[at, :] = (u * half).astype(BF16)
        slope = half * (1.0 + u * (1.0 - bend) * (ROOT + (3.0 * ROOT * CUBIC) * square))
        d_pre = cotangent.held[at, :].astype(F32) * slope
        low.held[at, :] = d_pre.astype(BF16)
        spread.held[at, :] = (d_pre * both).astype(BF16)
    for out in (spread, low, mixed):
        out.start()
    gather(spread.held, asked_column.all(), send.held)


def turn(base, scale, cotangent, back, asked_row, asked_column):
    masters, width = base.shape
    return run(
        turn_kernel,
        (),
        (
            (asked_row, 1),
            (back, 1),
            (base, 2),
            (scale, 2),
            (cotangent, 2),
            (asked_column, 1),
        ),
        ((struct(masters, width), 1, 0),) * 3 + ((struct(*back.shape), 1, 0),),
        flops=3e9,
    )


def add_back(n, column, b, tiles, values, total, low):
    blocks = total.shape[0] - 1
    for i in range(0, tiles.shape[1], 4):
        right = jnp.concatenate([tiles[b, i + k] for k in range(4)], axis=1)
        product = dot(values, right)
        for k in range(4):
            c = column[b, i + k] - low
            c = jnp.where((i + k < n) & (c >= 0) & (c < blocks), c, blocks)
            total[c] += product[:, k * EDGE : (k + 1) * EDGE]


def back_near_kernel(scalars, ins, outs):
    count, column = scalars
    values, tiles = ins
    (total,) = outs
    blocks = values.held.shape[0] // EDGE
    for g in range(blocks // GROUP):
        tiles.start(g)
    total.held[...] = jnp.zeros(total.held.shape, F32)
    values = values.all()
    for g in range(blocks // GROUP):
        tiles.wait(g)

        def body(b, carry):
            turned = jnp.transpose(values[block(b), :].astype(F32)).astype(BF16)
            add_back(count[b], column, b, tiles.held, turned, total.held, 0)
            return carry

        lax.fori_loop(g * GROUP, (g + 1) * GROUP, body, 0)


def back_near(tile_count, tile_column, values, tiles):
    row_blocks, width = tiles.shape[0], values.shape[1]
    (total,) = run(
        back_near_kernel,
        (tile_count, tile_column),
        ((values, 1), (tiles, groups(tiles))),
        ((struct(row_blocks, width, EDGE, dtype=F32), 1, 1),),
        flops=5e9,
    )
    return total


def mirror_back_kernel(scalars, ins, outs, total, rows, sem):
    count, column = scalars
    arrived, slot_column, tiles, partial, slot_row = ins
    send, turned = outs
    blocks = turned.held.shape[0]
    first = tiles.held.shape[0] - blocks
    last = tiles.pieces - 1
    tiles.start(last)
    copy = pltpu.make_async_copy(partial.at[pl.ds(first, blocks)], total.at[pl.ds(0, blocks)], sem)
    copy.start()
    pick = pick_columns(slot_column.all()[...], 0, arrived.held.shape[0])
    slab = dot(pick, arrived.all()[...])
    for b in range(blocks):
        turned.held[b] = jnp.transpose(slab[b * EDGE : (b + 1) * EDGE]).astype(BF16)
    turned.start()
    total[blocks] = jnp.zeros(total.shape[1:], F32)
    copy.wait()
    tiles.wait(last)
    for b in range(blocks):
        add_back(count[first + b], column, first + b, tiles.held, turned.held[b], total, first)
    for c in range(blocks):
        rows[c * EDGE : (c + 1) * EDGE, :] = jnp.transpose(total[c]).astype(BF16)
    slots = send.held.shape[0]
    send.held[...] = dot(pick_rows(slots, 0, slot_row.all()[...]), rows[...]).astype(BF16)


def mirror_back(tile_count, tile_column, arrived, slot_column, slot_row, partial, tiles):
    slots, width = arrived.shape
    mirrors = slot_row.shape[1]
    blocks = mirrors // EDGE
    return run(
        mirror_back_kernel,
        (tile_count, tile_column),
        ((arrived, 1), (slot_column, 1), (tiles, groups(tiles)), (partial, 0), (slot_row, 1)),
        ((struct(slots, width), 1, 0), (struct(blocks, width, EDGE), 1, 0)),
        (
            pltpu.VMEM((blocks + 1, width, EDGE), F32),
            pltpu.VMEM((mirrors, width), BF16),
            pltpu.SemaphoreType.DMA,
        ),
        flops=2e9,
    )


def back_far_kernel(scalars, ins, outs, sem):
    count, column = scalars
    turned, partial, tiles = ins
    (total,) = outs
    blocks = turned.held.shape[0]
    masters = total.held.shape[0] - 1
    copy = pltpu.make_async_copy(partial.at[pl.ds(0, masters)], total.held.at[pl.ds(0, masters)], sem)
    copy.start()
    tiles.start(tiles.pieces - 1)
    total.held[masters] = jnp.zeros(total.held.shape[1:], F32)
    turned.all()
    copy.wait()
    tiles.wait(tiles.pieces - 1)

    def body(b, carry):
        add_back(count[masters + b], column, masters + b, tiles.held, turned.held[b], total.held, 0)
        return carry

    lax.fori_loop(0, blocks, body, 0)


def back_far(tile_count, tile_column, tiles, turned, partial):
    blocks, width = turned.shape[:2]
    (total,) = run(
        back_far_kernel,
        (tile_count, tile_column),
        ((turned, 1), (partial, 0), (tiles, groups(tiles))),
        ((struct(tiles.shape[0] - blocks, width, EDGE, dtype=F32), 1, 1),),
        (pltpu.SemaphoreType.DMA,),
        flops=3e9,
    )
    return total


def finish_kernel(scalars, ins, outs):
    (core,) = scalars
    back, asked_column, partial, features, grad_self = ins
    turned, keep, give = outs
    width, masters = turned.held.shape
    inputs = features.held.shape[1]
    step = 512
    flipped = jnp.transpose(back.all()[...].astype(F32)).astype(BF16)
    asked, partial = asked_column.all(), partial.all()
    for g in range(masters // step):
        own = []
        for b in range(g * step // EDGE, (g + 1) * step // EDGE):
            own.append(partial[b])
        added = dot(flipped, pick_columns(asked[...], g * step, step))
        turned.held[:, g * step : (g + 1) * step] = (
            jnp.concatenate(own, axis=1) + added
        ).astype(BF16)
    turned.start()
    total = dot(turned.held[...], features.all()[...])
    grad_self = grad_self.all()
    for h in range(width // EDGE):
        lines = pl.ds(h * inputs, inputs)
        first = grad_self[:, h * EDGE : (h + 1) * EDGE].astype(F32)
        second = jnp.transpose(total[h * EDGE : (h + 1) * EDGE, :])
        keep.held[lines, :] = jnp.where(core[0] == 0, first, second)
        give.held[lines, :] = jnp.where(core[0] == 0, second, first).astype(BF16)


def finish(core, partial, back, asked_column, features, grad_self):
    width = back.shape[1]
    masters, inputs = features.shape
    lines = inputs * width // EDGE
    return run(
        finish_kernel,
        (core,),
        (
            (back, 1),
            (asked_column, 1),
            (partial, 1),
            (features, 1),
            (grad_self, 1),
        ),
        (
            (struct(width, masters), 1, 0),
            (struct(lines, EDGE, dtype=F32), 1, 0),
            (struct(lines, EDGE), 1, 0),
        ),
        flops=3e9,
    )


def input_grads_kernel(scalars, ins, outs):
    low, turned, w_self, w_neigh = ins
    (out,) = outs
    step = out.size
    own, other, low, turned = w_self.all(), w_neigh.all(), low.all(), turned.all()
    for g in range(out.pieces):
        at = slice(g * step, (g + 1) * step)
        d_projected = jnp.transpose(turned[:, at].astype(F32)).astype(BF16)
        value = dot(low[at, :], own[...], 1, 1) + dot(d_projected, other[...], 1, 1)
        out.held[at, :] = value.astype(BF16)
        out.start(g)


def input_grads(low, turned, w_self, w_neigh):
    masters, inputs = low.shape[0], w_self.shape[0]
    (out,) = run(
        input_grads_kernel,
        (),
        ((low, 1), (turned, 1), (w_self, 1), (w_neigh, 1)),
        ((struct(masters, inputs), 2, 0),),
        flops=3e9,
    )
    return out


def share_kernel(parts, out):
    share = jnp.sum(parts[...].astype(F32), axis=0, keepdims=True).astype(BF16)
    out[...] = jnp.broadcast_to(share, out.shape)


def share_out(parts):
    return pl.pallas_call(
        share_kernel,
        out_shape=struct(*parts.shape),
        compiler_params=params(),
        cost_estimate=cost(1e8),
    )(parts)


def unpack_kernel(core, mine, other, first, second):
    inputs = first.shape[0]
    for h in range(2):
        lines, lanes = pl.ds(h * inputs, inputs), pl.ds(h * EDGE, EDGE)
        a, b = mine[lines, :].astype(F32), other[lines, :].astype(F32)
        first[:, lanes] = jnp.where(core[0] == 0, a, b)
        second[:, lanes] = jnp.where(core[0] == 0, b, a)


def unpack(core, mine, other, inputs, width):
    smem, vmem = pl.BlockSpec(memory_space=pltpu.SMEM), pl.BlockSpec(memory_space=pltpu.VMEM)
    return pl.pallas_call(
        unpack_kernel,
        in_specs=[smem, vmem, vmem],
        out_specs=[vmem, vmem],
        out_shape=[struct(inputs, width, dtype=F32)] * 2,
        compiler_params=params(),
        cost_estimate=cost(1e8),
    )(core, mine, other)


def exchange(buffer, axes=EVERY):
    parts = lax.axis_size(axes)
    moved = lax.all_to_all(
        buffer.reshape(parts, buffer.shape[0] // parts, buffer.shape[1]),
        axes,
        split_axis=0,
        concat_axis=0,
        tiled=True,
    )
    return moved.reshape(buffer.shape)


def to_other_core(value):
    return lax.ppermute(value, "core", [(0, 1), (1, 0)])


def on_device(
    features,
    w_self,
    w_neigh,
    mirror_master_part,
    mirror_row,
    tile_count,
    tile_column,
    tile_weight,
    cotangent,
):
    inputs, width = w_neigh.shape
    parts = lax.axis_size(EVERY)
    core = lax.axis_index("core").astype(I32).reshape(1)
    slots = SLOTS * parts
    peer = mirror_master_part[:, 0]
    ask, slot_row, slot_column = place(tile_count, peer, mirror_row, tile_weight, parts)
    asked = exchange(ask)
    tiles = tile_weight
    projected = jnp.dot(features, w_neigh, preferred_element_type=F32).astype(BF16)
    own = jnp.dot(features, w_self, preferred_element_type=F32)
    rows, asked_column = fetch(asked, projected, slots)
    arrived = exchange(rows)
    partial, asked_row, degree_row = near(
        tile_count, tile_column, asked, asked_column, projected, tiles
    )
    send, padded = mirror_out(
        tile_count, tile_column, arrived, slot_column, slot_row, partial, tiles
    )
    back = exchange(send)
    base, scale = far(
        tile_count, tile_column, tiles, padded, partial, own, asked_row, degree_row
    )
    mixed, low, spread, send = turn(base, scale, cotangent, back, asked_row, asked_column)
    arrived = exchange(send)
    partial = back_near(tile_count, tile_column, spread, tiles)
    grad_self = lax.dot_general(
        features, low, (((0,), (0,)), ((), ())), preferred_element_type=F32
    ).astype(BF16)
    send, turned = mirror_back(
        tile_count, tile_column, arrived, slot_column, slot_row, partial, tiles
    )
    back = exchange(send)
    partial = back_far(tile_count, tile_column, tiles, turned, partial)
    d_projected, keep, give = finish(core, partial, back, asked_column, features, grad_self)
    pair = (keep + to_other_core(give).astype(F32)).astype(BF16)
    same = ("chip", "local")
    shares = exchange(pair, same).reshape(lax.axis_size(same), -1, EDGE)
    grad_features = input_grads(low, d_projected, w_self, w_neigh)
    shares, grad_features = lax.optimization_barrier((shares, grad_features))
    mine = exchange(share_out(shares).reshape(pair.shape), same)
    grad_self, grad_neigh = unpack(core, mine, to_other_core(mine), inputs, width)
    return (mixed, grad_features, grad_self, grad_neigh)


def solution(mesh):
    machine, local = mesh.devices.shape
    devices = mesh.devices.reshape(machine // 2, 2, local)
    split, rows = P(EVERY), P(EVERY, None)
    return jax.shard_map(
        on_device,
        mesh=jax.sharding.Mesh(devices, EVERY),
        in_specs=(rows, P(), P(), rows, split, split, rows, P(EVERY, None, None, None), rows),
        out_specs=(rows, rows, P(), P()),
        check_vma=False,
    )
```

time: 474 us -> 188 us (0.40); the launches traced: 465 us -> 187 us
  waiting for transfers between devices: 163 us -> 24.8 us
  matrix products: 111 us -> 8.55 us
  Pallas kernels: 0 us -> 80.7 us
  local copies, waits for them, and re-layouts: 65.8 us -> 2.8 us
  other arithmetic: 42 us -> 1.96 us
  between operations: 14.8 us -> 0.82 us
    psum x1 -> x0, waiting for transfers between devices: 137 us -> none  [on_device(): lax.psum((local_self, local_neigh), ('machine', 'local'))]
    dot_general x9 -> x3, matrix products: 111 us -> 8.55 us  [the longest x1 3.3 us: on_device(): lax.dot_general(features, low, (((0,), (0,)), ((), ())), preferred_elemen...]
    pallas_call x0 -> x13, Pallas kernels: none -> 80.7 us  [the longest x11 76.5 us: run(): pl.pallas_call(body, in_specs=[smem] * len(scalars) + [any_space] * n, ou...]
    gather x5 -> x0, local copies, waits for them, and re-layouts: 29.9 us -> none  [the longest x1 12.6 us: aggregate_tiles(): picked = blocks[tile_column]]
    scatter-add x3 -> x0, other arithmetic: 27.4 us -> none  [the longest x1 10.1 us: on_device(): d_partial[:masters].at[asked].add(back_grads * alive[:, None])]
    scatter x5 -> x0, local copies, waits for them, and re-layouts: 15 us -> none  [the longest x1 3.78 us: on_device(): send_grads = jnp.zeros((partition_list * capacity, width), jnp.float32).a...]
    slice x8 -> x0, local copies, waits for them, and re-layouts: 10.1 us -> none  [the longest x3 4.13 us: on_device(): d_partial[:masters].at[asked].add(back_grads * alive[:, None])]
    reduce_sum x2 -> x0, other arithmetic: 7.41 us -> none  [the longest x1 6.49 us: aggregate_tiles(): degree = jnp.sum(tiles, axis=(1, 3), dtype=jnp.float32)]
  transfers between devices with their start and end apart: 7 -> 8, of which waited for: 5 -> 7; matrix products, arithmetic and copies ran while one was open for 17% -> 5% of each run, Pallas kernels for 0% -> 24%
where the time goes in v2:
time: 188 us; the launch traced here: 187 us
  Pallas kernels  80.7 us (43%)
  starting transfers between devices  52.3 us (28%)
  waiting for transfers between devices  24.8 us (13%)
  blocking collectives  14.8 us (8%)
  matrix products  8.55 us (5%)
  local copies, waits for them, and re-layouts  2.8 us (1%)
  other arithmetic  1.96 us (1%)
    pallas_call x11, Pallas kernels, run(): pl.pallas_call(body, in_specs=[smem] * len(scalars) + [any_space] * n, ou...  76.5 us
    all_to_all x6, starting transfers between devices, exchange(): lax.all_to_all(buffer.reshape(parts, buffer.shape[0] // parts, buffer.sha...  48.8 us
    all_to_all x6, waiting for transfers between devices, exchange(): lax.all_to_all(buffer.reshape(parts, buffer.shape[0] // parts, buffer.sha...  21.7 us
    all_to_all x1, blocking collectives, exchange(): lax.all_to_all(buffer.reshape(parts, buffer.shape[0] // parts, buffer.sha...  14.8 us
  transfers between devices with their start and end apart: 8, of which 7 were waited for; matrix products, arithmetic and copies ran while one was open for 5% of the time, Pallas kernels for 24%

profile of v2, /device:TPU:1, one launch (start us, length us, event | category | flops | bytes accessed | tf_op | source)
XLA Modules:
  0.0 186.8 jit_solution(9272346771481584311)
XLA Ops:
  0.6 4.2 %shard_map.120 = (f32[128,128]{1,0:T(8,128)}, s32[1,512]{1,0:T(1,128)}, s32[512,128]{1,0:T(8,128)}) custom-call(s32[20]{0:T(128)} %refs_0_.13, s32[1,512]{1,0:T(1,128)} %bitcast.34, s32[1,512]{1,0:T(1,128)} %bitcast.35, bf16[20,16,128,128]{3,2,1,0:T(8,128)(2,1)} %refs_4_.6), custom_call_target="tpu_custom_call" | custom-call | flops 1000000000 | bytes 4194304 | tf_op jit(solution)/shard_map/pallas_call | solution.py:105
  4.9 11.5 %all-to-all-start = ((f32[128,1,128]{2,1,0:T(1,128)}), f32[128,1,128]{2,1,0:T(1,128)S(1)}, u32[]{:S(2)}, u32[]{:S(2)}) async-start(f32[128,1,128]{2,1,0:T(1,128)} %bitcast.33), calls=%async_computation | async-start | bytes 131072 | tf_op jit(solution)/shard_map/all_to_all | solution.py:668
  16.4 3.0 %convolution_convert_fusion.refs_1_.refs_2_ = bf16[2048,256]{1,0:T(8,128)(2,1)} fusion(bf16[2048,768]{1,0:T(8,128)(2,1)S(1)} %copy-done, bf16[768,256]{1,0:T(8,128)(2,1)} %refs_3_.5), kind=kOutput, calls=%fused_computation | convolution fusion | flops 805830656 | bytes 4587520 | tf_op jit(solution)/shard_map/dot_general | solution.py:701
  19.3 6.9 %all-to-all-done = f32[128,1,128]{2,1,0:T(1,128)S(1)} async-done(((f32[128,1,128]{2,1,0:T(1,128)}), f32[128,1,128]{2,1,0:T(1,128)S(1)}, u32[]{:S(2)}, u32[]{:S(2)}) %all-to-all-start) | async-done | bytes 65568 | tf_op jit(solution)/shard_map/all_to_all | solution.py:668
  26.8 3.3 %shard_map.121 = (bf16[1024,256]{1,0:T(8,128)(2,1)}, s32[1024,128]{1,0:T(8,128)}) custom-call(f32[128,128]{1,0:T(8,128)} %bitcast.31, bf16[2048,256]{1,0:T(8,128)(2,1)} %convolution_convert_fusion.refs_1_.refs_2_), custom_call_target="tpu_custom_call" | custom-call | flops 2000000000 | bytes 4194304 | tf_op jit(solution)/shard_map/pallas_call | solution.py:105
  30.2 4.9 %all-to-all-start.1 = ((bf16[128,8,256]{2,1,0:T(8,128)(2,1)}), bf16[128,8,256]{2,1,0:T(8,128)(2,1)}, u32[]{:S(2)}, u32[]{:S(2)}) async-start(bf16[128,8,256]{2,1,0:T(8,128)(2,1)} %bitcast.29), calls=%async_computation.1 | async-start | bytes 1048576 | tf_op jit(solution)/shard_map/all_to_all | solution.py:668
  35.7 9.8 %shard_map.122 = (f32[2560,256]{1,0:T(8,128)}, s32[8,1024]{1,0:T(8,128)}, f32[8,1024]{1,0:T(8,128)}) custom-call(s32[20]{0:T(128)} %refs_0_.13, s32[20,16]{1,0:T(8,128)} %copy.21.refs_1_, bf16[2048,256]{1,0:T(8,128)(2,1)} %convolution_convert_fusion.refs_1_.refs_2_, f32[128,128]{1,0:T(8,128)} %bitcast.32, ...), custom_call_target="tpu_custom_call" | custom-call | flops 5000000000 | bytes 4194304 | tf_op jit(solution)/shard_map/pallas_call | solution.py:105
  45.5 3.4 %all-to-all-done.1 = bf16[128,8,256]{2,1,0:T(8,128)(2,1)} async-done(((bf16[128,8,256]{2,1,0:T(8,128)(2,1)}), bf16[128,8,256]{2,1,0:T(8,128)(2,1)}, u32[]{:S(2)}, u32[]{:S(2)}) %all-to-all-start.1) | async-done | bytes 524320 | tf_op jit(solution)/shard_map/all_to_all | solution.py:668
  49.0 5.4 %shard_map.123 = (bf16[1024,256]{1,0:T(8,128)(2,1)}, bf16[640,256]{1,0:T(8,128)(2,1)}) custom-call(s32[20]{0:T(128)} %refs_0_.13, s32[20,16]{1,0:T(8,128)} %copy.21.refs_1_, bf16[1024,256]{1,0:T(8,128)(2,1)} %bitcast.6.refs_2_, s32[512,128]{1,0:T(8,128)} %get-tuple-element.33.refs_3_, f32[2560,256]{1,0:T(8,128)} %get-tuple-element.34.refs_4_.refs_6_, ...), custom_call_target="tpu_custom_call" | custom-call | flops 2000000000 | bytes 4194304 | tf_op jit(solution)/shard_map/pallas_call | solution.py:105
  54.4 7.0 %all-to-all-start.2 = ((bf16[128,8,256]{2,1,0:T(8,128)(2,1)}), bf16[128,8,256]{2,1,0:T(8,128)(2,1)}, u32[]{:S(2)}, u32[]{:S(2)}) async-start(bf16[128,8,256]{2,1,0:T(8,128)(2,1)} %bitcast.28), calls=%async_computation.2 | async-start | bytes 1048576 | tf_op jit(solution)/shard_map/all_to_all | solution.py:668
  61.3 2.3 %fusion.1.refs_7_ = f32[2048,256]{1,0:T(8,128)} fusion(bf16[2048,768]{1,0:T(8,128)(2,1)S(1)} %copy-done, bf16[768,256]{1,0:T(8,128)(2,1)S(1)} %copy-done.4), kind=kOutput, calls=%fused_computation.4 | convolution fusion | flops 805306368 | bytes 5636096 | tf_op jit(solution)/shard_map/dot_general | solution.py:702
  63.6 9.6 %shard_map.124 = (f32[2048,256]{1,0:T(8,128)}, f32[2048,128]{1,0:T(8,128)}) custom-call(s32[20]{0:T(128)} %refs_0_.13, s32[20,16]{1,0:T(8,128)} %copy.21.refs_1_, bf16[640,256]{1,0:T(8,128)(2,1)} %get-tuple-element.37.refs_2_, s32[8,1024]{1,0:T(8,128)} %get-tuple-element.31.refs_3_.refs_0_, f32[8,1024]{1,0:T(8,128)} %get-tuple-element.38.refs_4_, ...), custom_call_target="tpu_custom_call" | custom-call | flops 5000000000 | bytes 4194304 | tf_op jit(solution)/shard_map/pallas_call | solution.py:105
  73.3 1.8 all-to-all-done.2
  75.1 6.5 %shard_map.125 = (bf16[2048,256]{1,0:T(8,128)(2,1)}, bf16[2048,256]{1,0:T(8,128)(2,1)}, bf16[2048,256]{1,0:T(8,128)(2,1)}, bf16[1024,256]{1,0:T(8,128)(2,1)}) custom-call(s32[8,1024]{1,0:T(8,128)} %get-tuple-element.31.refs_3_.refs_0_, bf16[1024,256]{1,0:T(8,128)(2,1)} %bitcast.8.refs_1_, f32[2048,256]{1,0:T(8,128)} %get-tuple-element.39.refs_2_, ...), custom_call_target="tpu_custom_call" | custom-call | flops 3000000000 | bytes 4194304 | tf_op jit(solution)/shard_map/pallas_call | solution.py:105
  81.6 8.4 %all-to-all-start.3 = ((bf16[128,8,256]{2,1,0:T(8,128)(2,1)}), bf16[128,8,256]{2,1,0:T(8,128)(2,1)}, u32[]{:S(2)}, u32[]{:S(2)}) async-start(bf16[128,8,256]{2,1,0:T(8,128)(2,1)} %bitcast.27), calls=%async_computation.3 | async-start | bytes 1048576 | tf_op jit(solution)/shard_map/all_to_all | solution.py:668
  90.0 14.1 %shard_map.126.refs_5_.refs_3_ = f32[20,256,128]{2,1,0:T(8,128)} custom-call(s32[20]{0:T(128)} %refs_0_.13, s32[20,16]{1,0:T(8,128)} %copy.21.refs_1_, bf16[2048,256]{1,0:T(8,128)(2,1)} %get-tuple-element.43.refs_2_, bf16[20,16,128,128]{3,2,1,0:T(8,128)(2,1)} %refs_4_.6), custom_call_target="tpu_custom_call" | custom-call | flops 5000000000 | bytes 4194304 | tf_op jit(solution)/shard_map/pallas_call | solution.py:105
  104.1 6.2 %shard_map.127 = (bf16[1024,256]{1,0:T(8,128)(2,1)}, bf16[4,256,128]{2,1,0:T(8,128)(2,1)}) custom-call(s32[20]{0:T(128)} %refs_0_.13, s32[20,16]{1,0:T(8,128)} %copy.21.refs_1_, bf16[1024,256]{1,0:T(8,128)(2,1)} %bitcast.11.refs_2_, s32[512,128]{1,0:T(8,128)} %get-tuple-element.33.refs_3_, bf16[20,16,128,128]{3,2,1,0:T(8,128)(2,1)} %refs_4_.6, ...), custom_call_target="tpu_custom_call" | custom-call | flops 2000000000 | bytes 4194304 | tf_op jit(solution)/shard_map/pallas_call | solution.py:105
  110.4 10.2 %all-to-all-start.4 = ((bf16[128,8,256]{2,1,0:T(8,128)(2,1)}), bf16[128,8,256]{2,1,0:T(8,128)(2,1)}, u32[]{:S(2)}, u32[]{:S(2)}) async-start(bf16[128,8,256]{2,1,0:T(8,128)(2,1)} %bitcast.30), calls=%async_computation.4 | async-start | bytes 1048576 | tf_op jit(solution)/shard_map/all_to_all | solution.py:668
  120.6 3.3 %fusion.refs_5_ = bf16[768,256]{1,0:T(8,128)(2,1)} fusion(bf16[2048,256]{1,0:T(8,128)(2,1)} %get-tuple-element.46.refs_0_, bf16[2048,768]{1,0:T(8,128)(2,1)S(1)} %copy-done), kind=kOutput, calls=%fused_computation.2 | convolution fusion | flops 805502976 | bytes 4587520 | tf_op jit(solution)/shard_map/dot_general | solution.py:718
  123.9 6.5 %shard_map.128.refs_3_ = f32[16,256,128]{2,1,0:T(8,128)} custom-call(s32[20]{0:T(128)} %refs_0_.13, s32[20,16]{1,0:T(8,128)} %copy.21.refs_1_, bf16[4,256,128]{2,1,0:T(8,128)(2,1)} %get-tuple-element.45.refs_2_, f32[20,256,128]{2,1,0:T(8,128)} %shard_map.126.refs_5_.refs_3_, bf16[20,16,128,128]{3,2,1,0:T(8,128)(2,1)} %refs_4_.6), custom_call_target="tpu_custom_call" | custom-call | flops 3000000000 | bytes 4194304 | tf_op jit(solution)/shard_map/pallas_call | solution.py:105
  130.4 4.0 %all-to-all-done.4 = bf16[128,8,256]{2,1,0:T(8,128)(2,1)} async-done(((bf16[128,8,256]{2,1,0:T(8,128)(2,1)}), bf16[128,8,256]{2,1,0:T(8,128)(2,1)}, u32[]{:S(2)}, u32[]{:S(2)}) %all-to-all-start.4) | async-done | bytes 524320 | tf_op jit(solution)/shard_map/all_to_all | solution.py:668
  134.4 6.0 %shard_map.129 = (bf16[256,2048]{1,0:T(8,128)(2,1)}, f32[1536,128]{1,0:T(8,128)}, bf16[1536,128]{1,0:T(8,128)(2,1)}) custom-call(s32[1]{0:T(128)} %bitcast.9.refs_0_.core, bf16[1024,256]{1,0:T(8,128)(2,1)} %bitcast.13.refs_1_, s32[1024,128]{1,0:T(8,128)} %get-tuple-element.30.refs_4_.refs_5_.refs_2_, f32[16,256,128]{2,1,0:T(8,128)} %shard_map.128.refs_3_, ...), custom_call_target="tpu_custom_call" | custom-call | flops 3000000000 | bytes 4194304 | tf_op jit(solution)/shard_map/pallas_call | solution.py:105
  140.7 1.7 collective-permute-done
  142.4 2.0 %add_convert_fusion = bf16[1536,128]{1,0:T(8,128)(2,1)} fusion(f32[1536,128]{1,0:T(8,128)} %get-tuple-element.47, bf16[1536,128]{1,0:T(8,128)(2,1)S(1)} %collective-permute-done), kind=kLoop, calls=%fused_computation.3 | loop fusion | flops 589824 | bytes 1572864 | tf_op jit(solution)/shard_map/convert_element_type | solution.py:727
  144.4 6.8 %all-to-all-start.5 = ((bf16[64,24,128]{2,1,0:T(8,128)(2,1)}), bf16[64,24,128]{2,1,0:T(8,128)(2,1)S(1)}, u32[]{:S(2)}, u32[]{:S(2)}) async-start(bf16[64,24,128]{2,1,0:T(8,128)(2,1)} %bitcast.15), calls=%async_computation.5 | async-start | bytes 786432 | tf_op jit(solution)/shard_map/all_to_all | solution.py:668
  151.2 4.8 %shard_map.130 = bf16[2048,768]{1,0:T(8,128)(2,1)} custom-call(bf16[2048,256]{1,0:T(8,128)(2,1)} %get-tuple-element.46.refs_0_, bf16[256,2048]{1,0:T(8,128)(2,1)} %get-tuple-element.49.refs_1_, bf16[768,256]{1,0:T(8,128)(2,1)} %refs_2_.1, bf16[768,256]{1,0:T(8,128)(2,1)} %refs_3_.5), custom_call_target="tpu_custom_call" | custom-call | flops 3000000000 | bytes 4194304 | tf_op jit(solution)/shard_map/pallas_call | solution.py:105
  156.1 5.7 %all-to-all-done.5.parts = bf16[64,24,128]{2,1,0:T(8,128)(2,1)S(1)} async-done(((bf16[64,24,128]{2,1,0:T(8,128)(2,1)}), bf16[64,24,128]{2,1,0:T(8,128)(2,1)S(1)}, u32[]{:S(2)}, u32[]{:S(2)}) %all-to-all-start.5) | async-done | bytes 393248 | tf_op jit(solution)/shard_map/all_to_all | solution.py:668
  162.5 1.8 shard_map.131
  164.3 14.8 %all_to_all.35 = bf16[64,24,128]{2,1,0:T(8,128)(2,1)S(1)} all-to-all(bf16[64,24,128]{2,1,0:T(8,128)(2,1)} %shard_map.131), channel_id=1, replica_groups=mesh['chip'=16,'core'=2,'local'=4] {'chip','local'}, dimensions={0} | all-to-all | bytes 786432 | tf_op jit(solution)/shard_map/all_to_all | solution.py:668
  179.1 3.2 %collective-permute-start.1 = (bf16[1536,128]{1,0:T(8,128)(2,1)S(1)}, bf16[1536,128]{1,0:T(8,128)(2,1)S(1)}, u32[]{:S(2)}, u32[]{:S(2)}) collective-permute-start(bf16[1536,128]{1,0:T(8,128)(2,1)S(1)} %bitcast.25), channel_id=1, source_target_pairs={{0,4},{4,0},{1,5},{5,1},{2,6},{6,2},{3,7},{7,3},{8,12},{12,8},{9,1... | collective-permute-start | bytes 1179656 | tf_op jit(solution)/shard_map/ppermute | solution.py:679
  182.3 1.3 collective-permute-done.1.other
  184.4 2.4 %shard_map.132 = (f32[768,256]{1,0:T(8,128)}, f32[768,256]{1,0:T(8,128)}) custom-call(s32[1]{0:T(128)} %bitcast.9.refs_0_.core, bf16[1536,128]{1,0:T(8,128)(2,1)} %bitcast.26, bf16[1536,128]{1,0:T(8,128)(2,1)} %copy-done.3), custom_call_target="tpu_custom_call" | custom-call | flops 100000000 | bytes 4194304 | tf_op jit(solution)/shard_map/pallas_call | solution.py:656
  (17 shorter events, 3.1 us)
Async XLA Ops:
  0.6 15.7 %copy-start = (bf16[2048,768]{1,0:T(8,128)(2,1)S(1)}, bf16[2048,768]{1,0:T(8,128)(2,1)}, u32[]{:S(2)}) copy-start(bf16[2048,768]{1,0:T(8,128)(2,1)} %refs_4_.7) | copy-start | bytes 9437188
  4.9 21.3 %all-to-all-start = ((f32[128,1,128]{2,1,0:T(1,128)}), f32[128,1,128]{2,1,0:T(1,128)S(1)}, u32[]{:S(2)}, u32[]{:S(2)}) async-start(f32[128,1,128]{2,1,0:T(1,128)} %bitcast.33), calls=%async_computation | async-start | bytes 131072 | tf_op jit(solution)/shard_map/all_to_all | solution.py:668
  26.2 0.6 copy-start.5
  26.8 8.2 %copy-start.6 = (s32[20,16]{0,1:T(8,128)S(1)}, s32[20,16]{0,1:T(8,128)}, u32[]{:S(2)}) copy-start(s32[20,16]{0,1:T(8,128)} %param.15) | copy-start | bytes 3844
  30.2 18.8 %all-to-all-start.1 = ((bf16[128,8,256]{2,1,0:T(8,128)(2,1)}), bf16[128,8,256]{2,1,0:T(8,128)(2,1)}, u32[]{:S(2)}, u32[]{:S(2)}) async-start(bf16[128,8,256]{2,1,0:T(8,128)(2,1)} %bitcast.29), calls=%async_computation.1 | async-start | bytes 1048576 | tf_op jit(solution)/shard_map/all_to_all | solution.py:668
  48.9 12.4 %copy-start.4 = (bf16[768,256]{1,0:T(8,128)(2,1)S(1)}, bf16[768,256]{1,0:T(8,128)(2,1)}, u32[]{:S(2)}) copy-start(bf16[768,256]{1,0:T(8,128)(2,1)} %refs_2_.1) | copy-start | bytes 1179652
  54.4 20.7 %all-to-all-start.2 = ((bf16[128,8,256]{2,1,0:T(8,128)(2,1)}), bf16[128,8,256]{2,1,0:T(8,128)(2,1)}, u32[]{:S(2)}, u32[]{:S(2)}) async-start(bf16[128,8,256]{2,1,0:T(8,128)(2,1)} %bitcast.28), calls=%async_computation.2 | async-start | bytes 1048576 | tf_op jit(solution)/shard_map/all_to_all | solution.py:668
  81.6 22.5 %all-to-all-start.3 = ((bf16[128,8,256]{2,1,0:T(8,128)(2,1)}), bf16[128,8,256]{2,1,0:T(8,128)(2,1)}, u32[]{:S(2)}, u32[]{:S(2)}) async-start(bf16[128,8,256]{2,1,0:T(8,128)(2,1)} %bitcast.27), calls=%async_computation.3 | async-start | bytes 1048576 | tf_op jit(solution)/shard_map/all_to_all | solution.py:668
  110.4 24.0 %all-to-all-start.4 = ((bf16[128,8,256]{2,1,0:T(8,128)(2,1)}), bf16[128,8,256]{2,1,0:T(8,128)(2,1)}, u32[]{:S(2)}, u32[]{:S(2)}) async-start(bf16[128,8,256]{2,1,0:T(8,128)(2,1)} %bitcast.30), calls=%async_computation.4 | async-start | bytes 1048576 | tf_op jit(solution)/shard_map/all_to_all | solution.py:668
  140.4 2.0 %collective-permute-start = (bf16[1536,128]{1,0:T(8,128)(2,1)}, bf16[1536,128]{1,0:T(8,128)(2,1)S(1)}, u32[]{:S(2)}, u32[]{:S(2)}) collective-permute-start(bf16[1536,128]{1,0:T(8,128)(2,1)} %get-tuple-element.48), channel_id=1, source_target_pairs={{0,4},{4,0},{1,5},{5,1},{2,6},{6,2},{3,7},{7,3},{8,12},{12,8},{9,1... | collective-permute-start | bytes 1179656 | tf_op jit(solution)/shard_map/ppermute | solution.py:679
  144.4 17.3 %all-to-all-start.5 = ((bf16[64,24,128]{2,1,0:T(8,128)(2,1)}), bf16[64,24,128]{2,1,0:T(8,128)(2,1)S(1)}, u32[]{:S(2)}, u32[]{:S(2)}) async-start(bf16[64,24,128]{2,1,0:T(8,128)(2,1)} %bitcast.15), calls=%async_computation.5 | async-start | bytes 786432 | tf_op jit(solution)/shard_map/all_to_all | solution.py:668
  161.7 0.7 copy-start.1
  179.1 4.5 %copy-start.2 = (bf16[64,24,128]{2,1,0:T(8,128)(2,1)}, bf16[64,24,128]{2,1,0:T(8,128)(2,1)S(1)}, u32[]{:S(2)}) copy-start(bf16[64,24,128]{2,1,0:T(8,128)(2,1)S(1)} %all_to_all.35) | copy-start | bytes 1179652
  179.1 4.5 %collective-permute-start.1 = (bf16[1536,128]{1,0:T(8,128)(2,1)S(1)}, bf16[1536,128]{1,0:T(8,128)(2,1)S(1)}, u32[]{:S(2)}, u32[]{:S(2)}) collective-permute-start(bf16[1536,128]{1,0:T(8,128)(2,1)S(1)} %bitcast.25), channel_id=1, source_target_pairs={{0,4},{4,0},{1,5},{5,1},{2,6},{6,2},{3,7},{7,3},{8,12},{12,8},{9,1... | collective-permute-start | bytes 1179656 | tf_op jit(solution)/shard_map/ppermute | solution.py:679
  183.7 0.8 copy-start.3

commit v3 on v2

--- a/solution.py
+++ b/solution.py
@@ -38,10 +38,6 @@
     return jnp.concatenate(parts, axis=1)
 
 
-def block(b, size=EDGE):
-    return pl.ds(pl.multiple_of(b * size, size), size)
-
-
 def struct(*shape, dtype=BF16):
     return jax.ShapeDtypeStruct(shape, dtype)
 
@@ -78,7 +74,7 @@
 def run(kernel, scalars, ins, outs, scratch=(), flops=1e9):
     ins, outs = list(ins), list(outs)
     n, m = len(ins), len(outs)
-    own = [k for k in range(n + m) if k >= n or ins[k][1]]
+    own = [k for k in range(n + m) if (ins + outs)[k][1]]
 
     def body(*refs):
         scalar_refs, refs = refs[: len(scalars)], refs[len(scalars) :]
@@ -89,11 +85,12 @@
             if k < n and ins[k][1] == 1:
                 far[k].start()
         kernel(scalar_refs, far[:n], far[n:], *rest)
-        for out in far[n:]:
+        results = [far[k] for k in own if k >= n]
+        for out in results:
             if not out.started:
                 for p in range(out.pieces):
                     out.start(p)
-        for out in far[n:]:
+        for out in results:
             out.all()
 
     def place_of(k):
@@ -230,95 +227,126 @@
     )
 
 
-def near_kernel(scalars, ins, outs, slab):
+def flat(tiles, rows, columns):
+    lines = [jnp.concatenate([tiles[b, c] for c in columns], axis=1) for b in rows]
+    return jnp.concatenate(lines, axis=0)
+
+
+def densify(count, column, tiles, dense, g):
+    members = range(g * GROUP, (g + 1) * GROUP)
+    last = dense.shape[1] - 1
+    longest = count[g * GROUP]
+    for b in members:
+        longest = jnp.maximum(longest, count[b])
+
+    def body(t, carry):
+        for b in members:
+            c = jnp.where(t < count[b], column[b, t], last)
+            dense[b, c] = dense[b, c] + tiles[b, t]
+        return carry
+
+    lax.fori_loop(0, longest, body, 0)
+
+
+def near_kernel(scalars, ins, outs, dense, far_sems, near_sem):
     count, column = scalars
-    values, arrived, asked_column, tiles = ins
-    partial, asked_row, degree_row = outs
-    most = tiles.held.shape[1]
+    values, tiles, arrived, asked_column = ins
+    partial, degree, asked_row, degree_row, near, far = outs
+    row_blocks = tiles.held.shape[0]
+    cut, last = near.shape[1], dense.shape[1] - 1
+
+    def far_copy(g):
+        at = pl.ds(g * GROUP, GROUP)
+        return pltpu.make_async_copy(dense.at[at, pl.ds(cut, last - cut)], far.at[at], far_sems.at[g])
+
+    near_copy = pltpu.make_async_copy(
+        dense.at[pl.ds(row_blocks - GROUP, GROUP), pl.ds(0, cut)], near, near_sem
+    )
     for g in range(tiles.pieces):
         tiles.start(g)
-    rows, width = values.held.shape
-    blocks = rows // EDGE
-    slab[rows:, :] = jnp.zeros((EDGE, width), BF16)
-    slab[:rows, :] = values.all()[...]
-    for g in range(tiles.pieces):
-        tiles.wait(g)
-        for b in range(g * GROUP, (g + 1) * GROUP):
-            right = []
-            for t in range(most):
-                c = column[b, t]
-                c = jnp.where((t < count[b]) & (c < blocks), c, blocks)
-                right.append(slab[block(c), :])
-            left = jnp.concatenate([tiles.held[b, t] for t in range(most)], axis=1)
-            partial.held[b * EDGE : (b + 1) * EDGE, :] = dot(left, jnp.concatenate(right, axis=0))
-        partial.start(g)
+    for b in range(row_blocks):
+        dense[b] = jnp.zeros(dense.shape[1:], BF16)
     slots = asked_column.held.shape[0]
     asked_row.held[...] = jnp.transpose(asked_column.all()[...].astype(F32))[0:8].astype(I32)
     lane = iota((slots, EDGE), 1) - iota((slots, EDGE), 0) % SLOTS
     mine = (lane == 2 * SLOTS) | (lane == 3 * SLOTS) | (lane == 4 * SLOTS)
     sums = jnp.sum(jnp.where(mine, slot_lines(arrived.all(), slots), 0.0), axis=1, keepdims=True)
     degree_row.held[...] = jnp.transpose(jnp.broadcast_to(sums, (slots, EDGE)))[0:8]
-
-
-def near(tile_count, tile_column, arrived, asked_column, values, tiles):
+    values = values.all()
+    for g in range(tiles.pieces):
+        tiles.wait(g)
+        densify(count, column, tiles.held, dense, g)
+        far_copy(g).start()
+        if g == tiles.pieces - 1:
+            near_copy.start()
+        for b in range(g * GROUP, (g + 1) * GROUP):
+            at = slice(b * EDGE, (b + 1) * EDGE)
+            partial.held[at, :] = dot(flat(dense, (b,), range(cut)), values[...])
+            if g < degree.pieces:
+                weights = dense[b, 0].astype(F32)
+                for c in range(1, last):
+                    weights += dense[b, c].astype(F32)
+                total = jnp.sum(weights, axis=1, keepdims=True)
+                degree.held[at, :] = jnp.broadcast_to(total, (EDGE, EDGE))
+        partial.start(g)
+        if g < degree.pieces:
+            degree.start(g)
+    for g in range(tiles.pieces):
+        far_copy(g).wait()
+    near_copy.wait()
+
+
+def near(tile_count, tile_column, tiles, values, arrived, asked_column):
     rows, width = values.shape
     slots, row_blocks = asked_column.shape[0], tiles.shape[0]
+    masters = rows // EDGE
+    sems = pltpu.SemaphoreType.DMA((groups(tiles),))
     return run(
         near_kernel,
         (tile_count, tile_column),
-        ((values, 1), (arrived, 1), (asked_column, 1), (tiles, groups(tiles))),
+        ((values, 1), (tiles, groups(tiles)), (arrived, 1), (asked_column, 1)),
         (
             (struct(row_blocks * EDGE, width, dtype=F32), groups(tiles), 0),
+            (struct(rows, EDGE, dtype=F32), masters // GROUP, 0),
             (struct(8, slots, dtype=I32), 1, 0),
             (struct(8, slots, dtype=F32), 1, 0),
-        ),
-        (pltpu.VMEM((rows + EDGE, width), BF16),),
+            (struct(GROUP, masters, EDGE, EDGE), 0, 0),
+            (struct(row_blocks, row_blocks - masters, EDGE, EDGE), 0, 0),
+        ),
+        (
+            pltpu.VMEM((row_blocks, row_blocks + 1, EDGE, EDGE), BF16),
+            sems,
+            pltpu.SemaphoreType.DMA,
+        ),
         flops=5e9,
     )
 
 
-def far_product(n, column, b, tiles, padded, first):
-    blocks = padded.shape[0] // EDGE - 1
-    right = []
-    for t in range(tiles.shape[1]):
-        c = column[b, t]
-        c = jnp.where((t < n) & (c >= first), c - first, blocks)
-        right.append(padded[block(c), :])
-    left = jnp.concatenate([tiles[b, t] for t in range(tiles.shape[1])], axis=1)
-    return dot(left, jnp.concatenate(right, axis=0))
-
-
-def mirror_out_kernel(scalars, ins, outs, total):
-    count, column = scalars
+def mirror_out_kernel(scalars, ins, outs):
     arrived, slot_column, partial, tiles, slot_row = ins
-    send, padded = outs
-    mirrors = total.shape[0]
-    blocks = mirrors // EDGE
-    first = tiles.held.shape[0] - blocks
+    send, slab = outs
     last = tiles.pieces - 1
     tiles.start(last)
     partial.start(last)
     pick = pick_columns(slot_column.all()[...], 0, arrived.held.shape[0])
-    padded.held[:mirrors, :] = dot(pick, arrived.all()[...]).astype(BF16)
-    padded.held[mirrors:, :] = jnp.zeros((EDGE, padded.held.shape[1]), BF16)
-    padded.start()
+    slab.held[...] = dot(pick, arrived.all()[...]).astype(BF16)
+    slab.start()
+    tiles.wait(last)
+    blocks = range(tiles.held.shape[1])
+    left = flat(tiles.held, [last * GROUP + b for b in blocks], blocks)
+    more = dot(left, slab.held[...])
     partial.wait(last)
-    tiles.wait(last)
-    for b in range(first, first + blocks):
-        more = far_product(count[b], column, b, tiles.held, padded.held, first)
-        total[(b - first) * EDGE : (b - first + 1) * EDGE, :] = (
-            partial.held[b * EDGE : (b + 1) * EDGE, :] + more
-        ).astype(BF16)
+    total = (partial.held[partial.rows(last), :] + more).astype(BF16)
     slots = send.held.shape[0]
-    send.held[...] = dot(pick_rows(slots, 0, slot_row.all()[...]), total[...]).astype(BF16)
-
-
-def mirror_out(tile_count, tile_column, arrived, slot_column, slot_row, partial, tiles):
+    send.held[...] = dot(pick_rows(slots, 0, slot_row.all()[...]), total).astype(BF16)
+
+
+def mirror_out(arrived, slot_column, slot_row, partial, tiles):
     slots, width = arrived.shape
     mirrors = slot_row.shape[1]
     return run(
         mirror_out_kernel,
-        (tile_count, tile_column),
+        (),
         (
             (arrived, 1),
             (slot_column, 1),
@@ -326,58 +354,48 @@
             (tiles, groups(tiles)),
             (slot_row, 1),
         ),
-        ((struct(slots, width), 1, 0), (struct(mirrors + EDGE, width), 1, 0)),
-        (pltpu.VMEM((mirrors, width), BF16),),
+        ((struct(slots, width), 1, 0), (struct(mirrors, width), 1, 0)),
         flops=2e9,
     )
 
 
 def far_kernel(scalars, ins, outs):
-    count, column = scalars
-    padded, asked_row, degree_row, tiles, partial, own = ins
+    slab, asked_row, degree_row, tiles, partial, own, degree = ins
     base, scale = outs
     for g in range(own.pieces):
-        for source in (tiles, partial, own):
+        for source in (tiles, partial, own, degree):
             source.start(g)
-    row_blocks, most = base.held.shape[0] // EDGE, tiles.held.shape[1]
-    padded, asked, degrees = padded.all(), asked_row.all()[0:1], degree_row.all()[0:1]
+    slab, asked, degrees = slab.all(), asked_row.all()[0:1], degree_row.all()[0:1]
+    rows = own.size
     for g in range(own.pieces):
-        for source in (tiles, partial, own):
+        for source in (tiles, partial, own, degree):
             source.wait(g)
-        for b in range(g * GROUP, (g + 1) * GROUP):
-            at = slice(b * EDGE, (b + 1) * EDGE)
-            total = partial.held[at, :] + far_product(
-                count[b], column, b, tiles.held, padded, row_blocks
-            )
-            weights = jnp.zeros((EDGE, EDGE), F32)
-            for t in range(most):
-                used = jnp.where(t < count[b], 1.0, 0.0)
-                weights += tiles.held[b, t].astype(F32) * used
-            hit = iota((EDGE, asked.shape[1]), 0) + b * EDGE == asked
-            given = jnp.where(hit, degrees, 0.0)
-            for k in range(asked.shape[1] // EDGE):
-                weights += given[:, k * EDGE : (k + 1) * EDGE]
-            degree = jnp.sum(weights, axis=1, keepdims=True)
-            factor = jnp.broadcast_to(1.0 / (1.0 + degree), (EDGE, EDGE))
-            scale.held[at, :] = factor
-            base.held[at, :] = own.held[at, :] + total * jnp.concatenate([factor, factor], axis=1)
+        at = own.rows(g)
+        left = flat(tiles.held, range(g * GROUP, (g + 1) * GROUP), range(tiles.held.shape[1]))
+        total = partial.held[at, :] + dot(left, slab[...])
+        hit = iota((rows, asked.shape[1]), 0) + g * rows == asked
+        more = jnp.sum(jnp.where(hit, degrees, 0.0), axis=1, keepdims=True)
+        factor = 1.0 / (1.0 + (degree.held[at, :] + more))
+        scale.held[at, :] = factor
+        base.held[at, :] = own.held[at, :] + total * jnp.concatenate([factor, factor], axis=1)
         base.start(g)
     scale.start()
 
 
-def far(tile_count, tile_column, tiles, padded, partial, own, asked_row, degree_row):
+def far(tiles, slab, partial, degree, own, asked_row, degree_row):
     masters, width = own.shape
     n = masters // EDGE // GROUP
     return run(
         far_kernel,
-        (tile_count, tile_column),
-        (
-            (padded, 1),
+        (),
+        (
+            (slab, 1),
             (asked_row, 1),
             (degree_row, 1),
             (tiles, groups(tiles)),
             (partial, groups(tiles)),
             (own, n),
+            (degree, n),
         ),
         ((struct(masters, width, dtype=F32), n, 0), (struct(masters, EDGE, dtype=F32), 1, 0)),
         flops=5e9,
@@ -431,122 +449,104 @@
     )
 
 
-def add_back(n, column, b, tiles, values, total, low):
-    blocks = total.shape[0] - 1
-    for i in range(0, tiles.shape[1], 4):
-        right = jnp.concatenate([tiles[b, i + k] for k in range(4)], axis=1)
-        product = dot(values, right)
-        for k in range(4):
-            c = column[b, i + k] - low
-            c = jnp.where((i + k < n) & (c >= 0) & (c < blocks), c, blocks)
-            total[c] += product[:, k * EDGE : (k + 1) * EDGE]
-
-
-def back_near_kernel(scalars, ins, outs):
+def put_blocks(total, first, value):
+    for k in range(value.shape[1] // EDGE):
+        total[first + k] = value[:, k * EDGE : (k + 1) * EDGE]
+
+
+def back_near_kernel(scalars, ins, outs, dense):
     count, column = scalars
-    values, tiles = ins
+    tiles, values = ins
     (total,) = outs
-    blocks = values.held.shape[0] // EDGE
-    for g in range(blocks // GROUP):
+    rows = dense.shape[0]
+    for g in range(rows // GROUP):
         tiles.start(g)
-    total.held[...] = jnp.zeros(total.held.shape, F32)
-    values = values.all()
-    for g in range(blocks // GROUP):
+    for b in range(rows):
+        dense[b] = jnp.zeros(dense.shape[1:], BF16)
+    turned = jnp.transpose(values.all()[...].astype(F32)).astype(BF16)
+    for g in range(rows // GROUP):
         tiles.wait(g)
-
-        def body(b, carry):
-            turned = jnp.transpose(values[block(b), :].astype(F32)).astype(BF16)
-            add_back(count[b], column, b, tiles.held, turned, total.held, 0)
-            return carry
-
-        lax.fori_loop(g * GROUP, (g + 1) * GROUP, body, 0)
-
-
-def back_near(tile_count, tile_column, values, tiles):
+        densify(count, column, tiles.held, dense, g)
+    for g in range(total.pieces):
+        right = flat(dense, range(rows), range(g * GROUP, (g + 1) * GROUP))
+        put_blocks(total.held, g * GROUP, dot(turned, right))
+        total.start(g)
+
+
+def back_near(tile_count, tile_column, tiles, values):
     row_blocks, width = tiles.shape[0], values.shape[1]
+    n = groups(tiles)
     (total,) = run(
         back_near_kernel,
         (tile_count, tile_column),
-        ((values, 1), (tiles, groups(tiles))),
-        ((struct(row_blocks, width, EDGE, dtype=F32), 1, 1),),
+        ((tiles, n), (values, 1)),
+        ((struct(row_blocks, width, EDGE, dtype=F32), n, 0),),
+        (pltpu.VMEM((values.shape[0] // EDGE, row_blocks + 1, EDGE, EDGE), BF16),),
         flops=5e9,
     )
     return total
 
 
-def mirror_back_kernel(scalars, ins, outs, total, rows, sem):
-    count, column = scalars
+def mirror_back_kernel(scalars, ins, outs):
     arrived, slot_column, tiles, partial, slot_row = ins
     send, turned = outs
-    blocks = turned.held.shape[0]
-    first = tiles.held.shape[0] - blocks
     last = tiles.pieces - 1
     tiles.start(last)
-    copy = pltpu.make_async_copy(partial.at[pl.ds(first, blocks)], total.at[pl.ds(0, blocks)], sem)
-    copy.start()
+    partial.start(last)
     pick = pick_columns(slot_column.all()[...], 0, arrived.held.shape[0])
-    slab = dot(pick, arrived.all()[...])
-    for b in range(blocks):
-        turned.held[b] = jnp.transpose(slab[b * EDGE : (b + 1) * EDGE]).astype(BF16)
+    turned.held[...] = jnp.transpose(dot(pick, arrived.all()[...])).astype(BF16)
     turned.start()
-    total[blocks] = jnp.zeros(total.shape[1:], F32)
-    copy.wait()
     tiles.wait(last)
-    for b in range(blocks):
-        add_back(count[first + b], column, first + b, tiles.held, turned.held[b], total, first)
-    for c in range(blocks):
-        rows[c * EDGE : (c + 1) * EDGE, :] = jnp.transpose(total[c]).astype(BF16)
+    blocks = range(tiles.held.shape[1])
+    right = flat(tiles.held, [last * GROUP + b for b in blocks], blocks)
+    more = dot(turned.held[...], right)
+    partial.wait(last)
+    own = jnp.concatenate([partial.held[last * GROUP + c] for c in blocks], axis=1)
+    rows = jnp.transpose(own + more).astype(BF16)
     slots = send.held.shape[0]
-    send.held[...] = dot(pick_rows(slots, 0, slot_row.all()[...]), rows[...]).astype(BF16)
-
-
-def mirror_back(tile_count, tile_column, arrived, slot_column, slot_row, partial, tiles):
+    send.held[...] = dot(pick_rows(slots, 0, slot_row.all()[...]), rows).astype(BF16)
+
+
+def mirror_back(arrived, slot_column, slot_row, partial, tiles):
     slots, width = arrived.shape
     mirrors = slot_row.shape[1]
-    blocks = mirrors // EDGE
     return run(
         mirror_back_kernel,
-        (tile_count, tile_column),
-        ((arrived, 1), (slot_column, 1), (tiles, groups(tiles)), (partial, 0), (slot_row, 1)),
-        ((struct(slots, width), 1, 0), (struct(blocks, width, EDGE), 1, 0)),
-        (
-            pltpu.VMEM((blocks + 1, width, EDGE), F32),
-            pltpu.VMEM((mirrors, width), BF16),
-            pltpu.SemaphoreType.DMA,
-        ),
+        (),
+        (
+            (arrived, 1),
+            (slot_column, 1),
+            (tiles, groups(tiles)),
+            (partial, groups(tiles)),
+            (slot_row, 1),
+        ),
+        ((struct(slots, width), 1, 0), (struct(width, mirrors), 1, 0)),
         flops=2e9,
     )
 
 
-def back_far_kernel(scalars, ins, outs, sem):
-    count, column = scalars
-    turned, partial, tiles = ins
+def back_far_kernel(scalars, ins, outs):
+    tiles, turned, partial = ins
     (total,) = outs
-    blocks = turned.held.shape[0]
-    masters = total.held.shape[0] - 1
-    copy = pltpu.make_async_copy(partial.at[pl.ds(0, masters)], total.held.at[pl.ds(0, masters)], sem)
-    copy.start()
-    tiles.start(tiles.pieces - 1)
-    total.held[masters] = jnp.zeros(total.held.shape[1:], F32)
-    turned.all()
-    copy.wait()
-    tiles.wait(tiles.pieces - 1)
-
-    def body(b, carry):
-        add_back(count[masters + b], column, masters + b, tiles.held, turned.held[b], total.held, 0)
-        return carry
-
-    lax.fori_loop(0, blocks, body, 0)
-
-
-def back_far(tile_count, tile_column, tiles, turned, partial):
-    blocks, width = turned.shape[:2]
+    for g in range(total.pieces):
+        partial.start(g)
+    tiles, turned = tiles.all(), turned.all()
+    for g in range(total.pieces):
+        columns = range(g * GROUP, (g + 1) * GROUP)
+        right = flat(tiles, range(tiles.shape[0]), columns)
+        partial.wait(g)
+        own = jnp.concatenate([partial.held[c] for c in columns], axis=1)
+        put_blocks(total.held, g * GROUP, own + dot(turned[...], right))
+        total.start(g)
+
+
+def back_far(tiles, turned, partial):
+    width, masters = turned.shape[0], tiles.shape[1]
     (total,) = run(
         back_far_kernel,
-        (tile_count, tile_column),
-        ((turned, 1), (partial, 0), (tiles, groups(tiles))),
-        ((struct(tiles.shape[0] - blocks, width, EDGE, dtype=F32), 1, 1),),
-        (pltpu.SemaphoreType.DMA,),
+        (),
+        ((tiles, 1), (turned, 1), (partial, groups(partial))),
+        ((struct(masters, width, EDGE, dtype=F32), masters // GROUP, 0),),
         flops=3e9,
     )
     return total
@@ -697,32 +697,25 @@
     peer = mirror_master_part[:, 0]
     ask, slot_row, slot_column = place(tile_count, peer, mirror_row, tile_weight, parts)
     asked = exchange(ask)
-    tiles = tile_weight
     projected = jnp.dot(features, w_neigh, preferred_element_type=F32).astype(BF16)
     own = jnp.dot(features, w_self, preferred_element_type=F32)
     rows, asked_column = fetch(asked, projected, slots)
     arrived = exchange(rows)
-    partial, asked_row, degree_row = near(
-        tile_count, tile_column, asked, asked_column, projected, tiles
-    )
-    send, padded = mirror_out(
-        tile_count, tile_column, arrived, slot_column, slot_row, partial, tiles
-    )
+    partial, degree, asked_row, degree_row, near_tiles, far_tiles = near(
+        tile_count, tile_column, tile_weight, projected, asked, asked_column
+    )
+    send, slab = mirror_out(arrived, slot_column, slot_row, partial, far_tiles)
     back = exchange(send)
-    base, scale = far(
-        tile_count, tile_column, tiles, padded, partial, own, asked_row, degree_row
-    )
+    base, scale = far(far_tiles, slab, partial, degree, own, asked_row, degree_row)
     mixed, low, spread, send = turn(base, scale, cotangent, back, asked_row, asked_column)
     arrived = exchange(send)
-    partial = back_near(tile_count, tile_column, spread, tiles)
+    partial = back_near(tile_count, tile_column, tile_weight, spread)
     grad_self = lax.dot_general(
         features, low, (((0,), (0,)), ((), ())), preferred_element_type=F32
     ).astype(BF16)
-    send, turned = mirror_back(
-        tile_count, tile_column, arrived, slot_column, slot_row, partial, tiles
-    )
+    send, turned = mirror_back(arrived, slot_column, slot_row, partial, far_tiles)
     back = exchange(send)
-    partial = back_far(tile_count, tile_column, tiles, turned, partial)
+    partial = back_far(near_tiles, turned, partial)
     d_projected, keep, give = finish(core, partial, back, asked_column, features, grad_self)
     pair = (keep + to_other_core(give).astype(F32)).astype(BF16)
     same = ("chip", "local")

time: 188 us -> 179 us (0.952)
  Pallas kernels: 80.7 us -> 70.5 us
  waiting for transfers between devices: 24.8 us -> 31.8 us
  starting transfers between devices: 52.3 us -> 46.6 us
    pallas_call x11, Pallas kernels: 76.5 us -> 66.3 us  [run(): pl.pallas_call(body, in_specs=[smem] * len(scalars) + [any_space] * n, ou...]
    all_to_all x6, waiting for transfers between devices: 21.7 us -> 28.8 us  [exchange(): lax.all_to_all(buffer.reshape(parts, buffer.shape[0] // parts, buffer.sha...]
    all_to_all x6, starting transfers between devices: 48.8 us -> 43.4 us  [exchange(): lax.all_to_all(buffer.reshape(parts, buffer.shape[0] // parts, buffer.sha...]
  transfers between devices with their start and end apart: 8 -> 8, of which waited for: 7 -> 7; matrix products, arithmetic and copies ran while one was open for 5% -> 5% of each run, Pallas kernels for 24% -> 21%
where the time goes in v3:
time: 179 us; the launch traced here: 178 us
  Pallas kernels  70.5 us (39%)
  starting transfers between devices  46.6 us (26%)
  waiting for transfers between devices  31.8 us (18%)
  blocking collectives  15 us (8%)
  matrix products  8.63 us (5%)
  local copies, waits for them, and re-layouts  2.81 us (2%)
  other arithmetic  1.96 us (1%)
    pallas_call x11, Pallas kernels, run(): pl.pallas_call(body, in_specs=[smem] * len(scalars) + [any_space] * n, ou...  66.3 us
    all_to_all x6, starting transfers between devices, exchange(): lax.all_to_all(buffer.reshape(parts, buffer.shape[0] // parts, buffer.sha...  43.4 us
    all_to_all x6, waiting for transfers between devices, exchange(): lax.all_to_all(buffer.reshape(parts, buffer.shape[0] // parts, buffer.sha...  28.8 us
    all_to_all x1, blocking collectives, exchange(): lax.all_to_all(buffer.reshape(parts, buffer.shape[0] // parts, buffer.sha...  15 us
  transfers between devices with their start and end apart: 8, of which 7 were waited for; matrix products, arithmetic and copies ran while one was open for 5% of the time, Pallas kernels for 21%

profile of v3, /device:TPU:1, one launch (start us, length us, event | category | flops | bytes accessed | tf_op | source)
XLA Modules:
  0.0 178.2 jit_solution(5157334749586919709)
XLA Ops:
  0.6 4.2 %shard_map.120 = (f32[128,128]{1,0:T(8,128)}, s32[1,512]{1,0:T(1,128)}, s32[512,128]{1,0:T(8,128)}) custom-call(s32[20]{0:T(128)} %refs_0_.5, s32[1,512]{1,0:T(1,128)} %bitcast.34, s32[1,512]{1,0:T(1,128)} %bitcast.35, bf16[20,16,128,128]{3,2,1,0:T(8,128)(2,1)} %refs_2_.2), custom_call_target="tpu_custom_call" | custom-call | flops 1000000000 | bytes 4194304 | tf_op jit(solution)/shard_map/pallas_call | solution.py:102
  4.9 11.5 %all-to-all-start = ((f32[128,1,128]{2,1,0:T(1,128)}), f32[128,1,128]{2,1,0:T(1,128)S(1)}, u32[]{:S(2)}, u32[]{:S(2)}) async-start(f32[128,1,128]{2,1,0:T(1,128)} %bitcast.33), calls=%async_computation | async-start | bytes 131072 | tf_op jit(solution)/shard_map/all_to_all | solution.py:668
  16.4 3.0 %convolution_convert_fusion.refs_1_.refs_2_ = bf16[2048,256]{1,0:T(8,128)(2,1)} fusion(bf16[2048,768]{1,0:T(8,128)(2,1)S(1)} %copy-done, bf16[768,256]{1,0:T(8,128)(2,1)} %refs_3_.5), kind=kOutput, calls=%fused_computation | convolution fusion | flops 805830656 | bytes 4587520 | tf_op jit(solution)/shard_map/dot_general | solution.py:700
  19.3 6.9 %all-to-all-done = f32[128,1,128]{2,1,0:T(1,128)S(1)} async-done(((f32[128,1,128]{2,1,0:T(1,128)}), f32[128,1,128]{2,1,0:T(1,128)S(1)}, u32[]{:S(2)}, u32[]{:S(2)}) %all-to-all-start) | async-done | bytes 65568 | tf_op jit(solution)/shard_map/all_to_all | solution.py:668
  26.8 3.3 %shard_map.121 = (bf16[1024,256]{1,0:T(8,128)(2,1)}, s32[1024,128]{1,0:T(8,128)}) custom-call(f32[128,128]{1,0:T(8,128)} %bitcast.31, bf16[2048,256]{1,0:T(8,128)(2,1)} %convolution_convert_fusion.refs_1_.refs_2_), custom_call_target="tpu_custom_call" | custom-call | flops 2000000000 | bytes 4194304 | tf_op jit(solution)/shard_map/pallas_call | solution.py:102
  30.2 4.9 %all-to-all-start.1 = ((bf16[128,8,256]{2,1,0:T(8,128)(2,1)}), bf16[128,8,256]{2,1,0:T(8,128)(2,1)}, u32[]{:S(2)}, u32[]{:S(2)}) async-start(bf16[128,8,256]{2,1,0:T(8,128)(2,1)} %bitcast.28), calls=%async_computation.1 | async-start | bytes 1048576 | tf_op jit(solution)/shard_map/all_to_all | solution.py:668
  35.7 13.3 %shard_map.122 = (f32[2560,256]{1,0:T(8,128)}, f32[2048,128]{1,0:T(8,128)}, s32[8,1024]{1,0:T(8,128)}, f32[8,1024]{1,0:T(8,128)}, bf16[4,16,128,128]{3,2,1,0:T(8,128)(2,1)}, /*index=5*/bf16[20,4,128,128]{3,2,1,0:T(8,128)(2,1)}) custom-call(s32[20]{0:T(128)} %refs_0_.5, s32[20,16]{1,0:T(8,128)} %copy.17.refs_1_, ...), custom_call_target="tpu_custom_call" | custom-call | flops 5000000000 | bytes 4194304 | tf_op jit(solution)/shard_map/pallas_call | solution.py:102
  49.0 4.1 %shard_map.123 = (bf16[1024,256]{1,0:T(8,128)(2,1)}, bf16[512,256]{1,0:T(8,128)(2,1)}) custom-call(bf16[1024,256]{1,0:T(8,128)(2,1)} %bitcast.6.refs_0_, s32[512,128]{1,0:T(8,128)} %get-tuple-element.36.refs_1_, f32[2560,256]{1,0:T(8,128)} %get-tuple-element.37.refs_2_.refs_4_, bf16[20,4,128,128]{3,2,1,0:T(8,128)(2,1)} %get-tuple-element.38.refs_3_.refs_2_, ...), custom_call_target="tpu_custom_call" | custom-call | flops 2000000000 | bytes 4194304 | tf_op jit(solution)/shard_map/pallas_call | solution.py:102
  53.1 11.0 %all-to-all-start.2 = ((bf16[128,8,256]{2,1,0:T(8,128)(2,1)}), bf16[128,8,256]{2,1,0:T(8,128)(2,1)}, u32[]{:S(2)}, u32[]{:S(2)}) async-start(bf16[128,8,256]{2,1,0:T(8,128)(2,1)} %bitcast.29), calls=%async_computation.2 | async-start | bytes 1048576 | tf_op jit(solution)/shard_map/all_to_all | solution.py:668
  64.2 2.4 %fusion.1.refs_5_ = f32[2048,256]{1,0:T(8,128)} fusion(bf16[2048,768]{1,0:T(8,128)(2,1)S(1)} %copy-done, bf16[768,256]{1,0:T(8,128)(2,1)S(1)} %copy-done.4), kind=kOutput, calls=%fused_computation.4 | convolution fusion | flops 805306368 | bytes 5636096 | tf_op jit(solution)/shard_map/dot_general | solution.py:701
  66.5 5.9 %shard_map.124 = (f32[2048,256]{1,0:T(8,128)}, f32[2048,128]{1,0:T(8,128)}) custom-call(bf16[512,256]{1,0:T(8,128)(2,1)} %get-tuple-element.41.refs_0_, s32[8,1024]{1,0:T(8,128)} %get-tuple-element.34.refs_1_.refs_0_, f32[8,1024]{1,0:T(8,128)} %get-tuple-element.42.refs_2_, bf16[20,4,128,128]{3,2,1,0:T(8,128)(2,1)} %get-tuple-element.38.refs_3_.refs_2_, ...), custom_call_target="tpu_custom_call" | custom-call | flops 5000000000 | bytes 4194304 | tf_op jit(solution)/shard_map/pallas_call | solution.py:102
  72.4 5.5 %all-to-all-done.2 = bf16[128,8,256]{2,1,0:T(8,128)(2,1)} async-done(((bf16[128,8,256]{2,1,0:T(8,128)(2,1)}), bf16[128,8,256]{2,1,0:T(8,128)(2,1)}, u32[]{:S(2)}, u32[]{:S(2)}) %all-to-all-start.2) | async-done | bytes 524320 | tf_op jit(solution)/shard_map/all_to_all | solution.py:668
  77.9 6.5 %shard_map.125 = (bf16[2048,256]{1,0:T(8,128)(2,1)}, bf16[2048,256]{1,0:T(8,128)(2,1)}, bf16[2048,256]{1,0:T(8,128)(2,1)}, bf16[1024,256]{1,0:T(8,128)(2,1)}) custom-call(s32[8,1024]{1,0:T(8,128)} %get-tuple-element.34.refs_1_.refs_0_, bf16[1024,256]{1,0:T(8,128)(2,1)} %bitcast.8.refs_1_, f32[2048,256]{1,0:T(8,128)} %get-tuple-element.44.refs_2_, ...), custom_call_target="tpu_custom_call" | custom-call | flops 3000000000 | bytes 4194304 | tf_op jit(solution)/shard_map/pallas_call | solution.py:102
  84.4 4.8 %all-to-all-start.3 = ((bf16[128,8,256]{2,1,0:T(8,128)(2,1)}), bf16[128,8,256]{2,1,0:T(8,128)(2,1)}, u32[]{:S(2)}, u32[]{:S(2)}) async-start(bf16[128,8,256]{2,1,0:T(8,128)(2,1)} %bitcast.27), calls=%async_computation.3 | async-start | bytes 1048576 | tf_op jit(solution)/shard_map/all_to_all | solution.py:668
  89.2 9.8 %shard_map.126.refs_3_.refs_2_ = f32[20,256,128]{2,1,0:T(8,128)} custom-call(s32[20]{0:T(128)} %refs_0_.5, s32[20,16]{1,0:T(8,128)} %copy.17.refs_1_, bf16[20,16,128,128]{3,2,1,0:T(8,128)(2,1)} %refs_2_.2, bf16[2048,256]{1,0:T(8,128)(2,1)} %get-tuple-element.48.refs_3_), custom_call_target="tpu_custom_call" | custom-call | flops 5000000000 | bytes 4194304 | tf_op jit(solution)/shard_map/pallas_call | solution.py:102
  99.0 4.1 %all-to-all-done.3 = bf16[128,8,256]{2,1,0:T(8,128)(2,1)} async-done(((bf16[128,8,256]{2,1,0:T(8,128)(2,1)}), bf16[128,8,256]{2,1,0:T(8,128)(2,1)}, u32[]{:S(2)}, u32[]{:S(2)}) %all-to-all-start.3) | async-done | bytes 524320 | tf_op jit(solution)/shard_map/all_to_all | solution.py:668
  103.1 4.2 %shard_map.127 = (bf16[1024,256]{1,0:T(8,128)(2,1)}, bf16[256,512]{1,0:T(8,128)(2,1)}) custom-call(bf16[1024,256]{1,0:T(8,128)(2,1)} %bitcast.11.refs_0_, s32[512,128]{1,0:T(8,128)} %get-tuple-element.36.refs_1_, bf16[20,4,128,128]{3,2,1,0:T(8,128)(2,1)} %get-tuple-element.38.refs_3_.refs_2_, f32[20,256,128]{2,1,0:T(8,128)} %shard_map.126.refs_3_.refs_2_, ...), custom_call_target="tpu_custom_call" | custom-call | flops 2000000000 | bytes 4194304 | tf_op jit(solution)/shard_map/pallas_call | solution.py:102
  107.3 6.6 %all-to-all-start.4 = ((bf16[128,8,256]{2,1,0:T(8,128)(2,1)}), bf16[128,8,256]{2,1,0:T(8,128)(2,1)}, u32[]{:S(2)}, u32[]{:S(2)}) async-start(bf16[128,8,256]{2,1,0:T(8,128)(2,1)} %bitcast.30), calls=%async_computation.4 | async-start | bytes 1048576 | tf_op jit(solution)/shard_map/all_to_all | solution.py:668
  113.9 3.3 %fusion.refs_5_ = bf16[768,256]{1,0:T(8,128)(2,1)} fusion(bf16[2048,256]{1,0:T(8,128)(2,1)} %get-tuple-element.52.refs_0_, bf16[2048,768]{1,0:T(8,128)(2,1)S(1)} %copy-done), kind=kOutput, calls=%fused_computation.2 | convolution fusion | flops 805502976 | bytes 4587520 | tf_op jit(solution)/shard_map/dot_general | solution.py:713
  117.2 4.2 %shard_map.128.refs_3_ = f32[16,256,128]{2,1,0:T(8,128)} custom-call(bf16[4,16,128,128]{3,2,1,0:T(8,128)(2,1)} %get-tuple-element.50.refs_0_, bf16[256,512]{1,0:T(8,128)(2,1)} %get-tuple-element.51.refs_1_, f32[20,256,128]{2,1,0:T(8,128)} %shard_map.126.refs_3_.refs_2_), custom_call_target="tpu_custom_call" | custom-call | flops 3000000000 | bytes 4194304 | tf_op jit(solution)/shard_map/pallas_call | solution.py:102
  121.5 6.2 %all-to-all-done.4 = bf16[128,8,256]{2,1,0:T(8,128)(2,1)} async-done(((bf16[128,8,256]{2,1,0:T(8,128)(2,1)}), bf16[128,8,256]{2,1,0:T(8,128)(2,1)}, u32[]{:S(2)}, u32[]{:S(2)}) %all-to-all-start.4) | async-done | bytes 524320 | tf_op jit(solution)/shard_map/all_to_all | solution.py:668
  127.7 6.0 %shard_map.129 = (bf16[256,2048]{1,0:T(8,128)(2,1)}, f32[1536,128]{1,0:T(8,128)}, bf16[1536,128]{1,0:T(8,128)(2,1)}) custom-call(s32[1]{0:T(128)} %bitcast.9.refs_0_.core, bf16[1024,256]{1,0:T(8,128)(2,1)} %bitcast.13.refs_1_, s32[1024,128]{1,0:T(8,128)} %get-tuple-element.33.refs_5_.refs_2_, f32[16,256,128]{2,1,0:T(8,128)} %shard_map.128.refs_3_, ...), custom_call_target="tpu_custom_call" | custom-call | flops 3000000000 | bytes 4194304 | tf_op jit(solution)/shard_map/pallas_call | solution.py:102
  134.1 1.7 collective-permute-done
  135.8 2.0 %add_convert_fusion = bf16[1536,128]{1,0:T(8,128)(2,1)} fusion(f32[1536,128]{1,0:T(8,128)} %get-tuple-element.53, bf16[1536,128]{1,0:T(8,128)(2,1)S(1)} %collective-permute-done), kind=kLoop, calls=%fused_computation.3 | loop fusion | flops 589824 | bytes 1572864 | tf_op jit(solution)/shard_map/convert_element_type | solution.py:720
  137.7 4.6 %all-to-all-start.5 = ((bf16[64,24,128]{2,1,0:T(8,128)(2,1)}), bf16[64,24,128]{2,1,0:T(8,128)(2,1)S(1)}, u32[]{:S(2)}, u32[]{:S(2)}) async-start(bf16[64,24,128]{2,1,0:T(8,128)(2,1)} %bitcast.15), calls=%async_computation.5 | async-start | bytes 786432 | tf_op jit(solution)/shard_map/all_to_all | solution.py:668
  142.3 4.8 %shard_map.130 = bf16[2048,768]{1,0:T(8,128)(2,1)} custom-call(bf16[2048,256]{1,0:T(8,128)(2,1)} %get-tuple-element.52.refs_0_, bf16[256,2048]{1,0:T(8,128)(2,1)} %get-tuple-element.55.refs_1_, bf16[768,256]{1,0:T(8,128)(2,1)} %refs_2_.3, bf16[768,256]{1,0:T(8,128)(2,1)} %refs_3_.5), custom_call_target="tpu_custom_call" | custom-call | flops 3000000000 | bytes 4194304 | tf_op jit(solution)/shard_map/pallas_call | solution.py:102
  147.2 6.1 %all-to-all-done.5.parts = bf16[64,24,128]{2,1,0:T(8,128)(2,1)S(1)} async-done(((bf16[64,24,128]{2,1,0:T(8,128)(2,1)}), bf16[64,24,128]{2,1,0:T(8,128)(2,1)S(1)}, u32[]{:S(2)}, u32[]{:S(2)}) %all-to-all-start.5) | async-done | bytes 393248 | tf_op jit(solution)/shard_map/all_to_all | solution.py:668
  154.0 1.8 %shard_map.131 = bf16[64,24,128]{2,1,0:T(8,128)(2,1)} custom-call(bf16[64,24,128]{2,1,0:T(8,128)(2,1)} %copy-done.1), custom_call_target="tpu_custom_call" | custom-call | flops 100000000 | bytes 4194304 | tf_op jit(solution)/shard_map/pallas_call | solution.py:637
  155.8 15.0 %all_to_all.35 = bf16[64,24,128]{2,1,0:T(8,128)(2,1)S(1)} all-to-all(bf16[64,24,128]{2,1,0:T(8,128)(2,1)} %shard_map.131), channel_id=1, replica_groups=mesh['chip'=16,'core'=2,'local'=4] {'chip','local'}, dimensions={0} | all-to-all | bytes 786432 | tf_op jit(solution)/shard_map/all_to_all | solution.py:668
  170.8 2.9 %collective-permute-start.1 = (bf16[1536,128]{1,0:T(8,128)(2,1)S(1)}, bf16[1536,128]{1,0:T(8,128)(2,1)S(1)}, u32[]{:S(2)}, u32[]{:S(2)}) collective-permute-start(bf16[1536,128]{1,0:T(8,128)(2,1)S(1)} %bitcast.25), channel_id=1, source_target_pairs={{0,4},{4,0},{1,5},{5,1},{2,6},{6,2},{3,7},{7,3},{8,12},{12,8},{9,1... | collective-permute-start | bytes 1179656 | tf_op jit(solution)/shard_map/ppermute | solution.py:679
  173.7 1.3 collective-permute-done.1.other
  175.8 2.4 %shard_map.132 = (f32[768,256]{1,0:T(8,128)}, f32[768,256]{1,0:T(8,128)}) custom-call(s32[1]{0:T(128)} %bitcast.9.refs_0_.core, bf16[1536,128]{1,0:T(8,128)(2,1)} %bitcast.26, bf16[1536,128]{1,0:T(8,128)(2,1)} %copy-done.3), custom_call_target="tpu_custom_call" | custom-call | flops 100000000 | bytes 4194304 | tf_op jit(solution)/shard_map/pallas_call | solution.py:656
  (17 shorter events, 3.1 us)
Async XLA Ops:
  0.6 15.7 %copy-start = (bf16[2048,768]{1,0:T(8,128)(2,1)S(1)}, bf16[2048,768]{1,0:T(8,128)(2,1)}, u32[]{:S(2)}) copy-start(bf16[2048,768]{1,0:T(8,128)(2,1)} %refs_4_.3) | copy-start | bytes 9437188
  4.9 21.3 %all-to-all-start = ((f32[128,1,128]{2,1,0:T(1,128)}), f32[128,1,128]{2,1,0:T(1,128)S(1)}, u32[]{:S(2)}, u32[]{:S(2)}) async-start(f32[128,1,128]{2,1,0:T(1,128)} %bitcast.33), calls=%async_computation | async-start | bytes 131072 | tf_op jit(solution)/shard_map/all_to_all | solution.py:668
  26.2 0.6 copy-start.5
  26.8 8.2 %copy-start.6 = (s32[20,16]{0,1:T(8,128)S(1)}, s32[20,16]{0,1:T(8,128)}, u32[]{:S(2)}) copy-start(s32[20,16]{0,1:T(8,128)} %param.15) | copy-start | bytes 3844
  30.2 18.9 %all-to-all-start.1 = ((bf16[128,8,256]{2,1,0:T(8,128)(2,1)}), bf16[128,8,256]{2,1,0:T(8,128)(2,1)}, u32[]{:S(2)}, u32[]{:S(2)}) async-start(bf16[128,8,256]{2,1,0:T(8,128)(2,1)} %bitcast.28), calls=%async_computation.1 | async-start | bytes 1048576 | tf_op jit(solution)/shard_map/all_to_all | solution.py:668
  49.0 15.1 %copy-start.4 = (bf16[768,256]{1,0:T(8,128)(2,1)S(1)}, bf16[768,256]{1,0:T(8,128)(2,1)}, u32[]{:S(2)}) copy-start(bf16[768,256]{1,0:T(8,128)(2,1)} %refs_2_.3) | copy-start | bytes 1179652
  53.1 24.8 %all-to-all-start.2 = ((bf16[128,8,256]{2,1,0:T(8,128)(2,1)}), bf16[128,8,256]{2,1,0:T(8,128)(2,1)}, u32[]{:S(2)}, u32[]{:S(2)}) async-start(bf16[128,8,256]{2,1,0:T(8,128)(2,1)} %bitcast.29), calls=%async_computation.2 | async-start | bytes 1048576 | tf_op jit(solution)/shard_map/all_to_all | solution.py:668
  84.4 18.7 %all-to-all-start.3 = ((bf16[128,8,256]{2,1,0:T(8,128)(2,1)}), bf16[128,8,256]{2,1,0:T(8,128)(2,1)}, u32[]{:S(2)}, u32[]{:S(2)}) async-start(bf16[128,8,256]{2,1,0:T(8,128)(2,1)} %bitcast.27), calls=%async_computation.3 | async-start | bytes 1048576 | tf_op jit(solution)/shard_map/all_to_all | solution.py:668
  107.3 20.4 %all-to-all-start.4 = ((bf16[128,8,256]{2,1,0:T(8,128)(2,1)}), bf16[128,8,256]{2,1,0:T(8,128)(2,1)}, u32[]{:S(2)}, u32[]{:S(2)}) async-start(bf16[128,8,256]{2,1,0:T(8,128)(2,1)} %bitcast.30), calls=%async_computation.4 | async-start | bytes 1048576 | tf_op jit(solution)/shard_map/all_to_all | solution.py:668
  133.7 2.0 %collective-permute-start = (bf16[1536,128]{1,0:T(8,128)(2,1)}, bf16[1536,128]{1,0:T(8,128)(2,1)S(1)}, u32[]{:S(2)}, u32[]{:S(2)}) collective-permute-start(bf16[1536,128]{1,0:T(8,128)(2,1)} %get-tuple-element.54), channel_id=1, source_target_pairs={{0,4},{4,0},{1,5},{5,1},{2,6},{6,2},{3,7},{7,3},{8,12},{12,8},{9,1... | collective-permute-start | bytes 1179656 | tf_op jit(solution)/shard_map/ppermute | solution.py:679
  137.7 15.5 %all-to-all-start.5 = ((bf16[64,24,128]{2,1,0:T(8,128)(2,1)}), bf16[64,24,128]{2,1,0:T(8,128)(2,1)S(1)}, u32[]{:S(2)}, u32[]{:S(2)}) async-start(bf16[64,24,128]{2,1,0:T(8,128)(2,1)} %bitcast.15), calls=%async_computation.5 | async-start | bytes 786432 | tf_op jit(solution)/shard_map/all_to_all | solution.py:668
  153.3 0.7 copy-start.1
  170.8 4.2 %copy-start.2 = (bf16[64,24,128]{2,1,0:T(8,128)(2,1)}, bf16[64,24,128]{2,1,0:T(8,128)(2,1)S(1)}, u32[]{:S(2)}) copy-start(bf16[64,24,128]{2,1,0:T(8,128)(2,1)S(1)} %all_to_all.35) | copy-start | bytes 1179652
  170.8 4.2 %collective-permute-start.1 = (bf16[1536,128]{1,0:T(8,128)(2,1)S(1)}, bf16[1536,128]{1,0:T(8,128)(2,1)S(1)}, u32[]{:S(2)}, u32[]{:S(2)}) collective-permute-start(bf16[1536,128]{1,0:T(8,128)(2,1)S(1)} %bitcast.25), channel_id=1, source_target_pairs={{0,4},{4,0},{1,5},{5,1},{2,6},{6,2},{3,7},{7,3},{8,12},{12,8},{9,1... | collective-permute-start | bytes 1179656 | tf_op jit(solution)/shard_map/ppermute | solution.py:679
  175.1 0.8 copy-start.3

commit v4 on v3

--- a/solution.py
+++ b/solution.py
@@ -13,6 +13,7 @@
 MIB = 1024 * 1024
 VMEM_BYTES = 60 * MIB
 GROUP = 4
+AHEAD = 2
 ROOT = 0.7978845608028654
 CUBIC = 0.044715
 EVERY = ("chip", "core", "local")
@@ -69,6 +70,20 @@
                 self.wait(p)
         self.waited = True
         return self.held
+
+
+def begin(sources, pieces):
+    for g in range(min(AHEAD, pieces)):
+        for source in sources:
+            source.start(g)
+
+
+def take(sources, pieces, g):
+    for source in sources:
+        source.wait(g)
+    if g + AHEAD < pieces:
+        for source in sources:
+            source.start(g + AHEAD)
 
 
 def run(kernel, scalars, ins, outs, scratch=(), flops=1e9):
@@ -112,8 +127,8 @@
     )(*scalars, *[x for x, _ in ins])
 
 
-def params():
-    return pltpu.CompilerParams(vmem_limit_bytes=VMEM_BYTES)
+def params(limit=VMEM_BYTES):
+    return pltpu.CompilerParams(vmem_limit_bytes=limit)
 
 
 def cost(flops):
@@ -232,7 +247,7 @@
     return jnp.concatenate(lines, axis=0)
 
 
-def densify(count, column, tiles, dense, g):
+def densify(count, column, tiles, dense, g, first=0):
     members = range(g * GROUP, (g + 1) * GROUP)
     last = dense.shape[1] - 1
     longest = count[g * GROUP]
@@ -241,44 +256,33 @@
 
     def body(t, carry):
         for b in members:
-            c = jnp.where(t < count[b], column[b, t], last)
-            dense[b, c] = dense[b, c] + tiles[b, t]
+            c = jnp.where(t < count[b], column[t, b], last)
+            dense[b - first, c] = dense[b - first, c] + tiles[b, t]
         return carry
 
     lax.fori_loop(0, longest, body, 0)
 
 
-def near_kernel(scalars, ins, outs, dense, far_sems, near_sem):
+def near_kernel(scalars, ins, outs, dense, far_sems):
     count, column = scalars
-    values, tiles, arrived, asked_column = ins
-    partial, degree, asked_row, degree_row, near, far = outs
+    tiles, values = ins
+    partial, degree, far = outs
     row_blocks = tiles.held.shape[0]
-    cut, last = near.shape[1], dense.shape[1] - 1
+    last = dense.shape[1] - 1
+    cut = last - far.shape[1]
 
     def far_copy(g):
         at = pl.ds(g * GROUP, GROUP)
         return pltpu.make_async_copy(dense.at[at, pl.ds(cut, last - cut)], far.at[at], far_sems.at[g])
 
-    near_copy = pltpu.make_async_copy(
-        dense.at[pl.ds(row_blocks - GROUP, GROUP), pl.ds(0, cut)], near, near_sem
-    )
-    for g in range(tiles.pieces):
-        tiles.start(g)
+    begin((tiles,), tiles.pieces)
     for b in range(row_blocks):
         dense[b] = jnp.zeros(dense.shape[1:], BF16)
-    slots = asked_column.held.shape[0]
-    asked_row.held[...] = jnp.transpose(asked_column.all()[...].astype(F32))[0:8].astype(I32)
-    lane = iota((slots, EDGE), 1) - iota((slots, EDGE), 0) % SLOTS
-    mine = (lane == 2 * SLOTS) | (lane == 3 * SLOTS) | (lane == 4 * SLOTS)
-    sums = jnp.sum(jnp.where(mine, slot_lines(arrived.all(), slots), 0.0), axis=1, keepdims=True)
-    degree_row.held[...] = jnp.transpose(jnp.broadcast_to(sums, (slots, EDGE)))[0:8]
     values = values.all()
     for g in range(tiles.pieces):
-        tiles.wait(g)
+        take((tiles,), tiles.pieces, g)
         densify(count, column, tiles.held, dense, g)
         far_copy(g).start()
-        if g == tiles.pieces - 1:
-            near_copy.start()
         for b in range(g * GROUP, (g + 1) * GROUP):
             at = slice(b * EDGE, (b + 1) * EDGE)
             partial.held[at, :] = dot(flat(dense, (b,), range(cut)), values[...])
@@ -293,30 +297,24 @@
             degree.start(g)
     for g in range(tiles.pieces):
         far_copy(g).wait()
-    near_copy.wait()
-
-
-def near(tile_count, tile_column, tiles, values, arrived, asked_column):
+
+
+def near(tile_count, tile_column, tiles, values):
     rows, width = values.shape
-    slots, row_blocks = asked_column.shape[0], tiles.shape[0]
+    row_blocks = tiles.shape[0]
     masters = rows // EDGE
-    sems = pltpu.SemaphoreType.DMA((groups(tiles),))
     return run(
         near_kernel,
         (tile_count, tile_column),
-        ((values, 1), (tiles, groups(tiles)), (arrived, 1), (asked_column, 1)),
+        ((tiles, groups(tiles)), (values, 1)),
         (
             (struct(row_blocks * EDGE, width, dtype=F32), groups(tiles), 0),
             (struct(rows, EDGE, dtype=F32), masters // GROUP, 0),
-            (struct(8, slots, dtype=I32), 1, 0),
-            (struct(8, slots, dtype=F32), 1, 0),
-            (struct(GROUP, masters, EDGE, EDGE), 0, 0),
             (struct(row_blocks, row_blocks - masters, EDGE, EDGE), 0, 0),
         ),
         (
             pltpu.VMEM((row_blocks, row_blocks + 1, EDGE, EDGE), BF16),
-            sems,
-            pltpu.SemaphoreType.DMA,
+            pltpu.SemaphoreType.DMA((groups(tiles),)),
         ),
         flops=5e9,
     )
@@ -360,20 +358,26 @@
 
 
 def far_kernel(scalars, ins, outs):
-    slab, asked_row, degree_row, tiles, partial, own, degree = ins
-    base, scale = outs
-    for g in range(own.pieces):
-        for source in (tiles, partial, own, degree):
-            source.start(g)
-    slab, asked, degrees = slab.all(), asked_row.all()[0:1], degree_row.all()[0:1]
+    slab, arrived, asked_column, tiles, partial, own, degree = ins
+    base, scale, asked_row = outs
+    sources = (tiles, partial, own, degree)
+    begin(sources, own.pieces)
+    slots = asked_column.held.shape[0]
+    asked = jnp.transpose(asked_column.all()[...].astype(F32))[0:8].astype(I32)
+    asked_row.held[...] = asked
+    asked_row.start()
+    lane = iota((slots, EDGE), 1) - iota((slots, EDGE), 0) % SLOTS
+    mine = (lane == 2 * SLOTS) | (lane == 3 * SLOTS) | (lane == 4 * SLOTS)
+    sums = jnp.sum(jnp.where(mine, slot_lines(arrived.all(), slots), 0.0), axis=1, keepdims=True)
+    degrees = jnp.transpose(jnp.broadcast_to(sums, (slots, EDGE)))[0:1]
+    slab = slab.all()
     rows = own.size
     for g in range(own.pieces):
-        for source in (tiles, partial, own, degree):
-            source.wait(g)
+        take(sources, own.pieces, g)
         at = own.rows(g)
         left = flat(tiles.held, range(g * GROUP, (g + 1) * GROUP), range(tiles.held.shape[1]))
         total = partial.held[at, :] + dot(left, slab[...])
-        hit = iota((rows, asked.shape[1]), 0) + g * rows == asked
+        hit = iota((rows, slots), 0) + g * rows == asked[0:1]
         more = jnp.sum(jnp.where(hit, degrees, 0.0), axis=1, keepdims=True)
         factor = 1.0 / (1.0 + (degree.held[at, :] + more))
         scale.held[at, :] = factor
@@ -382,7 +386,7 @@
     scale.start()
 
 
-def far(tiles, slab, partial, degree, own, asked_row, degree_row):
+def far(tiles, slab, partial, degree, own, arrived, asked_column):
     masters, width = own.shape
     n = masters // EDGE // GROUP
     return run(
@@ -390,14 +394,18 @@
         (),
         (
             (slab, 1),
-            (asked_row, 1),
-            (degree_row, 1),
+            (arrived, 1),
+            (asked_column, 1),
             (tiles, groups(tiles)),
             (partial, groups(tiles)),
             (own, n),
             (degree, n),
         ),
-        ((struct(masters, width, dtype=F32), n, 0), (struct(masters, EDGE, dtype=F32), 1, 0)),
+        (
+            (struct(masters, width, dtype=F32), n, 0),
+            (struct(masters, EDGE, dtype=F32), 1, 0),
+            (struct(8, asked_column.shape[0], dtype=I32), 1, 0),
+        ),
         flops=5e9,
     )
 
@@ -405,15 +413,18 @@
 def turn_kernel(scalars, ins, outs):
     asked_row, back, base, scale, cotangent, asked_column = ins
     mixed, low, spread, send = outs
-    for p in range(base.pieces):
-        for source in (base, scale, cotangent):
-            source.start(p)
+    for source in (base, scale, cotangent):
+        source.start(0)
     asked, back = asked_row.all()[0:1], back.all()
     step = 512
     for g in range(base.held.shape[0] // step):
         if g * step % base.size == 0:
+            p = g * step // base.size
             for source in (base, scale, cotangent):
-                source.wait(g * step // base.size)
+                source.wait(p)
+            for source in (base, scale, cotangent, asked_column):
+                if p + 1 < source.pieces:
+                    source.start(p + 1)
         at = slice(g * step, (g + 1) * step)
         both = jnp.concatenate([scale.held[at, :], scale.held[at, :]], axis=1)
         added = dot(pick_rows(step, g * step, asked), back[...])
@@ -426,6 +437,7 @@
         d_pre = cotangent.held[at, :].astype(F32) * slope
         low.held[at, :] = d_pre.astype(BF16)
         spread.held[at, :] = (d_pre * both).astype(BF16)
+    asked_column.start(0)
     for out in (spread, low, mixed):
         out.start()
     gather(spread.held, asked_column.all(), send.held)
@@ -442,7 +454,7 @@
             (base, 2),
             (scale, 2),
             (cotangent, 2),
-            (asked_column, 1),
+            (asked_column, 2),
         ),
         ((struct(masters, width), 1, 0),) * 3 + ((struct(*back.shape), 1, 0),),
         flops=3e9,
@@ -459,13 +471,12 @@
     tiles, values = ins
     (total,) = outs
     rows = dense.shape[0]
-    for g in range(rows // GROUP):
-        tiles.start(g)
+    begin((tiles,), rows // GROUP)
     for b in range(rows):
         dense[b] = jnp.zeros(dense.shape[1:], BF16)
     turned = jnp.transpose(values.all()[...].astype(F32)).astype(BF16)
     for g in range(rows // GROUP):
-        tiles.wait(g)
+        take((tiles,), rows // GROUP, g)
         densify(count, column, tiles.held, dense, g)
     for g in range(total.pieces):
         right = flat(dense, range(rows), range(g * GROUP, (g + 1) * GROUP))
@@ -525,28 +536,37 @@
     )
 
 
-def back_far_kernel(scalars, ins, outs):
+def back_far_kernel(scalars, ins, outs, dense):
+    count, column = scalars
     tiles, turned, partial = ins
     (total,) = outs
+    last = tiles.pieces - 1
+    tiles.start(last)
     for g in range(total.pieces):
         partial.start(g)
-    tiles, turned = tiles.all(), turned.all()
+    dense[...] = jnp.zeros(dense.shape, BF16)
+    turned = turned.all()
+    tiles.wait(last)
+    densify(count, column, tiles.held, dense, last, last * GROUP)
     for g in range(total.pieces):
         columns = range(g * GROUP, (g + 1) * GROUP)
-        right = flat(tiles, range(tiles.shape[0]), columns)
+        right = flat(dense, range(GROUP), columns)
         partial.wait(g)
         own = jnp.concatenate([partial.held[c] for c in columns], axis=1)
         put_blocks(total.held, g * GROUP, own + dot(turned[...], right))
         total.start(g)
 
 
-def back_far(tiles, turned, partial):
-    width, masters = turned.shape[0], tiles.shape[1]
+def back_far(tile_count, tile_column, tiles, turned, partial):
+    width, mirrors = turned.shape
+    row_blocks = tiles.shape[0]
+    masters = row_blocks - mirrors // EDGE
     (total,) = run(
         back_far_kernel,
-        (),
-        ((tiles, 1), (turned, 1), (partial, groups(partial))),
+        (tile_count, tile_column),
+        ((tiles, groups(tiles)), (turned, 1), (partial, groups(partial))),
         ((struct(masters, width, EDGE, dtype=F32), masters // GROUP, 0),),
+        (pltpu.VMEM((mirrors // EDGE, row_blocks + 1, EDGE, EDGE), BF16),),
         flops=3e9,
     )
     return total
@@ -637,7 +657,7 @@
     return pl.pallas_call(
         share_kernel,
         out_shape=struct(*parts.shape),
-        compiler_params=params(),
+        compiler_params=params(8 * MIB),
         cost_estimate=cost(1e8),
     )(parts)
 
@@ -658,7 +678,7 @@
         in_specs=[smem, vmem, vmem],
         out_specs=[vmem, vmem],
         out_shape=[struct(inputs, width, dtype=F32)] * 2,
-        compiler_params=params(),
+        compiler_params=params(8 * MIB),
         cost_estimate=cost(1e8),
     )(core, mine, other)
 
@@ -695,18 +715,20 @@
     core = lax.axis_index("core").astype(I32).reshape(1)
     slots = SLOTS * parts
     peer = mirror_master_part[:, 0]
+    tile_column = tile_column.T
     ask, slot_row, slot_column = place(tile_count, peer, mirror_row, tile_weight, parts)
     asked = exchange(ask)
     projected = jnp.dot(features, w_neigh, preferred_element_type=F32).astype(BF16)
     own = jnp.dot(features, w_self, preferred_element_type=F32)
+    asked, own = lax.optimization_barrier((asked, own))
+    asked = pltpu.with_memory_space_constraint(asked, pltpu.HBM)
     rows, asked_column = fetch(asked, projected, slots)
+    rows, projected = lax.optimization_barrier((rows, projected))
     arrived = exchange(rows)
-    partial, degree, asked_row, degree_row, near_tiles, far_tiles = near(
-        tile_count, tile_column, tile_weight, projected, asked, asked_column
-    )
+    partial, degree, far_tiles = near(tile_count, tile_column, tile_weight, projected)
     send, slab = mirror_out(arrived, slot_column, slot_row, partial, far_tiles)
     back = exchange(send)
-    base, scale = far(far_tiles, slab, partial, degree, own, asked_row, degree_row)
+    base, scale, asked_row = far(far_tiles, slab, partial, degree, own, asked, asked_column)
     mixed, low, spread, send = turn(base, scale, cotangent, back, asked_row, asked_column)
     arrived = exchange(send)
     partial = back_near(tile_count, tile_column, tile_weight, spread)
@@ -715,7 +737,7 @@
     ).astype(BF16)
     send, turned = mirror_back(arrived, slot_column, slot_row, partial, far_tiles)
     back = exchange(send)
-    partial = back_far(near_tiles, turned, partial)
+    partial = back_far(tile_count, tile_column, tile_weight, turned, partial)
     d_projected, keep, give = finish(core, partial, back, asked_column, features, grad_self)
     pair = (keep + to_other_core(give).astype(F32)).astype(BF16)
     same = ("chip", "local")

time: 179 us -> 171 us (0.955)
  Pallas kernels: 70.5 us -> 65.8 us
  waiting for transfers between devices: 31.8 us -> 35.1 us
  starting transfers between devices: 46.6 us -> 43.8 us
  local copies, waits for them, and re-layouts: 2.81 us -> 0.02 us
    all_to_all x6, waiting for transfers between devices: 28.8 us -> 32.1 us  [exchange(): lax.all_to_all(buffer.reshape(parts, buffer.shape[0] // parts, buffer.sha...]
    all_to_all x6, starting transfers between devices: 43.4 us -> 40.2 us  [exchange(): lax.all_to_all(buffer.reshape(parts, buffer.shape[0] // parts, buffer.sha...]
    unnamed x15 -> x6, local copies, waits for them, and re-layouts: 2.81 us -> 0.02 us
    pallas_call x11, Pallas kernels: 66.3 us -> 64.4 us  [run(): pl.pallas_call(body, in_specs=[smem] * len(scalars) + [any_space] * n, ou...]
  transfers between devices with their start and end apart: 8 -> 8, of which waited for: 7 -> 8; matrix products, arithmetic and copies ran while one was open for 5% -> 4% of each run, Pallas kernels for 21% -> 21%
where the time goes in v4:
time: 171 us; the launch traced here: 170 us
  Pallas kernels  65.8 us (38%)
  starting transfers between devices  43.8 us (26%)
  waiting for transfers between devices  35.1 us (21%)
  blocking collectives  14.6 us (9%)
  matrix products  7.64 us (4%)
  other arithmetic  1.96 us (1%)
    pallas_call x11, Pallas kernels, run(): pl.pallas_call(body, in_specs=[smem] * len(scalars) + [any_space] * n, ou...  64.4 us
    all_to_all x6, starting transfers between devices, exchange(): lax.all_to_all(buffer.reshape(parts, buffer.shape[0] // parts, buffer.sha...  40.2 us
    all_to_all x6, waiting for transfers between devices, exchange(): lax.all_to_all(buffer.reshape(parts, buffer.shape[0] // parts, buffer.sha...  32.1 us
    all_to_all x1, blocking collectives, exchange(): lax.all_to_all(buffer.reshape(parts, buffer.shape[0] // parts, buffer.sha...  14.6 us
    ppermute x2, starting transfers between devices, to_other_core(): return lax.ppermute(value, 'core', [(0, 1), (1, 0)])  3.53 us
  transfers between devices with their start and end apart: 8, of which 8 were waited for; matrix products, arithmetic and copies ran while one was open for 4% of the time, Pallas kernels for 21%

profile of v4, /device:TPU:1, one launch (start us, length us, event | category | flops | bytes accessed | tf_op | source)
XLA Modules:
  0.0 169.7 jit_solution(9797003074321763771)
XLA Ops:
  0.7 4.3 %shard_map.120 = (f32[128,128]{1,0:T(8,128)}, s32[1,512]{1,0:T(1,128)}, s32[512,128]{1,0:T(8,128)}) custom-call(s32[20]{0:T(128)} %refs_0_.7, s32[1,512]{1,0:T(1,128)} %bitcast.36, s32[1,512]{1,0:T(1,128)} %bitcast.37, bf16[20,16,128,128]{3,2,1,0:T(8,128)(2,1)} %refs_2_.6), custom_call_target="tpu_custom_call" | custom-call | flops 1000000000 | bytes 4194304 | tf_op jit(solution)/shard_map/pallas_call | solution.py:117
  5.0 12.0 %all-to-all-start = ((f32[128,1,128]{2,1,0:T(1,128)}), f32[128,1,128]{2,1,0:T(1,128)}, u32[]{:S(2)}, u32[]{:S(2)}) async-start(f32[128,1,128]{2,1,0:T(1,128)} %bitcast.32), calls=%async_computation | async-start | bytes 131072 | tf_op jit(solution)/shard_map/all_to_all | solution.py:688
  17.0 2.4 %fusion.1.refs_5_ = f32[2048,256]{1,0:T(8,128)} fusion(bf16[2048,768]{1,0:T(8,128)(2,1)S(1)} %copy-done, bf16[768,256]{1,0:T(8,128)(2,1)S(1)} %copy-done.1), kind=kOutput, calls=%fused_computation.4 | convolution fusion | flops 805306368 | bytes 5636096 | tf_op jit(solution)/shard_map/dot_general | solution.py:722
  19.3 2.0 %convolution_convert_fusion.refs_1_.refs_3_ = bf16[2048,256]{1,0:T(8,128)(2,1)} fusion(bf16[2048,768]{1,0:T(8,128)(2,1)S(1)} %copy-done, bf16[768,256]{1,0:T(8,128)(2,1)S(1)} %copy-done.2), kind=kOutput, calls=%fused_computation | convolution fusion | flops 805830656 | bytes 4587520 | tf_op jit(solution)/shard_map/dot_general | solution.py:721
  21.3 5.4 %all-to-all-done = f32[128,1,128]{2,1,0:T(1,128)} async-done(((f32[128,1,128]{2,1,0:T(1,128)}), f32[128,1,128]{2,1,0:T(1,128)}, u32[]{:S(2)}, u32[]{:S(2)}) %all-to-all-start) | async-done | bytes 65568 | tf_op jit(solution)/shard_map/all_to_all | solution.py:688
  26.7 3.3 %shard_map.121 = (bf16[1024,256]{1,0:T(8,128)(2,1)}, s32[1024,128]{1,0:T(8,128)}) custom-call(f32[128,128]{1,0:T(8,128)} %bitcast.4.refs_0_.refs_1_, bf16[2048,256]{1,0:T(8,128)(2,1)} %convolution_convert_fusion.refs_1_.refs_3_), custom_call_target="tpu_custom_call" | custom-call | flops 2000000000 | bytes 4194304 | tf_op jit(solution)/shard_map/pallas_call | solution.py:117
  30.1 4.8 %all-to-all-start.1 = ((bf16[128,8,256]{2,1,0:T(8,128)(2,1)}), bf16[128,8,256]{2,1,0:T(8,128)(2,1)}, u32[]{:S(2)}, u32[]{:S(2)}) async-start(bf16[128,8,256]{2,1,0:T(8,128)(2,1)} %bitcast.31), calls=%async_computation.1 | async-start | bytes 1048576 | tf_op jit(solution)/shard_map/all_to_all | solution.py:688
  34.9 9.4 %shard_map.122 = (f32[2560,256]{1,0:T(8,128)}, f32[2048,128]{1,0:T(8,128)}, bf16[20,4,128,128]{3,2,1,0:T(8,128)(2,1)}) custom-call(s32[20]{0:T(128)} %refs_0_.7, s32[16,20]{1,0:T(8,128)} %bitcast.33, bf16[20,16,128,128]{3,2,1,0:T(8,128)(2,1)} %refs_2_.6, bf16[2048,256]{1,0:T(8,128)(2,1)} %convolution_convert_fusion.refs_1_.refs_3_), custom_call_target="tpu_custom_call" | custom-call | flops 5000000000 | bytes 4194304 | tf_op jit(solution)/shard_map/pallas_call | solution.py:117
  44.3 4.5 %all-to-all-done.1 = bf16[128,8,256]{2,1,0:T(8,128)(2,1)} async-done(((bf16[128,8,256]{2,1,0:T(8,128)(2,1)}), bf16[128,8,256]{2,1,0:T(8,128)(2,1)}, u32[]{:S(2)}, u32[]{:S(2)}) %all-to-all-start.1) | async-done | bytes 524320 | tf_op jit(solution)/shard_map/all_to_all | solution.py:688
  48.8 4.0 %shard_map.123 = (bf16[1024,256]{1,0:T(8,128)(2,1)}, bf16[512,256]{1,0:T(8,128)(2,1)}) custom-call(bf16[1024,256]{1,0:T(8,128)(2,1)} %bitcast.6.refs_0_, s32[512,128]{1,0:T(8,128)} %get-tuple-element.38.refs_1_, f32[2560,256]{1,0:T(8,128)} %get-tuple-element.40.refs_2_.refs_4_, bf16[20,4,128,128]{3,2,1,0:T(8,128)(2,1)} %get-tuple-element.41.refs_3_.refs_2_, ...), custom_call_target="tpu_custom_call" | custom-call | flops 2000000000 | bytes 4194304 | tf_op jit(solution)/shard_map/pallas_call | solution.py:117
  52.8 6.5 %all-to-all-start.2 = ((bf16[128,8,256]{2,1,0:T(8,128)(2,1)}), bf16[128,8,256]{2,1,0:T(8,128)(2,1)}, u32[]{:S(2)}, u32[]{:S(2)}) async-start(bf16[128,8,256]{2,1,0:T(8,128)(2,1)} %bitcast.29), calls=%async_computation.2 | async-start | bytes 1048576 | tf_op jit(solution)/shard_map/all_to_all | solution.py:688
  59.3 6.9 %shard_map.124 = (f32[2048,256]{1,0:T(8,128)}, f32[2048,128]{1,0:T(8,128)}, s32[8,1024]{1,0:T(8,128)}) custom-call(bf16[512,256]{1,0:T(8,128)(2,1)} %get-tuple-element.43.refs_0_, f32[128,128]{1,0:T(8,128)} %bitcast.4.refs_0_.refs_1_, s32[1024,128]{1,0:T(8,128)} %get-tuple-element.44.refs_2_.refs_5_, ...), custom_call_target="tpu_custom_call" | custom-call | flops 5000000000 | bytes 4194304 | tf_op jit(solution)/shard_map/pallas_call | solution.py:117
  66.3 6.8 %all-to-all-done.2 = bf16[128,8,256]{2,1,0:T(8,128)(2,1)} async-done(((bf16[128,8,256]{2,1,0:T(8,128)(2,1)}), bf16[128,8,256]{2,1,0:T(8,128)(2,1)}, u32[]{:S(2)}, u32[]{:S(2)}) %all-to-all-start.2) | async-done | bytes 524320 | tf_op jit(solution)/shard_map/all_to_all | solution.py:688
  73.1 6.7 %shard_map.125 = (bf16[2048,256]{1,0:T(8,128)(2,1)}, bf16[2048,256]{1,0:T(8,128)(2,1)}, bf16[2048,256]{1,0:T(8,128)(2,1)}, bf16[1024,256]{1,0:T(8,128)(2,1)}) custom-call(s32[8,1024]{1,0:T(8,128)} %get-tuple-element.47.refs_0_, bf16[1024,256]{1,0:T(8,128)(2,1)} %bitcast.9.refs_1_, f32[2048,256]{1,0:T(8,128)} %get-tuple-element.49.refs_2_, ...), custom_call_target="tpu_custom_call" | custom-call | flops 3000000000 | bytes 4194304 | tf_op jit(solution)/shard_map/pallas_call | solution.py:117
  79.8 4.7 %all-to-all-start.3 = ((bf16[128,8,256]{2,1,0:T(8,128)(2,1)}), bf16[128,8,256]{2,1,0:T(8,128)(2,1)}, u32[]{:S(2)}, u32[]{:S(2)}) async-start(bf16[128,8,256]{2,1,0:T(8,128)(2,1)} %bitcast.28), calls=%async_computation.3 | async-start | bytes 1048576 | tf_op jit(solution)/shard_map/all_to_all | solution.py:688
  84.6 9.4 %shard_map.126.refs_3_.refs_4_ = f32[20,256,128]{2,1,0:T(8,128)} custom-call(s32[20]{0:T(128)} %refs_0_.7, s32[16,20]{1,0:T(8,128)} %bitcast.34, bf16[20,16,128,128]{3,2,1,0:T(8,128)(2,1)} %refs_2_.6, bf16[2048,256]{1,0:T(8,128)(2,1)} %get-tuple-element.53.refs_3_), custom_call_target="tpu_custom_call" | custom-call | flops 5000000000 | bytes 4194304 | tf_op jit(solution)/shard_map/pallas_call | solution.py:117
  94.0 4.5 %all-to-all-done.3 = bf16[128,8,256]{2,1,0:T(8,128)(2,1)} async-done(((bf16[128,8,256]{2,1,0:T(8,128)(2,1)}), bf16[128,8,256]{2,1,0:T(8,128)(2,1)}, u32[]{:S(2)}, u32[]{:S(2)}) %all-to-all-start.3) | async-done | bytes 524320 | tf_op jit(solution)/shard_map/all_to_all | solution.py:688
  98.5 4.2 %shard_map.127 = (bf16[1024,256]{1,0:T(8,128)(2,1)}, bf16[256,512]{1,0:T(8,128)(2,1)}) custom-call(bf16[1024,256]{1,0:T(8,128)(2,1)} %bitcast.12.refs_0_, s32[512,128]{1,0:T(8,128)} %get-tuple-element.38.refs_1_, bf16[20,4,128,128]{3,2,1,0:T(8,128)(2,1)} %get-tuple-element.41.refs_3_.refs_2_, f32[20,256,128]{2,1,0:T(8,128)} %shard_map.126.refs_3_.refs_4_, ...), custom_call_target="tpu_custom_call" | custom-call | flops 2000000000 | bytes 4194304 | tf_op jit(solution)/shard_map/pallas_call | solution.py:117
  102.7 6.2 %all-to-all-start.4 = ((bf16[128,8,256]{2,1,0:T(8,128)(2,1)}), bf16[128,8,256]{2,1,0:T(8,128)(2,1)}, u32[]{:S(2)}, u32[]{:S(2)}) async-start(bf16[128,8,256]{2,1,0:T(8,128)(2,1)} %bitcast.30), calls=%async_computation.4 | async-start | bytes 1048576 | tf_op jit(solution)/shard_map/all_to_all | solution.py:688
  108.9 3.3 %fusion.refs_5_ = bf16[768,256]{1,0:T(8,128)(2,1)} fusion(bf16[2048,256]{1,0:T(8,128)(2,1)} %get-tuple-element.56.refs_0_, bf16[2048,768]{1,0:T(8,128)(2,1)S(1)} %copy-done), kind=kOutput, calls=%fused_computation.2 | convolution fusion | flops 805502976 | bytes 4587520 | tf_op jit(solution)/shard_map/dot_general | solution.py:735
  112.2 5.3 %shard_map.128.refs_3_ = f32[16,256,128]{2,1,0:T(8,128)} custom-call(s32[20]{0:T(128)} %refs_0_.7, s32[16,20]{1,0:T(8,128)} %bitcast.35, bf16[20,16,128,128]{3,2,1,0:T(8,128)(2,1)} %refs_2_.6, bf16[256,512]{1,0:T(8,128)(2,1)} %get-tuple-element.55.refs_3_, f32[20,256,128]{2,1,0:T(8,128)} %shard_map.126.refs_3_.refs_4_), custom_call_target="tpu_custom_call" | custom-call | flops 3000000000 | bytes 4194304 | tf_op jit(solution)/shard_map/pallas_call | solution.py:117
  117.5 5.2 %all-to-all-done.4 = bf16[128,8,256]{2,1,0:T(8,128)(2,1)} async-done(((bf16[128,8,256]{2,1,0:T(8,128)(2,1)}), bf16[128,8,256]{2,1,0:T(8,128)(2,1)}, u32[]{:S(2)}, u32[]{:S(2)}) %all-to-all-start.4) | async-done | bytes 524320 | tf_op jit(solution)/shard_map/all_to_all | solution.py:688
  122.6 6.0 %shard_map.129 = (bf16[256,2048]{1,0:T(8,128)(2,1)}, f32[1536,128]{1,0:T(8,128)}, bf16[1536,128]{1,0:T(8,128)(2,1)}) custom-call(s32[1]{0:T(128)} %bitcast.10.refs_0_.core, bf16[1024,256]{1,0:T(8,128)(2,1)} %bitcast.14.refs_1_, s32[1024,128]{1,0:T(8,128)} %get-tuple-element.44.refs_2_.refs_5_, f32[16,256,128]{2,1,0:T(8,128)} %shard_map.128.refs_3_, ...), custom_call_target="tpu_custom_call" | custom-call | flops 3000000000 | bytes 4194304 | tf_op jit(solution)/shard_map/pallas_call | solution.py:117
  129.0 1.7 collective-permute-done
  130.7 2.0 %add_convert_fusion = bf16[1536,128]{1,0:T(8,128)(2,1)} fusion(f32[1536,128]{1,0:T(8,128)} %get-tuple-element.57, bf16[1536,128]{1,0:T(8,128)(2,1)S(1)} %collective-permute-done), kind=kLoop, calls=%fused_computation.3 | loop fusion | flops 589824 | bytes 1572864 | tf_op jit(solution)/shard_map/convert_element_type | solution.py:742
  132.6 6.1 %all-to-all-start.5 = ((bf16[64,24,128]{2,1,0:T(8,128)(2,1)}), bf16[64,24,128]{2,1,0:T(8,128)(2,1)S(1)}, u32[]{:S(2)}, u32[]{:S(2)}) async-start(bf16[64,24,128]{2,1,0:T(8,128)(2,1)} %bitcast.16), calls=%async_computation.5 | async-start | bytes 786432 | tf_op jit(solution)/shard_map/all_to_all | solution.py:688
  138.7 4.8 %shard_map.130 = bf16[2048,768]{1,0:T(8,128)(2,1)} custom-call(bf16[2048,256]{1,0:T(8,128)(2,1)} %get-tuple-element.56.refs_0_, bf16[256,2048]{1,0:T(8,128)(2,1)} %get-tuple-element.59.refs_1_, bf16[768,256]{1,0:T(8,128)(2,1)} %refs_2_.7, bf16[768,256]{1,0:T(8,128)(2,1)} %refs_3_.3), custom_call_target="tpu_custom_call" | custom-call | flops 3000000000 | bytes 4194304 | tf_op jit(solution)/shard_map/pallas_call | solution.py:117
  143.5 5.7 %all-to-all-done.5.parts = bf16[64,24,128]{2,1,0:T(8,128)(2,1)S(1)} async-done(((bf16[64,24,128]{2,1,0:T(8,128)(2,1)}), bf16[64,24,128]{2,1,0:T(8,128)(2,1)S(1)}, u32[]{:S(2)}, u32[]{:S(2)}) %all-to-all-start.5) | async-done | bytes 393248 | tf_op jit(solution)/shard_map/all_to_all | solution.py:688
  149.3 14.6 %all_to_all.35 = bf16[64,24,128]{2,1,0:T(8,128)(2,1)S(1)} all-to-all(bf16[64,24,128]{2,1,0:T(8,128)(2,1)S(1)} %shard_map.131), channel_id=1, replica_groups=mesh['chip'=16,'core'=2,'local'=4] {'chip','local'}, dimensions={0} | all-to-all | bytes 786432 | tf_op jit(solution)/shard_map/all_to_all | solution.py:688
  163.9 3.2 %collective-permute-start.1 = (bf16[1536,128]{1,0:T(8,128)(2,1)S(1)}, bf16[1536,128]{1,0:T(8,128)(2,1)S(1)}, u32[]{:S(2)}, u32[]{:S(2)}) collective-permute-start(bf16[1536,128]{1,0:T(8,128)(2,1)S(1)} %bitcast.26), channel_id=1, source_target_pairs={{0,4},{4,0},{1,5},{5,1},{2,6},{6,2},{3,7},{7,3},{8,12},{12,8},{9,1... | collective-permute-start | bytes 1179656 | tf_op jit(solution)/shard_map/ppermute | solution.py:699
  167.1 1.3 collective-permute-done.1.other
  168.4 1.3 shard_map.132
  (8 shorter events, 0.4 us)
Async XLA Ops:
  0.6 16.3 %copy-start = (bf16[2048,768]{1,0:T(8,128)(2,1)S(1)}, bf16[2048,768]{1,0:T(8,128)(2,1)}, u32[]{:S(2)}) copy-start(bf16[2048,768]{1,0:T(8,128)(2,1)} %refs_4_.3) | copy-start | bytes 9437188
  0.6 16.3 %copy-start.1 = (bf16[768,256]{1,0:T(8,128)(2,1)S(1)}, bf16[768,256]{1,0:T(8,128)(2,1)}, u32[]{:S(2)}) copy-start(bf16[768,256]{1,0:T(8,128)(2,1)} %refs_2_.7) | copy-start | bytes 1179652
  5.0 21.7 %all-to-all-start = ((f32[128,1,128]{2,1,0:T(1,128)}), f32[128,1,128]{2,1,0:T(1,128)}, u32[]{:S(2)}, u32[]{:S(2)}) async-start(f32[128,1,128]{2,1,0:T(1,128)} %bitcast.32), calls=%async_computation | async-start | bytes 131072 | tf_op jit(solution)/shard_map/all_to_all | solution.py:688
  17.0 2.4 %copy-start.2 = (bf16[768,256]{1,0:T(8,128)(2,1)S(1)}, bf16[768,256]{1,0:T(8,128)(2,1)}, u32[]{:S(2)}) copy-start(bf16[768,256]{1,0:T(8,128)(2,1)} %refs_3_.3) | copy-start | bytes 1179652
  30.1 18.8 %all-to-all-start.1 = ((bf16[128,8,256]{2,1,0:T(8,128)(2,1)}), bf16[128,8,256]{2,1,0:T(8,128)(2,1)}, u32[]{:S(2)}, u32[]{:S(2)}) async-start(bf16[128,8,256]{2,1,0:T(8,128)(2,1)} %bitcast.31), calls=%async_computation.1 | async-start | bytes 1048576 | tf_op jit(solution)/shard_map/all_to_all | solution.py:688
  52.8 20.3 %all-to-all-start.2 = ((bf16[128,8,256]{2,1,0:T(8,128)(2,1)}), bf16[128,8,256]{2,1,0:T(8,128)(2,1)}, u32[]{:S(2)}, u32[]{:S(2)}) async-start(bf16[128,8,256]{2,1,0:T(8,128)(2,1)} %bitcast.29), calls=%async_computation.2 | async-start | bytes 1048576 | tf_op jit(solution)/shard_map/all_to_all | solution.py:688
  79.8 18.7 %all-to-all-start.3 = ((bf16[128,8,256]{2,1,0:T(8,128)(2,1)}), bf16[128,8,256]{2,1,0:T(8,128)(2,1)}, u32[]{:S(2)}, u32[]{:S(2)}) async-start(bf16[128,8,256]{2,1,0:T(8,128)(2,1)} %bitcast.28), calls=%async_computation.3 | async-start | bytes 1048576 | tf_op jit(solution)/shard_map/all_to_all | solution.py:688
  102.7 20.0 %all-to-all-start.4 = ((bf16[128,8,256]{2,1,0:T(8,128)(2,1)}), bf16[128,8,256]{2,1,0:T(8,128)(2,1)}, u32[]{:S(2)}, u32[]{:S(2)}) async-start(bf16[128,8,256]{2,1,0:T(8,128)(2,1)} %bitcast.30), calls=%async_computation.4 | async-start | bytes 1048576 | tf_op jit(solution)/shard_map/all_to_all | solution.py:688
  128.7 2.0 %collective-permute-start = (bf16[1536,128]{1,0:T(8,128)(2,1)}, bf16[1536,128]{1,0:T(8,128)(2,1)S(1)}, u32[]{:S(2)}, u32[]{:S(2)}) collective-permute-start(bf16[1536,128]{1,0:T(8,128)(2,1)} %get-tuple-element.58), channel_id=1, source_target_pairs={{0,4},{4,0},{1,5},{5,1},{2,6},{6,2},{3,7},{7,3},{8,12},{12,8},{9,1... | collective-permute-start | bytes 1179656 | tf_op jit(solution)/shard_map/ppermute | solution.py:699
  132.6 16.6 %all-to-all-start.5 = ((bf16[64,24,128]{2,1,0:T(8,128)(2,1)}), bf16[64,24,128]{2,1,0:T(8,128)(2,1)S(1)}, u32[]{:S(2)}, u32[]{:S(2)}) async-start(bf16[64,24,128]{2,1,0:T(8,128)(2,1)} %bitcast.16), calls=%async_computation.5 | async-start | bytes 786432 | tf_op jit(solution)/shard_map/all_to_all | solution.py:688
  163.9 4.5 %collective-permute-start.1 = (bf16[1536,128]{1,0:T(8,128)(2,1)S(1)}, bf16[1536,128]{1,0:T(8,128)(2,1)S(1)}, u32[]{:S(2)}, u32[]{:S(2)}) collective-permute-start(bf16[1536,128]{1,0:T(8,128)(2,1)S(1)} %bitcast.26), channel_id=1, source_target_pairs={{0,4},{4,0},{1,5},{5,1},{2,6},{6,2},{3,7},{7,3},{8,12},{12,8},{9,1... | collective-permute-start | bytes 1179656 | tf_op jit(solution)/shard_map/ppermute | solution.py:699

commit v5 on v4

--- a/solution.py
+++ b/solution.py
@@ -72,6 +72,23 @@
         return self.held
 
 
+class Here(Moved):
+    def __init__(self, held, pieces):
+        self.held, self.pieces = held, pieces
+        self.size = held.shape[0] // pieces
+        self.waited = True
+
+    def start(self, p=0):
+        pass
+
+    def wait(self, p=0):
+        pass
+
+
+def inner(array):
+    return ("inner", array)
+
+
 def begin(sources, pieces):
     for g in range(min(AHEAD, pieces)):
         for source in sources:
@@ -87,17 +104,22 @@
 
 
 def run(kernel, scalars, ins, outs, scratch=(), flops=1e9):
-    ins, outs = list(ins), list(outs)
-    n, m = len(ins), len(outs)
-    own = [k for k in range(n + m) if (ins + outs)[k][1]]
+    entries = [(x, pieces, 0) for x, pieces in ins] + list(outs)
+    n = len(ins)
+    kept = [isinstance(entry[0], tuple) for entry in entries]
+    arrays = [entry[0][1] if k else entry[0] for entry, k in zip(entries, kept)]
+    own = [k for k, entry in enumerate(entries) if entry[1] and not kept[k]]
 
     def body(*refs):
         scalar_refs, refs = refs[: len(scalars)], refs[len(scalars) :]
-        far, refs = list(refs[: n + m]), refs[n + m :]
+        far, refs = list(refs[: len(entries)]), refs[len(entries) :]
         held, sems, rest = refs[: len(own)], refs[len(own) : 2 * len(own)], refs[2 * len(own) :]
+        for k, entry in enumerate(entries):
+            if kept[k]:
+                far[k] = Here(far[k], entry[1])
         for at, k in enumerate(own):
-            far[k] = Moved(far[k], held[at], sems[at], (ins + outs)[k][1], k < n)
-            if k < n and ins[k][1] == 1:
+            far[k] = Moved(far[k], held[at], sems[at], entries[k][1], k < n)
+            if k < n and entries[k][1] == 1:
                 far[k].start()
         kernel(scalar_refs, far[:n], far[n:], *rest)
         results = [far[k] for k in own if k >= n]
@@ -109,22 +131,28 @@
             out.all()
 
     def place_of(k):
-        shape = ins[k][0] if k < n else outs[k - n][0]
-        spare = 0 if k < n else outs[k - n][2]
-        return pltpu.VMEM((shape.shape[0] + spare, *shape.shape[1:]), shape.dtype)
-
-    smem, any_space = pl.BlockSpec(memory_space=pltpu.SMEM), pl.BlockSpec(memory_space=pl.ANY)
+        shape = arrays[k].shape
+        return pltpu.VMEM((shape[0] + entries[k][2], *shape[1:]), arrays[k].dtype)
+
+    smem, vmem = pl.BlockSpec(memory_space=pltpu.SMEM), pl.BlockSpec(memory_space=pltpu.VMEM)
+    specs = [vmem if k else pl.BlockSpec(memory_space=pl.ANY) for k in kept]
+    given = [
+        pltpu.with_memory_space_constraint(x, pltpu.VMEM) if k else x
+        for x, k in zip(arrays[:n], kept)
+    ]
     return pl.pallas_call(
         body,
-        in_specs=[smem] * len(scalars) + [any_space] * n,
-        out_specs=[any_space] * m,
-        out_shape=[out[0] for out in outs],
+        in_specs=[smem] * len(scalars) + specs[:n],
+        out_specs=specs[n:],
+        out_shape=[
+            pltpu.VMEM(x.shape, x.dtype) if k else x for x, k in zip(arrays[n:], kept[n:])
+        ],
         scratch_shapes=[place_of(k) for k in own]
-        + [pltpu.SemaphoreType.DMA(((ins + outs)[k][1],)) for k in own]
+        + [pltpu.SemaphoreType.DMA((entries[k][1],)) for k in own]
         + list(scratch),
         compiler_params=params(),
         cost_estimate=cost(flops),
-    )(*scalars, *[x for x, _ in ins])
+    )(*scalars, *given)
 
 
 def params(limit=VMEM_BYTES):
@@ -213,10 +241,18 @@
 
 
 def gather(values, asked_column, rows):
-    step = 512
-    for g in range(rows.shape[0] // step):
-        at = slice(g * step, (g + 1) * step)
-        rows[at, :] = dot(pick_columns(asked_column[at, :], 0, values.shape[0]), values[...]).astype(BF16)
+    for g in range(rows.pieces):
+        at = rows.rows(g)
+        pick = pick_columns(asked_column[at, :], 0, values.shape[0])
+        rows.held[at, :] = dot(pick, values[...]).astype(BF16)
+        rows.start(g)
+
+
+def to_slots(slot_row, values, send):
+    for g in range(send.pieces):
+        pick = pick_rows(send.size, g * send.size, slot_row)
+        send.held[send.rows(g), :] = dot(pick, values).astype(BF16)
+        send.start(g)
 
 
 def fetch_kernel(scalars, ins, outs):
@@ -229,7 +265,7 @@
     asked = jnp.sum(asked, axis=1, keepdims=True) - 1.0
     asked_column.held[...] = jnp.broadcast_to(asked, (slots, EDGE)).astype(I32)
     asked_column.start()
-    gather(values.all(), asked_column.held, rows.held)
+    gather(values.all(), asked_column.held, rows)
 
 
 def fetch(arrived, values, slots):
@@ -237,7 +273,7 @@
         fetch_kernel,
         (),
         ((arrived, 1), (values, 1)),
-        ((struct(slots, values.shape[1]), 1, 0), (struct(slots, EDGE, dtype=I32), 1, 0)),
+        ((struct(slots, values.shape[1]), 2, 0), (struct(slots, EDGE, dtype=I32), 1, 0)),
         flops=2e9,
     )
 
@@ -335,8 +371,7 @@
     more = dot(left, slab.held[...])
     partial.wait(last)
     total = (partial.held[partial.rows(last), :] + more).astype(BF16)
-    slots = send.held.shape[0]
-    send.held[...] = dot(pick_rows(slots, 0, slot_row.all()[...]), total).astype(BF16)
+    to_slots(slot_row.all()[...], total, send)
 
 
 def mirror_out(arrived, slot_column, slot_row, partial, tiles):
@@ -346,13 +381,13 @@
         mirror_out_kernel,
         (),
         (
-            (arrived, 1),
+            (inner(arrived), 1),
             (slot_column, 1),
             (partial, groups(tiles)),
             (tiles, groups(tiles)),
             (slot_row, 1),
         ),
-        ((struct(slots, width), 1, 0), (struct(mirrors, width), 1, 0)),
+        ((struct(slots, width), 2, 0), (struct(mirrors, width), 1, 0)),
         flops=2e9,
     )
 
@@ -402,7 +437,7 @@
             (degree, n),
         ),
         (
-            (struct(masters, width, dtype=F32), n, 0),
+            (inner(struct(masters, width, dtype=F32)), n, 0),
             (struct(masters, EDGE, dtype=F32), 1, 0),
             (struct(8, asked_column.shape[0], dtype=I32), 1, 0),
         ),
@@ -440,7 +475,7 @@
     asked_column.start(0)
     for out in (spread, low, mixed):
         out.start()
-    gather(spread.held, asked_column.all(), send.held)
+    gather(spread.held, asked_column.all(), send)
 
 
 def turn(base, scale, cotangent, back, asked_row, asked_column):
@@ -450,13 +485,13 @@
         (),
         (
             (asked_row, 1),
-            (back, 1),
-            (base, 2),
+            (inner(back), 1),
+            (inner(base), 2),
             (scale, 2),
             (cotangent, 2),
             (asked_column, 2),
         ),
-        ((struct(masters, width), 1, 0),) * 3 + ((struct(*back.shape), 1, 0),),
+        ((struct(masters, width), 1, 0),) * 3 + ((struct(*back.shape), 2, 0),),
         flops=3e9,
     )
 
@@ -514,8 +549,7 @@
     partial.wait(last)
     own = jnp.concatenate([partial.held[last * GROUP + c] for c in blocks], axis=1)
     rows = jnp.transpose(own + more).astype(BF16)
-    slots = send.held.shape[0]
-    send.held[...] = dot(pick_rows(slots, 0, slot_row.all()[...]), rows).astype(BF16)
+    to_slots(slot_row.all()[...], rows, send)
 
 
 def mirror_back(arrived, slot_column, slot_row, partial, tiles):
@@ -525,13 +559,13 @@
         mirror_back_kernel,
         (),
         (
-            (arrived, 1),
+            (inner(arrived), 1),
             (slot_column, 1),
             (tiles, groups(tiles)),
             (partial, groups(tiles)),
             (slot_row, 1),
         ),
-        ((struct(slots, width), 1, 0), (struct(width, mirrors), 1, 0)),
+        ((struct(slots, width), 2, 0), (struct(width, mirrors), 1, 0)),
         flops=2e9,
     )
 
@@ -565,7 +599,7 @@
         back_far_kernel,
         (tile_count, tile_column),
         ((tiles, groups(tiles)), (turned, 1), (partial, groups(partial))),
-        ((struct(masters, width, EDGE, dtype=F32), masters // GROUP, 0),),
+        ((inner(struct(masters, width, EDGE, dtype=F32)), masters // GROUP, 0),),
         (pltpu.VMEM((mirrors // EDGE, row_blocks + 1, EDGE, EDGE), BF16),),
         flops=3e9,
     )
@@ -608,9 +642,9 @@
         finish_kernel,
         (core,),
         (
-            (back, 1),
+            (inner(back), 1),
             (asked_column, 1),
-            (partial, 1),
+            (inner(partial), 1),
             (features, 1),
             (grad_self, 1),
         ),

time: 171 us -> 171 us (level)
  local copies, waits for them, and re-layouts: 0.02 us -> 5.83 us
  Pallas kernels: 65.8 us -> 63.5 us
  starting transfers between devices: 43.8 us -> 41.5 us
    unnamed x6 -> x16, local copies, waits for them, and re-layouts: 0.02 us -> 5.83 us
    pallas_call x11, Pallas kernels: 64.4 us -> 62.1 us  [run(): pl.pallas_call(body, in_specs=[smem] * len(scalars) + specs[:n], out_spec...]
    all_to_all x6, starting transfers between devices: 40.2 us -> 38 us  [exchange(): lax.all_to_all(buffer.reshape(parts, buffer.shape[0] // parts, buffer.sha...]
  transfers between devices with their start and end apart: 8 -> 8, of which waited for: 8 -> 8; matrix products, arithmetic and copies ran while one was open for 4% -> 5% of each run, Pallas kernels for 21% -> 21%
where the time goes in v5:
time: 171 us
  Pallas kernels  63.5 us (37%)
  starting transfers between devices  41.5 us (24%)
  waiting for transfers between devices  33.9 us (20%)
  blocking collectives  14.8 us (9%)
  matrix products  8.29 us (5%)
  local copies, waits for them, and re-layouts  5.83 us (3%)
  other arithmetic  1.96 us (1%)
    pallas_call x11, Pallas kernels, run(): pl.pallas_call(body, in_specs=[smem] * len(scalars) + specs[:n], out_spec...  62.1 us
    all_to_all x6, starting transfers between devices, exchange(): lax.all_to_all(buffer.reshape(parts, buffer.shape[0] // parts, buffer.sha...  38 us
    all_to_all x6, waiting for transfers between devices, exchange(): lax.all_to_all(buffer.reshape(parts, buffer.shape[0] // parts, buffer.sha...  30.9 us
    all_to_all x1, blocking collectives, exchange(): lax.all_to_all(buffer.reshape(parts, buffer.shape[0] // parts, buffer.sha...  14.8 us
    unnamed x16, local copies, waits for them, and re-layouts  5.83 us
    dot_general x1, matrix products, on_device(): lax.dot_general(features, low, (((0,), (0,)), ((), ())), preferred_elemen...  3.97 us
    ppermute x2, starting transfers between devices, to_other_core(): return lax.ppermute(value, 'core', [(0, 1), (1, 0)])  3.44 us
  transfers between devices with their start and end apart: 8, of which 8 were waited for; matrix products, arithmetic and copies ran while one was open for 5% of the time, Pallas kernels for 21%

profile of v5, /device:TPU:1, one launch (start us, length us, event | category | flops | bytes accessed | tf_op | source)
XLA Modules:
  0.0 170.6 jit_solution(10803410660178819249)
XLA Ops:
  0.7 4.3 %shard_map.120 = (f32[128,128]{1,0:T(8,128)}, s32[1,512]{1,0:T(1,128)}, s32[512,128]{1,0:T(8,128)}) custom-call(s32[20]{0:T(128)} %refs_0_.7, s32[1,512]{1,0:T(1,128)} %bitcast.40, s32[1,512]{1,0:T(1,128)} %bitcast.41, bf16[20,16,128,128]{3,2,1,0:T(8,128)(2,1)} %refs_2_.6), custom_call_target="tpu_custom_call" | custom-call | flops 1000000000 | bytes 4194304 | tf_op jit(solution)/shard_map/pallas_call | solution.py:143
  5.0 12.0 %all-to-all-start = ((f32[128,1,128]{2,1,0:T(1,128)}), f32[128,1,128]{2,1,0:T(1,128)}, u32[]{:S(2)}, u32[]{:S(2)}) async-start(f32[128,1,128]{2,1,0:T(1,128)} %bitcast.36), calls=%async_computation | async-start | bytes 131072 | tf_op jit(solution)/shard_map/all_to_all | solution.py:722
  17.0 2.4 %fusion.1.refs_5_ = f32[2048,256]{1,0:T(8,128)} fusion(bf16[2048,768]{1,0:T(8,128)(2,1)S(1)} %copy-done.4, bf16[768,256]{1,0:T(8,128)(2,1)S(1)} %copy-done.5), kind=kOutput, calls=%fused_computation.4 | convolution fusion | flops 805306368 | bytes 5636096 | tf_op jit(solution)/shard_map/dot_general | solution.py:756
  19.3 2.0 %convolution_convert_fusion.refs_1_.refs_3_ = bf16[2048,256]{1,0:T(8,128)(2,1)} fusion(bf16[2048,768]{1,0:T(8,128)(2,1)S(1)} %copy-done.4, bf16[768,256]{1,0:T(8,128)(2,1)S(1)} %copy-done.6), kind=kOutput, calls=%fused_computation | convolution fusion | flops 805830656 | bytes 4587520 | tf_op jit(solution)/shard_map/dot_general | solution.py:755
  21.3 5.6 %all-to-all-done = f32[128,1,128]{2,1,0:T(1,128)} async-done(((f32[128,1,128]{2,1,0:T(1,128)}), f32[128,1,128]{2,1,0:T(1,128)}, u32[]{:S(2)}, u32[]{:S(2)}) %all-to-all-start) | async-done | bytes 65568 | tf_op jit(solution)/shard_map/all_to_all | solution.py:722
  26.9 3.3 %shard_map.121 = (bf16[1024,256]{1,0:T(8,128)(2,1)}, s32[1024,128]{1,0:T(8,128)}) custom-call(f32[128,128]{1,0:T(8,128)} %bitcast.4.refs_0_.refs_1_, bf16[2048,256]{1,0:T(8,128)(2,1)} %convolution_convert_fusion.refs_1_.refs_3_), custom_call_target="tpu_custom_call" | custom-call | flops 2000000000 | bytes 4194304 | tf_op jit(solution)/shard_map/pallas_call | solution.py:143
  30.2 4.2 %all-to-all-start.1 = ((bf16[128,8,256]{2,1,0:T(8,128)(2,1)}), bf16[128,8,256]{2,1,0:T(8,128)(2,1)S(1)}, u32[]{:S(2)}, u32[]{:S(2)}) async-start(bf16[128,8,256]{2,1,0:T(8,128)(2,1)} %bitcast.35), calls=%async_computation.1 | async-start | bytes 1048576 | tf_op jit(solution)/shard_map/all_to_all | solution.py:722
  34.4 10.0 %shard_map.122 = (f32[2560,256]{1,0:T(8,128)}, f32[2048,128]{1,0:T(8,128)}, bf16[20,4,128,128]{3,2,1,0:T(8,128)(2,1)}) custom-call(s32[20]{0:T(128)} %refs_0_.7, s32[16,20]{1,0:T(8,128)} %bitcast.37, bf16[20,16,128,128]{3,2,1,0:T(8,128)(2,1)} %refs_2_.6, bf16[2048,256]{1,0:T(8,128)(2,1)} %convolution_convert_fusion.refs_1_.refs_3_), custom_call_target="tpu_custom_call" | custom-call | flops 5000000000 | bytes 4194304 | tf_op jit(solution)/shard_map/pallas_call | solution.py:143
  44.5 4.1 %all-to-all-done.1 = bf16[128,8,256]{2,1,0:T(8,128)(2,1)S(1)} async-done(((bf16[128,8,256]{2,1,0:T(8,128)(2,1)}), bf16[128,8,256]{2,1,0:T(8,128)(2,1)S(1)}, u32[]{:S(2)}, u32[]{:S(2)}) %all-to-all-start.1) | async-done | bytes 524320 | tf_op jit(solution)/shard_map/all_to_all | solution.py:722
  48.6 3.3 %shard_map.123 = (bf16[1024,256]{1,0:T(8,128)(2,1)}, bf16[512,256]{1,0:T(8,128)(2,1)}) custom-call(bf16[1024,256]{1,0:T(8,128)(2,1)S(1)} %bitcast.31, s32[512,128]{1,0:T(8,128)} %get-tuple-element.38.refs_1_, f32[2560,256]{1,0:T(8,128)} %get-tuple-element.40.refs_2_.refs_4_, bf16[20,4,128,128]{3,2,1,0:T(8,128)(2,1)} %get-tuple-element.41.refs_3_.refs_2_, ...), custom_call_target="tpu_custom_call" | custom-call | flops 2000000000 | bytes 4194304 | tf_op jit(solution)/shard_map/pallas_call | solution.py:143
  51.9 6.1 %all-to-all-start.2 = ((bf16[128,8,256]{2,1,0:T(8,128)(2,1)}), bf16[128,8,256]{2,1,0:T(8,128)(2,1)S(1)}, u32[]{:S(2)}, u32[]{:S(2)}) async-start(bf16[128,8,256]{2,1,0:T(8,128)(2,1)} %bitcast.33), calls=%async_computation.2 | async-start | bytes 1048576 | tf_op jit(solution)/shard_map/all_to_all | solution.py:722
  58.0 6.3 %shard_map.124 = (f32[2048,256]{1,0:T(8,128)S(1)}, f32[2048,128]{1,0:T(8,128)}, s32[8,1024]{1,0:T(8,128)}) custom-call(bf16[512,256]{1,0:T(8,128)(2,1)} %get-tuple-element.43.refs_0_, f32[128,128]{1,0:T(8,128)} %bitcast.4.refs_0_.refs_1_, s32[1024,128]{1,0:T(8,128)} %get-tuple-element.44.refs_2_.refs_5_, ...), custom_call_target="tpu_custom_call" | custom-call | flops 5000000000 | bytes 4194304 | tf_op jit(solution)/shard_map/pallas_call | solution.py:143
  65.7 6.5 %all-to-all-done.2 = bf16[128,8,256]{2,1,0:T(8,128)(2,1)S(1)} async-done(((bf16[128,8,256]{2,1,0:T(8,128)(2,1)}), bf16[128,8,256]{2,1,0:T(8,128)(2,1)S(1)}, u32[]{:S(2)}, u32[]{:S(2)}) %all-to-all-start.2) | async-done | bytes 524320 | tf_op jit(solution)/shard_map/all_to_all | solution.py:722
  72.2 1.6 copy-done.3
  73.8 6.0 %shard_map.125 = (bf16[2048,256]{1,0:T(8,128)(2,1)}, bf16[2048,256]{1,0:T(8,128)(2,1)}, bf16[2048,256]{1,0:T(8,128)(2,1)}, bf16[1024,256]{1,0:T(8,128)(2,1)}) custom-call(s32[8,1024]{1,0:T(8,128)} %get-tuple-element.47.refs_0_, bf16[1024,256]{1,0:T(8,128)(2,1)S(1)} %bitcast.28, f32[2048,256]{1,0:T(8,128)S(1)} %copy-done.3, ...), custom_call_target="tpu_custom_call" | custom-call | flops 3000000000 | bytes 4194304 | tf_op jit(solution)/shard_map/pallas_call | solution.py:143
  79.8 3.7 %all-to-all-start.3 = ((bf16[128,8,256]{2,1,0:T(8,128)(2,1)}), bf16[128,8,256]{2,1,0:T(8,128)(2,1)S(1)}, u32[]{:S(2)}, u32[]{:S(2)}) async-start(bf16[128,8,256]{2,1,0:T(8,128)(2,1)} %bitcast.32), calls=%async_computation.3 | async-start | bytes 1048576 | tf_op jit(solution)/shard_map/all_to_all | solution.py:722
  83.5 9.5 %shard_map.126.refs_3_.refs_4_ = f32[20,256,128]{2,1,0:T(8,128)} custom-call(s32[20]{0:T(128)} %refs_0_.7, s32[16,20]{1,0:T(8,128)} %bitcast.38, bf16[20,16,128,128]{3,2,1,0:T(8,128)(2,1)} %refs_2_.6, bf16[2048,256]{1,0:T(8,128)(2,1)} %get-tuple-element.53.refs_3_), custom_call_target="tpu_custom_call" | custom-call | flops 5000000000 | bytes 4194304 | tf_op jit(solution)/shard_map/pallas_call | solution.py:143
  93.0 4.7 %all-to-all-done.3 = bf16[128,8,256]{2,1,0:T(8,128)(2,1)S(1)} async-done(((bf16[128,8,256]{2,1,0:T(8,128)(2,1)}), bf16[128,8,256]{2,1,0:T(8,128)(2,1)S(1)}, u32[]{:S(2)}, u32[]{:S(2)}) %all-to-all-start.3) | async-done | bytes 524320 | tf_op jit(solution)/shard_map/all_to_all | solution.py:722
  97.7 3.6 %shard_map.127 = (bf16[1024,256]{1,0:T(8,128)(2,1)}, bf16[256,512]{1,0:T(8,128)(2,1)}) custom-call(bf16[1024,256]{1,0:T(8,128)(2,1)S(1)} %bitcast.29, s32[512,128]{1,0:T(8,128)} %get-tuple-element.38.refs_1_, bf16[20,4,128,128]{3,2,1,0:T(8,128)(2,1)} %get-tuple-element.41.refs_3_.refs_2_, f32[20,256,128]{2,1,0:T(8,128)} %shard_map.126.refs_3_.refs_4_, ...), custom_call_target="tpu_custom_call" | custom-call | flops 2000000000 | bytes 4194304 | tf_op jit(solution)/shard_map/pallas_call | solution.py:143
  101.3 5.5 %all-to-all-start.4 = ((bf16[128,8,256]{2,1,0:T(8,128)(2,1)}), bf16[128,8,256]{2,1,0:T(8,128)(2,1)S(1)}, u32[]{:S(2)}, u32[]{:S(2)}) async-start(bf16[128,8,256]{2,1,0:T(8,128)(2,1)} %bitcast.34), calls=%async_computation.4 | async-start | bytes 1048576 | tf_op jit(solution)/shard_map/all_to_all | solution.py:722
  106.8 4.0 %fusion.refs_5_ = bf16[768,256]{1,0:T(8,128)(2,1)} fusion(bf16[2048,256]{1,0:T(8,128)(2,1)S(1)} %copy-done.7, bf16[2048,768]{1,0:T(8,128)(2,1)} %refs_4_.3), kind=kOutput, calls=%fused_computation.2 | convolution fusion | flops 805502976 | bytes 4587520 | tf_op jit(solution)/shard_map/dot_general | solution.py:769
  110.8 4.7 %shard_map.128.refs_3_ = f32[16,256,128]{2,1,0:T(8,128)S(1)} custom-call(s32[20]{0:T(128)} %refs_0_.7, s32[16,20]{1,0:T(8,128)} %bitcast.39, bf16[20,16,128,128]{3,2,1,0:T(8,128)(2,1)} %refs_2_.6, bf16[256,512]{1,0:T(8,128)(2,1)} %get-tuple-element.55.refs_3_, f32[20,256,128]{2,1,0:T(8,128)} %shard_map.126.refs_3_.refs_4_), custom_call_target="tpu_custom_call" | custom-call | flops 3000000000 | bytes 4194304 | tf_op jit(solution)/shard_map/pallas_call | solution.py:143
  116.8 4.1 %all-to-all-done.4 = bf16[128,8,256]{2,1,0:T(8,128)(2,1)S(1)} async-done(((bf16[128,8,256]{2,1,0:T(8,128)(2,1)}), bf16[128,8,256]{2,1,0:T(8,128)(2,1)S(1)}, u32[]{:S(2)}, u32[]{:S(2)}) %all-to-all-start.4) | async-done | bytes 524320 | tf_op jit(solution)/shard_map/all_to_all | solution.py:722
  121.0 1.6 copy-done.1
  122.6 6.2 %shard_map.129 = (bf16[256,2048]{1,0:T(8,128)(2,1)}, f32[1536,128]{1,0:T(8,128)}, bf16[1536,128]{1,0:T(8,128)(2,1)}) custom-call(s32[1]{0:T(128)} %bitcast.10.refs_0_.core, bf16[1024,256]{1,0:T(8,128)(2,1)S(1)} %bitcast.30, s32[1024,128]{1,0:T(8,128)} %get-tuple-element.44.refs_2_.refs_5_, f32[16,256,128]{2,1,0:T(8,128)S(1)} %copy-done.1, ...), custom_call_target="tpu_custom_call" | custom-call | flops 3000000000 | bytes 4194304 | tf_op jit(solution)/shard_map/pallas_call | solution.py:143
  129.1 1.7 collective-permute-done
  130.8 2.0 %add_convert_fusion = bf16[1536,128]{1,0:T(8,128)(2,1)} fusion(f32[1536,128]{1,0:T(8,128)} %get-tuple-element.57, bf16[1536,128]{1,0:T(8,128)(2,1)S(1)} %collective-permute-done), kind=kLoop, calls=%fused_computation.3 | loop fusion | flops 589824 | bytes 1572864 | tf_op jit(solution)/shard_map/convert_element_type | solution.py:776
  132.7 6.6 %all-to-all-start.5 = ((bf16[64,24,128]{2,1,0:T(8,128)(2,1)}), bf16[64,24,128]{2,1,0:T(8,128)(2,1)S(1)}, u32[]{:S(2)}, u32[]{:S(2)}) async-start(bf16[64,24,128]{2,1,0:T(8,128)(2,1)} %bitcast.16), calls=%async_computation.5 | async-start | bytes 786432 | tf_op jit(solution)/shard_map/all_to_all | solution.py:722
  139.3 4.8 %shard_map.130 = bf16[2048,768]{1,0:T(8,128)(2,1)} custom-call(bf16[2048,256]{1,0:T(8,128)(2,1)} %get-tuple-element.56.refs_0_, bf16[256,2048]{1,0:T(8,128)(2,1)} %get-tuple-element.59.refs_1_, bf16[768,256]{1,0:T(8,128)(2,1)} %refs_2_.7, bf16[768,256]{1,0:T(8,128)(2,1)} %refs_3_.3), custom_call_target="tpu_custom_call" | custom-call | flops 3000000000 | bytes 4194304 | tf_op jit(solution)/shard_map/pallas_call | solution.py:143
  144.1 5.9 %all-to-all-done.5.parts = bf16[64,24,128]{2,1,0:T(8,128)(2,1)S(1)} async-done(((bf16[64,24,128]{2,1,0:T(8,128)(2,1)}), bf16[64,24,128]{2,1,0:T(8,128)(2,1)S(1)}, u32[]{:S(2)}, u32[]{:S(2)}) %all-to-all-start.5) | async-done | bytes 393248 | tf_op jit(solution)/shard_map/all_to_all | solution.py:722
  150.1 14.8 %all_to_all.35 = bf16[64,24,128]{2,1,0:T(8,128)(2,1)S(1)} all-to-all(bf16[64,24,128]{2,1,0:T(8,128)(2,1)S(1)} %shard_map.131), channel_id=1, replica_groups=mesh['chip'=16,'core'=2,'local'=4] {'chip','local'}, dimensions={0} | all-to-all | bytes 786432 | tf_op jit(solution)/shard_map/all_to_all | solution.py:722
  164.9 3.1 %collective-permute-start.1 = (bf16[1536,128]{1,0:T(8,128)(2,1)S(1)}, bf16[1536,128]{1,0:T(8,128)(2,1)S(1)}, u32[]{:S(2)}, u32[]{:S(2)}) collective-permute-start(bf16[1536,128]{1,0:T(8,128)(2,1)S(1)} %bitcast.26), channel_id=1, source_target_pairs={{0,4},{4,0},{1,5},{5,1},{2,6},{6,2},{3,7},{7,3},{8,12},{12,8},{9,1... | collective-permute-start | bytes 1179656 | tf_op jit(solution)/shard_map/ppermute | solution.py:733
  (18 shorter events, 5.7 us)
Async XLA Ops:
  0.6 16.3 %copy-start.4 = (bf16[2048,768]{1,0:T(8,128)(2,1)S(1)}, bf16[2048,768]{1,0:T(8,128)(2,1)}, u32[]{:S(2)}) copy-start(bf16[2048,768]{1,0:T(8,128)(2,1)} %refs_4_.3) | copy-start | bytes 9437188
  0.6 16.3 %copy-start.5 = (bf16[768,256]{1,0:T(8,128)(2,1)S(1)}, bf16[768,256]{1,0:T(8,128)(2,1)}, u32[]{:S(2)}) copy-start(bf16[768,256]{1,0:T(8,128)(2,1)} %refs_2_.7) | copy-start | bytes 1179652
  5.0 21.9 %all-to-all-start = ((f32[128,1,128]{2,1,0:T(1,128)}), f32[128,1,128]{2,1,0:T(1,128)}, u32[]{:S(2)}, u32[]{:S(2)}) async-start(f32[128,1,128]{2,1,0:T(1,128)} %bitcast.36), calls=%async_computation | async-start | bytes 131072 | tf_op jit(solution)/shard_map/all_to_all | solution.py:722
  17.0 2.4 %copy-start.6 = (bf16[768,256]{1,0:T(8,128)(2,1)S(1)}, bf16[768,256]{1,0:T(8,128)(2,1)}, u32[]{:S(2)}) copy-start(bf16[768,256]{1,0:T(8,128)(2,1)} %refs_3_.3) | copy-start | bytes 1179652
  30.2 18.4 %all-to-all-start.1 = ((bf16[128,8,256]{2,1,0:T(8,128)(2,1)}), bf16[128,8,256]{2,1,0:T(8,128)(2,1)S(1)}, u32[]{:S(2)}, u32[]{:S(2)}) async-start(bf16[128,8,256]{2,1,0:T(8,128)(2,1)} %bitcast.35), calls=%async_computation.1 | async-start | bytes 1048576 | tf_op jit(solution)/shard_map/all_to_all | solution.py:722
  51.9 20.3 %all-to-all-start.2 = ((bf16[128,8,256]{2,1,0:T(8,128)(2,1)}), bf16[128,8,256]{2,1,0:T(8,128)(2,1)S(1)}, u32[]{:S(2)}, u32[]{:S(2)}) async-start(bf16[128,8,256]{2,1,0:T(8,128)(2,1)} %bitcast.33), calls=%async_computation.2 | async-start | bytes 1048576 | tf_op jit(solution)/shard_map/all_to_all | solution.py:722
  64.3 1.3 copy-start.2
  72.2 1.6 copy-start.3
  79.8 18.0 %all-to-all-start.3 = ((bf16[128,8,256]{2,1,0:T(8,128)(2,1)}), bf16[128,8,256]{2,1,0:T(8,128)(2,1)S(1)}, u32[]{:S(2)}, u32[]{:S(2)}) async-start(bf16[128,8,256]{2,1,0:T(8,128)(2,1)} %bitcast.32), calls=%async_computation.3 | async-start | bytes 1048576 | tf_op jit(solution)/shard_map/all_to_all | solution.py:722
  97.7 9.1 %copy-start.7 = (bf16[2048,256]{1,0:T(8,128)(2,1)S(1)}, bf16[2048,256]{1,0:T(8,128)(2,1)}, u32[]{:S(2)}) copy-start(bf16[2048,256]{1,0:T(8,128)(2,1)} %get-tuple-element.56.refs_0_) | copy-start | bytes 3145732
  101.3 19.6 %all-to-all-start.4 = ((bf16[128,8,256]{2,1,0:T(8,128)(2,1)}), bf16[128,8,256]{2,1,0:T(8,128)(2,1)S(1)}, u32[]{:S(2)}, u32[]{:S(2)}) async-start(bf16[128,8,256]{2,1,0:T(8,128)(2,1)} %bitcast.34), calls=%async_computation.4 | async-start | bytes 1048576 | tf_op jit(solution)/shard_map/all_to_all | solution.py:722
  115.5 1.3 copy-start
  121.0 1.6 copy-start.1
  128.8 2.0 %collective-permute-start = (bf16[1536,128]{1,0:T(8,128)(2,1)}, bf16[1536,128]{1,0:T(8,128)(2,1)S(1)}, u32[]{:S(2)}, u32[]{:S(2)}) collective-permute-start(bf16[1536,128]{1,0:T(8,128)(2,1)} %get-tuple-element.58), channel_id=1, source_target_pairs={{0,4},{4,0},{1,5},{5,1},{2,6},{6,2},{3,7},{7,3},{8,12},{12,8},{9,1... | collective-permute-start | bytes 1179656 | tf_op jit(solution)/shard_map/ppermute | solution.py:733
  132.7 17.2 %all-to-all-start.5 = ((bf16[64,24,128]{2,1,0:T(8,128)(2,1)}), bf16[64,24,128]{2,1,0:T(8,128)(2,1)S(1)}, u32[]{:S(2)}, u32[]{:S(2)}) async-start(bf16[64,24,128]{2,1,0:T(8,128)(2,1)} %bitcast.16), calls=%async_computation.5 | async-start | bytes 786432 | tf_op jit(solution)/shard_map/all_to_all | solution.py:722
  164.9 4.5 %collective-permute-start.1 = (bf16[1536,128]{1,0:T(8,128)(2,1)S(1)}, bf16[1536,128]{1,0:T(8,128)(2,1)S(1)}, u32[]{:S(2)}, u32[]{:S(2)}) collective-permute-start(bf16[1536,128]{1,0:T(8,128)(2,1)S(1)} %bitcast.26), channel_id=1, source_target_pairs={{0,4},{4,0},{1,5},{5,1},{2,6},{6,2},{3,7},{7,3},{8,12},{12,8},{9,1... | collective-permute-start | bytes 1179656 | tf_op jit(solution)/shard_map/ppermute | solution.py:733

commit v6 on v5

--- a/solution.py
+++ b/solution.py
@@ -485,7 +485,7 @@
         (),
         (
             (asked_row, 1),
-            (inner(back), 1),
+            (back, 1),
             (inner(base), 2),
             (scale, 2),
             (cotangent, 2),
@@ -642,7 +642,7 @@
         finish_kernel,
         (core,),
         (
-            (inner(back), 1),
+            (back, 1),
             (asked_column, 1),
             (inner(partial), 1),
             (features, 1),
@@ -761,7 +761,7 @@
     arrived = exchange(rows)
     partial, degree, far_tiles = near(tile_count, tile_column, tile_weight, projected)
     send, slab = mirror_out(arrived, slot_column, slot_row, partial, far_tiles)
-    back = exchange(send)
+    back = pltpu.with_memory_space_constraint(exchange(send), pltpu.HBM)
     base, scale, asked_row = far(far_tiles, slab, partial, degree, own, asked, asked_column)
     mixed, low, spread, send = turn(base, scale, cotangent, back, asked_row, asked_column)
     arrived = exchange(send)
@@ -770,7 +770,7 @@
         features, low, (((0,), (0,)), ((), ())), preferred_element_type=F32
     ).astype(BF16)
     send, turned = mirror_back(arrived, slot_column, slot_row, partial, far_tiles)
-    back = exchange(send)
+    back = pltpu.with_memory_space_constraint(exchange(send), pltpu.HBM)
     partial = back_far(tile_count, tile_column, tile_weight, turned, partial)
     d_projected, keep, give = finish(core, partial, back, asked_column, features, grad_self)
     pair = (keep + to_other_core(give).astype(F32)).astype(BF16)

time: 171 us -> 167 us (0.977)
  local copies, waits for them, and re-layouts: 5.83 us -> 1.61 us
  waiting for transfers between devices: 33.9 us -> 35.7 us
  starting transfers between devices: 41.5 us -> 39.7 us
    unnamed x16 -> x12, local copies, waits for them, and re-layouts: 5.83 us -> 1.61 us
    all_to_all x6, starting transfers between devices: 38 us -> 36.2 us  [exchange(): lax.all_to_all(buffer.reshape(parts, buffer.shape[0] // parts, buffer.sha...]
    all_to_all x6, waiting for transfers between devices: 30.9 us -> 32.7 us  [exchange(): lax.all_to_all(buffer.reshape(parts, buffer.shape[0] // parts, buffer.sha...]
  transfers between devices with their start and end apart: 8 -> 8, of which waited for: 8 -> 8; matrix products, arithmetic and copies ran while one was open for 5% -> 5% of each run, Pallas kernels for 21% -> 22%
where the time goes in v6:
time: 167 us; the launch traced here: 166 us
  Pallas kernels  63.6 us (38%)
  starting transfers between devices  39.7 us (24%)
  waiting for transfers between devices  35.7 us (21%)
  blocking collectives  14.6 us (9%)
  matrix products  8.29 us (5%)
  other arithmetic  1.96 us (1%)
    pallas_call x11, Pallas kernels, run(): pl.pallas_call(body, in_specs=[smem] * len(scalars) + specs[:n], out_spec...  62.2 us
    all_to_all x6, starting transfers between devices, exchange(): lax.all_to_all(buffer.reshape(parts, buffer.shape[0] // parts, buffer.sha...  36.2 us
    all_to_all x6, waiting for transfers between devices, exchange(): lax.all_to_all(buffer.reshape(parts, buffer.shape[0] // parts, buffer.sha...  32.7 us
    all_to_all x1, blocking collectives, exchange(): lax.all_to_all(buffer.reshape(parts, buffer.shape[0] // parts, buffer.sha...  14.6 us
    dot_general x1, matrix products, on_device(): lax.dot_general(features, low, (((0,), (0,)), ((), ())), preferred_elemen...  3.97 us
    ppermute x2, starting transfers between devices, to_other_core(): return lax.ppermute(value, 'core', [(0, 1), (1, 0)])  3.53 us
  transfers between devices with their start and end apart: 8, of which 8 were waited for; matrix products, arithmetic and copies ran while one was open for 5% of the time, Pallas kernels for 22%

profile of v6, /device:TPU:1, one launch (start us, length us, event | category | flops | bytes accessed | tf_op | source)
XLA Modules:
  0.0 166.3 jit_solution(6065826921686045080)
XLA Ops:
  0.7 4.3 %shard_map.120 = (f32[128,128]{1,0:T(8,128)}, s32[1,512]{1,0:T(1,128)}, s32[512,128]{1,0:T(8,128)}) custom-call(s32[20]{0:T(128)} %refs_0_.7, s32[1,512]{1,0:T(1,128)} %bitcast.40, s32[1,512]{1,0:T(1,128)} %bitcast.41, bf16[20,16,128,128]{3,2,1,0:T(8,128)(2,1)} %refs_2_.6), custom_call_target="tpu_custom_call" | custom-call | flops 1000000000 | bytes 4194304 | tf_op jit(solution)/shard_map/pallas_call | solution.py:143
  5.0 12.0 %all-to-all-start = ((f32[128,1,128]{2,1,0:T(1,128)}), f32[128,1,128]{2,1,0:T(1,128)}, u32[]{:S(2)}, u32[]{:S(2)}) async-start(f32[128,1,128]{2,1,0:T(1,128)} %bitcast.36), calls=%async_computation | async-start | bytes 131072 | tf_op jit(solution)/shard_map/all_to_all | solution.py:722
  17.0 2.4 %fusion.1.refs_5_ = f32[2048,256]{1,0:T(8,128)} fusion(bf16[2048,768]{1,0:T(8,128)(2,1)S(1)} %copy-done, bf16[768,256]{1,0:T(8,128)(2,1)S(1)} %copy-done.3), kind=kOutput, calls=%fused_computation.4 | convolution fusion | flops 805306368 | bytes 5636096 | tf_op jit(solution)/shard_map/dot_general | solution.py:756
  19.3 2.0 %convolution_convert_fusion.refs_1_.refs_3_ = bf16[2048,256]{1,0:T(8,128)(2,1)} fusion(bf16[2048,768]{1,0:T(8,128)(2,1)S(1)} %copy-done, bf16[768,256]{1,0:T(8,128)(2,1)S(1)} %copy-done.4), kind=kOutput, calls=%fused_computation | convolution fusion | flops 805830656 | bytes 4587520 | tf_op jit(solution)/shard_map/dot_general | solution.py:755
  21.3 5.4 %all-to-all-done = f32[128,1,128]{2,1,0:T(1,128)} async-done(((f32[128,1,128]{2,1,0:T(1,128)}), f32[128,1,128]{2,1,0:T(1,128)}, u32[]{:S(2)}, u32[]{:S(2)}) %all-to-all-start) | async-done | bytes 65568 | tf_op jit(solution)/shard_map/all_to_all | solution.py:722
  26.7 3.3 %shard_map.121 = (bf16[1024,256]{1,0:T(8,128)(2,1)}, s32[1024,128]{1,0:T(8,128)}) custom-call(f32[128,128]{1,0:T(8,128)} %bitcast.4.refs_0_.refs_1_, bf16[2048,256]{1,0:T(8,128)(2,1)} %convolution_convert_fusion.refs_1_.refs_3_), custom_call_target="tpu_custom_call" | custom-call | flops 2000000000 | bytes 4194304 | tf_op jit(solution)/shard_map/pallas_call | solution.py:143
  30.1 4.4 %all-to-all-start.1 = ((bf16[128,8,256]{2,1,0:T(8,128)(2,1)}), bf16[128,8,256]{2,1,0:T(8,128)(2,1)S(1)}, u32[]{:S(2)}, u32[]{:S(2)}) async-start(bf16[128,8,256]{2,1,0:T(8,128)(2,1)} %bitcast.35), calls=%async_computation.1 | async-start | bytes 1048576 | tf_op jit(solution)/shard_map/all_to_all | solution.py:722
  34.4 10.3 %shard_map.122 = (f32[2560,256]{1,0:T(8,128)}, f32[2048,128]{1,0:T(8,128)}, bf16[20,4,128,128]{3,2,1,0:T(8,128)(2,1)}) custom-call(s32[20]{0:T(128)} %refs_0_.7, s32[16,20]{1,0:T(8,128)} %bitcast.37, bf16[20,16,128,128]{3,2,1,0:T(8,128)(2,1)} %refs_2_.6, bf16[2048,256]{1,0:T(8,128)(2,1)} %convolution_convert_fusion.refs_1_.refs_3_), custom_call_target="tpu_custom_call" | custom-call | flops 5000000000 | bytes 4194304 | tf_op jit(solution)/shard_map/pallas_call | solution.py:143
  44.8 3.8 %all-to-all-done.1 = bf16[128,8,256]{2,1,0:T(8,128)(2,1)S(1)} async-done(((bf16[128,8,256]{2,1,0:T(8,128)(2,1)}), bf16[128,8,256]{2,1,0:T(8,128)(2,1)S(1)}, u32[]{:S(2)}, u32[]{:S(2)}) %all-to-all-start.1) | async-done | bytes 524320 | tf_op jit(solution)/shard_map/all_to_all | solution.py:722
  48.6 3.3 %shard_map.123 = (bf16[1024,256]{1,0:T(8,128)(2,1)}, bf16[512,256]{1,0:T(8,128)(2,1)}) custom-call(bf16[1024,256]{1,0:T(8,128)(2,1)S(1)} %bitcast.29, s32[512,128]{1,0:T(8,128)} %get-tuple-element.38.refs_1_, f32[2560,256]{1,0:T(8,128)} %get-tuple-element.40.refs_2_.refs_4_, bf16[20,4,128,128]{3,2,1,0:T(8,128)(2,1)} %get-tuple-element.41.refs_3_.refs_2_, ...), custom_call_target="tpu_custom_call" | custom-call | flops 2000000000 | bytes 4194304 | tf_op jit(solution)/shard_map/pallas_call | solution.py:143
  51.9 5.7 %all-to-all-start.2 = ((bf16[128,8,256]{2,1,0:T(8,128)(2,1)}), bf16[128,8,256]{2,1,0:T(8,128)(2,1)S(1)}, u32[]{:S(2)}, u32[]{:S(2)}) async-start(bf16[128,8,256]{2,1,0:T(8,128)(2,1)} %bitcast.33), calls=%async_computation.2 | async-start | bytes 1048576 | tf_op jit(solution)/shard_map/all_to_all | solution.py:722
  57.6 6.3 %shard_map.124 = (f32[2048,256]{1,0:T(8,128)S(1)}, f32[2048,128]{1,0:T(8,128)}, s32[8,1024]{1,0:T(8,128)}) custom-call(bf16[512,256]{1,0:T(8,128)(2,1)} %get-tuple-element.43.refs_0_, f32[128,128]{1,0:T(8,128)} %bitcast.4.refs_0_.refs_1_, s32[1024,128]{1,0:T(8,128)} %get-tuple-element.44.refs_2_.refs_5_, ...), custom_call_target="tpu_custom_call" | custom-call | flops 5000000000 | bytes 4194304 | tf_op jit(solution)/shard_map/pallas_call | solution.py:143
  63.9 7.8 %all-to-all-done.2 = bf16[128,8,256]{2,1,0:T(8,128)(2,1)S(1)} async-done(((bf16[128,8,256]{2,1,0:T(8,128)(2,1)}), bf16[128,8,256]{2,1,0:T(8,128)(2,1)S(1)}, u32[]{:S(2)}, u32[]{:S(2)}) %all-to-all-start.2) | async-done | bytes 524320 | tf_op jit(solution)/shard_map/all_to_all | solution.py:722
  72.5 6.2 %shard_map.125 = (bf16[2048,256]{1,0:T(8,128)(2,1)}, bf16[2048,256]{1,0:T(8,128)(2,1)}, bf16[2048,256]{1,0:T(8,128)(2,1)}, bf16[1024,256]{1,0:T(8,128)(2,1)}) custom-call(s32[8,1024]{1,0:T(8,128)} %get-tuple-element.47.refs_0_, bf16[1024,256]{1,0:T(8,128)(2,1)} %bitcast.30, f32[2048,256]{1,0:T(8,128)S(1)} %get-tuple-element.49.refs_2_, ...), custom_call_target="tpu_custom_call" | custom-call | flops 3000000000 | bytes 4194304 | tf_op jit(solution)/shard_map/pallas_call | solution.py:143
  78.7 3.7 %all-to-all-start.3 = ((bf16[128,8,256]{2,1,0:T(8,128)(2,1)}), bf16[128,8,256]{2,1,0:T(8,128)(2,1)S(1)}, u32[]{:S(2)}, u32[]{:S(2)}) async-start(bf16[128,8,256]{2,1,0:T(8,128)(2,1)} %bitcast.31), calls=%async_computation.3 | async-start | bytes 1048576 | tf_op jit(solution)/shard_map/all_to_all | solution.py:722
  82.4 9.8 %shard_map.126.refs_3_.refs_4_ = f32[20,256,128]{2,1,0:T(8,128)} custom-call(s32[20]{0:T(128)} %refs_0_.7, s32[16,20]{1,0:T(8,128)} %bitcast.38, bf16[20,16,128,128]{3,2,1,0:T(8,128)(2,1)} %refs_2_.6, bf16[2048,256]{1,0:T(8,128)(2,1)} %get-tuple-element.53.refs_3_), custom_call_target="tpu_custom_call" | custom-call | flops 5000000000 | bytes 4194304 | tf_op jit(solution)/shard_map/pallas_call | solution.py:143
  92.2 4.5 %all-to-all-done.3 = bf16[128,8,256]{2,1,0:T(8,128)(2,1)S(1)} async-done(((bf16[128,8,256]{2,1,0:T(8,128)(2,1)}), bf16[128,8,256]{2,1,0:T(8,128)(2,1)S(1)}, u32[]{:S(2)}, u32[]{:S(2)}) %all-to-all-start.3) | async-done | bytes 524320 | tf_op jit(solution)/shard_map/all_to_all | solution.py:722
  96.7 3.6 %shard_map.127 = (bf16[1024,256]{1,0:T(8,128)(2,1)}, bf16[256,512]{1,0:T(8,128)(2,1)}) custom-call(bf16[1024,256]{1,0:T(8,128)(2,1)S(1)} %bitcast.28, s32[512,128]{1,0:T(8,128)} %get-tuple-element.38.refs_1_, bf16[20,4,128,128]{3,2,1,0:T(8,128)(2,1)} %get-tuple-element.41.refs_3_.refs_2_, f32[20,256,128]{2,1,0:T(8,128)} %shard_map.126.refs_3_.refs_4_, ...), custom_call_target="tpu_custom_call" | custom-call | flops 2000000000 | bytes 4194304 | tf_op jit(solution)/shard_map/pallas_call | solution.py:143
  100.3 5.2 %all-to-all-start.4 = ((bf16[128,8,256]{2,1,0:T(8,128)(2,1)}), bf16[128,8,256]{2,1,0:T(8,128)(2,1)S(1)}, u32[]{:S(2)}, u32[]{:S(2)}) async-start(bf16[128,8,256]{2,1,0:T(8,128)(2,1)} %bitcast.34), calls=%async_computation.4 | async-start | bytes 1048576 | tf_op jit(solution)/shard_map/all_to_all | solution.py:722
  105.5 4.0 %fusion.refs_5_ = bf16[768,256]{1,0:T(8,128)(2,1)} fusion(bf16[2048,256]{1,0:T(8,128)(2,1)S(1)} %copy-done.5, bf16[2048,768]{1,0:T(8,128)(2,1)} %refs_4_.3), kind=kOutput, calls=%fused_computation.2 | convolution fusion | flops 805502976 | bytes 4587520 | tf_op jit(solution)/shard_map/dot_general | solution.py:769
  109.5 4.9 %shard_map.128.refs_3_ = f32[16,256,128]{2,1,0:T(8,128)S(1)} custom-call(s32[20]{0:T(128)} %refs_0_.7, s32[16,20]{1,0:T(8,128)} %bitcast.39, bf16[20,16,128,128]{3,2,1,0:T(8,128)(2,1)} %refs_2_.6, bf16[256,512]{1,0:T(8,128)(2,1)} %get-tuple-element.55.refs_3_, f32[20,256,128]{2,1,0:T(8,128)} %shard_map.126.refs_3_.refs_4_), custom_call_target="tpu_custom_call" | custom-call | flops 3000000000 | bytes 4194304 | tf_op jit(solution)/shard_map/pallas_call | solution.py:143
  114.3 5.3 %all-to-all-done.4 = bf16[128,8,256]{2,1,0:T(8,128)(2,1)S(1)} async-done(((bf16[128,8,256]{2,1,0:T(8,128)(2,1)}), bf16[128,8,256]{2,1,0:T(8,128)(2,1)S(1)}, u32[]{:S(2)}, u32[]{:S(2)}) %all-to-all-start.4) | async-done | bytes 524320 | tf_op jit(solution)/shard_map/all_to_all | solution.py:722
  120.4 5.4 %shard_map.129 = (bf16[256,2048]{1,0:T(8,128)(2,1)}, f32[1536,128]{1,0:T(8,128)}, bf16[1536,128]{1,0:T(8,128)(2,1)}) custom-call(s32[1]{0:T(128)} %bitcast.10.refs_0_.core, bf16[1024,256]{1,0:T(8,128)(2,1)} %bitcast.32, s32[1024,128]{1,0:T(8,128)} %get-tuple-element.44.refs_2_.refs_5_, f32[16,256,128]{2,1,0:T(8,128)S(1)} %shard_map.128.refs_3_, ...), custom_call_target="tpu_custom_call" | custom-call | flops 3000000000 | bytes 4194304 | tf_op jit(solution)/shard_map/pallas_call | solution.py:143
  126.1 1.7 %collective-permute-done = bf16[1536,128]{1,0:T(8,128)(2,1)S(1)} collective-permute-done((bf16[1536,128]{1,0:T(8,128)(2,1)}, bf16[1536,128]{1,0:T(8,128)(2,1)S(1)}, u32[]{:S(2)}, u32[]{:S(2)}) %collective-permute-start) | collective-permute-done | bytes 393248 | tf_op jit(solution)/shard_map/ppermute | solution.py:733
  127.8 2.0 %add_convert_fusion = bf16[1536,128]{1,0:T(8,128)(2,1)} fusion(f32[1536,128]{1,0:T(8,128)} %get-tuple-element.57, bf16[1536,128]{1,0:T(8,128)(2,1)S(1)} %collective-permute-done), kind=kLoop, calls=%fused_computation.3 | loop fusion | flops 589824 | bytes 1572864 | tf_op jit(solution)/shard_map/convert_element_type | solution.py:776
  129.8 5.3 %all-to-all-start.5 = ((bf16[64,24,128]{2,1,0:T(8,128)(2,1)}), bf16[64,24,128]{2,1,0:T(8,128)(2,1)S(1)}, u32[]{:S(2)}, u32[]{:S(2)}) async-start(bf16[64,24,128]{2,1,0:T(8,128)(2,1)} %bitcast.16), calls=%async_computation.5 | async-start | bytes 786432 | tf_op jit(solution)/shard_map/all_to_all | solution.py:722
  135.0 4.8 %shard_map.130 = bf16[2048,768]{1,0:T(8,128)(2,1)} custom-call(bf16[2048,256]{1,0:T(8,128)(2,1)} %get-tuple-element.56.refs_0_, bf16[256,2048]{1,0:T(8,128)(2,1)} %get-tuple-element.59.refs_1_, bf16[768,256]{1,0:T(8,128)(2,1)} %refs_2_.7, bf16[768,256]{1,0:T(8,128)(2,1)} %refs_3_.3), custom_call_target="tpu_custom_call" | custom-call | flops 3000000000 | bytes 4194304 | tf_op jit(solution)/shard_map/pallas_call | solution.py:143
  139.8 5.9 %all-to-all-done.5.parts = bf16[64,24,128]{2,1,0:T(8,128)(2,1)S(1)} async-done(((bf16[64,24,128]{2,1,0:T(8,128)(2,1)}), bf16[64,24,128]{2,1,0:T(8,128)(2,1)S(1)}, u32[]{:S(2)}, u32[]{:S(2)}) %all-to-all-start.5) | async-done | bytes 393248 | tf_op jit(solution)/shard_map/all_to_all | solution.py:722
  145.9 14.6 %all_to_all.35 = bf16[64,24,128]{2,1,0:T(8,128)(2,1)S(1)} all-to-all(bf16[64,24,128]{2,1,0:T(8,128)(2,1)S(1)} %shard_map.131), channel_id=1, replica_groups=mesh['chip'=16,'core'=2,'local'=4] {'chip','local'}, dimensions={0} | all-to-all | bytes 786432 | tf_op jit(solution)/shard_map/all_to_all | solution.py:722
  160.5 3.2 %collective-permute-start.1 = (bf16[1536,128]{1,0:T(8,128)(2,1)S(1)}, bf16[1536,128]{1,0:T(8,128)(2,1)S(1)}, u32[]{:S(2)}, u32[]{:S(2)}) collective-permute-start(bf16[1536,128]{1,0:T(8,128)(2,1)S(1)} %bitcast.26), channel_id=1, source_target_pairs={{0,4},{4,0},{1,5},{5,1},{2,6},{6,2},{3,7},{7,3},{8,12},{12,8},{9,1... | collective-permute-start | bytes 1179656 | tf_op jit(solution)/shard_map/ppermute | solution.py:733
  163.7 1.3 collective-permute-done.1.other
  165.0 1.3 shard_map.132
  (14 shorter events, 2.0 us)
Async XLA Ops:
  0.6 16.3 %copy-start = (bf16[2048,768]{1,0:T(8,128)(2,1)S(1)}, bf16[2048,768]{1,0:T(8,128)(2,1)}, u32[]{:S(2)}) copy-start(bf16[2048,768]{1,0:T(8,128)(2,1)} %refs_4_.3) | copy-start | bytes 9437188
  0.6 16.3 %copy-start.3 = (bf16[768,256]{1,0:T(8,128)(2,1)S(1)}, bf16[768,256]{1,0:T(8,128)(2,1)}, u32[]{:S(2)}) copy-start(bf16[768,256]{1,0:T(8,128)(2,1)} %refs_2_.7) | copy-start | bytes 1179652
  5.0 21.7 %all-to-all-start = ((f32[128,1,128]{2,1,0:T(1,128)}), f32[128,1,128]{2,1,0:T(1,128)}, u32[]{:S(2)}, u32[]{:S(2)}) async-start(f32[128,1,128]{2,1,0:T(1,128)} %bitcast.36), calls=%async_computation | async-start | bytes 131072 | tf_op jit(solution)/shard_map/all_to_all | solution.py:722
  17.0 2.4 %copy-start.4 = (bf16[768,256]{1,0:T(8,128)(2,1)S(1)}, bf16[768,256]{1,0:T(8,128)(2,1)}, u32[]{:S(2)}) copy-start(bf16[768,256]{1,0:T(8,128)(2,1)} %refs_3_.3) | copy-start | bytes 1179652
  30.1 18.5 %all-to-all-start.1 = ((bf16[128,8,256]{2,1,0:T(8,128)(2,1)}), bf16[128,8,256]{2,1,0:T(8,128)(2,1)S(1)}, u32[]{:S(2)}, u32[]{:S(2)}) async-start(bf16[128,8,256]{2,1,0:T(8,128)(2,1)} %bitcast.35), calls=%async_computation.1 | async-start | bytes 1048576 | tf_op jit(solution)/shard_map/all_to_all | solution.py:722
  51.9 19.8 %all-to-all-start.2 = ((bf16[128,8,256]{2,1,0:T(8,128)(2,1)}), bf16[128,8,256]{2,1,0:T(8,128)(2,1)S(1)}, u32[]{:S(2)}, u32[]{:S(2)}) async-start(bf16[128,8,256]{2,1,0:T(8,128)(2,1)} %bitcast.33), calls=%async_computation.2 | async-start | bytes 1048576 | tf_op jit(solution)/shard_map/all_to_all | solution.py:722
  71.7 0.8 copy-start.1
  78.7 18.0 %all-to-all-start.3 = ((bf16[128,8,256]{2,1,0:T(8,128)(2,1)}), bf16[128,8,256]{2,1,0:T(8,128)(2,1)S(1)}, u32[]{:S(2)}, u32[]{:S(2)}) async-start(bf16[128,8,256]{2,1,0:T(8,128)(2,1)} %bitcast.31), calls=%async_computation.3 | async-start | bytes 1048576 | tf_op jit(solution)/shard_map/all_to_all | solution.py:722
  96.7 8.8 %copy-start.5 = (bf16[2048,256]{1,0:T(8,128)(2,1)S(1)}, bf16[2048,256]{1,0:T(8,128)(2,1)}, u32[]{:S(2)}) copy-start(bf16[2048,256]{1,0:T(8,128)(2,1)} %get-tuple-element.56.refs_0_) | copy-start | bytes 3145732
  100.3 19.4 %all-to-all-start.4 = ((bf16[128,8,256]{2,1,0:T(8,128)(2,1)}), bf16[128,8,256]{2,1,0:T(8,128)(2,1)S(1)}, u32[]{:S(2)}, u32[]{:S(2)}) async-start(bf16[128,8,256]{2,1,0:T(8,128)(2,1)} %bitcast.34), calls=%async_computation.4 | async-start | bytes 1048576 | tf_op jit(solution)/shard_map/all_to_all | solution.py:722
  119.6 0.8 copy-start.2
  125.8 2.0 %collective-permute-start = (bf16[1536,128]{1,0:T(8,128)(2,1)}, bf16[1536,128]{1,0:T(8,128)(2,1)S(1)}, u32[]{:S(2)}, u32[]{:S(2)}) collective-permute-start(bf16[1536,128]{1,0:T(8,128)(2,1)} %get-tuple-element.58), channel_id=1, source_target_pairs={{0,4},{4,0},{1,5},{5,1},{2,6},{6,2},{3,7},{7,3},{8,12},{12,8},{9,1... | collective-permute-start | bytes 1179656 | tf_op jit(solution)/shard_map/ppermute | solution.py:733
  129.8 16.0 %all-to-all-start.5 = ((bf16[64,24,128]{2,1,0:T(8,128)(2,1)}), bf16[64,24,128]{2,1,0:T(8,128)(2,1)S(1)}, u32[]{:S(2)}, u32[]{:S(2)}) async-start(bf16[64,24,128]{2,1,0:T(8,128)(2,1)} %bitcast.16), calls=%async_computation.5 | async-start | bytes 786432 | tf_op jit(solution)/shard_map/all_to_all | solution.py:722
  160.5 4.5 %collective-permute-start.1 = (bf16[1536,128]{1,0:T(8,128)(2,1)S(1)}, bf16[1536,128]{1,0:T(8,128)(2,1)S(1)}, u32[]{:S(2)}, u32[]{:S(2)}) collective-permute-start(bf16[1536,128]{1,0:T(8,128)(2,1)S(1)} %bitcast.26), channel_id=1, source_target_pairs={{0,4},{4,0},{1,5},{5,1},{2,6},{6,2},{3,7},{7,3},{8,12},{12,8},{9,1... | collective-permute-start | bytes 1179656 | tf_op jit(solution)/shard_map/ppermute | solution.py:733

commit v7 on v5

--- a/solution.py
+++ b/solution.py
@@ -437,7 +437,7 @@
             (degree, n),
         ),
         (
-            (inner(struct(masters, width, dtype=F32)), n, 0),
+            (struct(masters, width, dtype=F32), n, 0),
             (struct(masters, EDGE, dtype=F32), 1, 0),
             (struct(8, asked_column.shape[0], dtype=I32), 1, 0),
         ),
@@ -486,7 +486,7 @@
         (
             (asked_row, 1),
             (inner(back), 1),
-            (inner(base), 2),
+            (base, 2),
             (scale, 2),
             (cotangent, 2),
             (asked_column, 2),
@@ -599,7 +599,7 @@
         back_far_kernel,
         (tile_count, tile_column),
         ((tiles, groups(tiles)), (turned, 1), (partial, groups(partial))),
-        ((inner(struct(masters, width, EDGE, dtype=F32)), masters // GROUP, 0),),
+        ((struct(masters, width, EDGE, dtype=F32), masters // GROUP, 0),),
         (pltpu.VMEM((mirrors // EDGE, row_blocks + 1, EDGE, EDGE), BF16),),
         flops=3e9,
     )
@@ -644,7 +644,7 @@
         (
             (inner(back), 1),
             (asked_column, 1),
-            (inner(partial), 1),
+            (partial, 1),
             (features, 1),
             (grad_self, 1),
         ),

time: 171 us -> 169 us (0.988)
  local copies, waits for them, and re-layouts: 5.83 us -> 0.02 us
  Pallas kernels: 63.5 us -> 66.8 us
    unnamed x16 -> x8, local copies, waits for them, and re-layouts: 5.83 us -> 0.02 us
    pallas_call x11, Pallas kernels: 62.1 us -> 65.5 us  [run(): pl.pallas_call(body, in_specs=[smem] * len(scalars) + specs[:n], out_spec...]
  transfers between devices with their start and end apart: 8 -> 8, of which waited for: 8 -> 8; matrix products, arithmetic and copies ran while one was open for 5% -> 5% of each run, Pallas kernels for 21% -> 22%
where the time goes in v7:
time: 169 us; the launch traced here: 168 us
  Pallas kernels  66.8 us (40%)
  starting transfers between devices  40.7 us (24%)
  waiting for transfers between devices  34.4 us (20%)
  blocking collectives  14.8 us (9%)
  matrix products  8.27 us (5%)
  other arithmetic  1.96 us (1%)
    pallas_call x11, Pallas kernels, run(): pl.pallas_call(body, in_specs=[smem] * len(scalars) + specs[:n], out_spec...  65.5 us
    all_to_all x6, starting transfers between devices, exchange(): lax.all_to_all(buffer.reshape(parts, buffer.shape[0] // parts, buffer.sha...  37.4 us
    all_to_all x6, waiting for transfers between devices, exchange(): lax.all_to_all(buffer.reshape(parts, buffer.shape[0] // parts, buffer.sha...  31.4 us
    all_to_all x1, blocking collectives, exchange(): lax.all_to_all(buffer.reshape(parts, buffer.shape[0] // parts, buffer.sha...  14.8 us
    dot_general x1, matrix products, on_device(): lax.dot_general(features, low, (((0,), (0,)), ((), ())), preferred_elemen...  3.97 us
  transfers between devices with their start and end apart: 8, of which 8 were waited for; matrix products, arithmetic and copies ran while one was open for 5% of the time, Pallas kernels for 22%

profile of v7, /device:TPU:1, one launch (start us, length us, event | category | flops | bytes accessed | tf_op | source)
XLA Modules:
  0.0 167.8 jit_solution(8462852745024249796)
XLA Ops:
  0.7 4.3 %shard_map.120 = (f32[128,128]{1,0:T(8,128)}, s32[1,512]{1,0:T(1,128)}, s32[512,128]{1,0:T(8,128)}) custom-call(s32[20]{0:T(128)} %refs_0_.7, s32[1,512]{1,0:T(1,128)} %bitcast.40, s32[1,512]{1,0:T(1,128)} %bitcast.41, bf16[20,16,128,128]{3,2,1,0:T(8,128)(2,1)} %refs_2_.6), custom_call_target="tpu_custom_call" | custom-call | flops 1000000000 | bytes 4194304 | tf_op jit(solution)/shard_map/pallas_call | solution.py:143
  5.0 12.0 %all-to-all-start = ((f32[128,1,128]{2,1,0:T(1,128)}), f32[128,1,128]{2,1,0:T(1,128)}, u32[]{:S(2)}, u32[]{:S(2)}) async-start(f32[128,1,128]{2,1,0:T(1,128)} %bitcast.36), calls=%async_computation | async-start | bytes 131072 | tf_op jit(solution)/shard_map/all_to_all | solution.py:722
  17.0 2.3 %fusion.1.refs_5_ = f32[2048,256]{1,0:T(8,128)} fusion(bf16[2048,768]{1,0:T(8,128)(2,1)S(1)} %copy-done, bf16[768,256]{1,0:T(8,128)(2,1)S(1)} %copy-done.1), kind=kOutput, calls=%fused_computation.4 | convolution fusion | flops 805306368 | bytes 5636096 | tf_op jit(solution)/shard_map/dot_general | solution.py:756
  19.3 2.0 %convolution_convert_fusion.refs_1_.refs_3_ = bf16[2048,256]{1,0:T(8,128)(2,1)} fusion(bf16[2048,768]{1,0:T(8,128)(2,1)S(1)} %copy-done, bf16[768,256]{1,0:T(8,128)(2,1)S(1)} %copy-done.2), kind=kOutput, calls=%fused_computation | convolution fusion | flops 805830656 | bytes 4587520 | tf_op jit(solution)/shard_map/dot_general | solution.py:755
  21.3 5.4 %all-to-all-done = f32[128,1,128]{2,1,0:T(1,128)} async-done(((f32[128,1,128]{2,1,0:T(1,128)}), f32[128,1,128]{2,1,0:T(1,128)}, u32[]{:S(2)}, u32[]{:S(2)}) %all-to-all-start) | async-done | bytes 65568 | tf_op jit(solution)/shard_map/all_to_all | solution.py:722
  26.7 3.3 %shard_map.121 = (bf16[1024,256]{1,0:T(8,128)(2,1)}, s32[1024,128]{1,0:T(8,128)}) custom-call(f32[128,128]{1,0:T(8,128)} %bitcast.4.refs_0_.refs_1_, bf16[2048,256]{1,0:T(8,128)(2,1)} %convolution_convert_fusion.refs_1_.refs_3_), custom_call_target="tpu_custom_call" | custom-call | flops 2000000000 | bytes 4194304 | tf_op jit(solution)/shard_map/pallas_call | solution.py:143
  30.1 4.3 %all-to-all-start.1 = ((bf16[128,8,256]{2,1,0:T(8,128)(2,1)}), bf16[128,8,256]{2,1,0:T(8,128)(2,1)S(1)}, u32[]{:S(2)}, u32[]{:S(2)}) async-start(bf16[128,8,256]{2,1,0:T(8,128)(2,1)} %bitcast.35), calls=%async_computation.1 | async-start | bytes 1048576 | tf_op jit(solution)/shard_map/all_to_all | solution.py:722
  34.4 10.4 %shard_map.122 = (f32[2560,256]{1,0:T(8,128)}, f32[2048,128]{1,0:T(8,128)}, bf16[20,4,128,128]{3,2,1,0:T(8,128)(2,1)}) custom-call(s32[20]{0:T(128)} %refs_0_.7, s32[16,20]{1,0:T(8,128)} %bitcast.37, bf16[20,16,128,128]{3,2,1,0:T(8,128)(2,1)} %refs_2_.6, bf16[2048,256]{1,0:T(8,128)(2,1)} %convolution_convert_fusion.refs_1_.refs_3_), custom_call_target="tpu_custom_call" | custom-call | flops 5000000000 | bytes 4194304 | tf_op jit(solution)/shard_map/pallas_call | solution.py:143
  44.8 3.7 %all-to-all-done.1 = bf16[128,8,256]{2,1,0:T(8,128)(2,1)S(1)} async-done(((bf16[128,8,256]{2,1,0:T(8,128)(2,1)}), bf16[128,8,256]{2,1,0:T(8,128)(2,1)S(1)}, u32[]{:S(2)}, u32[]{:S(2)}) %all-to-all-start.1) | async-done | bytes 524320 | tf_op jit(solution)/shard_map/all_to_all | solution.py:722
  48.5 3.3 %shard_map.123 = (bf16[1024,256]{1,0:T(8,128)(2,1)}, bf16[512,256]{1,0:T(8,128)(2,1)}) custom-call(bf16[1024,256]{1,0:T(8,128)(2,1)S(1)} %bitcast.31, s32[512,128]{1,0:T(8,128)} %get-tuple-element.38.refs_1_, f32[2560,256]{1,0:T(8,128)} %get-tuple-element.40.refs_2_.refs_4_, bf16[20,4,128,128]{3,2,1,0:T(8,128)(2,1)} %get-tuple-element.41.refs_3_.refs_2_, ...), custom_call_target="tpu_custom_call" | custom-call | flops 2000000000 | bytes 4194304 | tf_op jit(solution)/shard_map/pallas_call | solution.py:143
  51.9 5.9 %all-to-all-start.2 = ((bf16[128,8,256]{2,1,0:T(8,128)(2,1)}), bf16[128,8,256]{2,1,0:T(8,128)(2,1)S(1)}, u32[]{:S(2)}, u32[]{:S(2)}) async-start(bf16[128,8,256]{2,1,0:T(8,128)(2,1)} %bitcast.33), calls=%async_computation.2 | async-start | bytes 1048576 | tf_op jit(solution)/shard_map/all_to_all | solution.py:722
  57.8 6.9 %shard_map.124 = (f32[2048,256]{1,0:T(8,128)}, f32[2048,128]{1,0:T(8,128)}, s32[8,1024]{1,0:T(8,128)}) custom-call(bf16[512,256]{1,0:T(8,128)(2,1)} %get-tuple-element.43.refs_0_, f32[128,128]{1,0:T(8,128)} %bitcast.4.refs_0_.refs_1_, s32[1024,128]{1,0:T(8,128)} %get-tuple-element.44.refs_2_.refs_5_, ...), custom_call_target="tpu_custom_call" | custom-call | flops 5000000000 | bytes 4194304 | tf_op jit(solution)/shard_map/pallas_call | solution.py:143
  64.7 7.2 %all-to-all-done.2 = bf16[128,8,256]{2,1,0:T(8,128)(2,1)S(1)} async-done(((bf16[128,8,256]{2,1,0:T(8,128)(2,1)}), bf16[128,8,256]{2,1,0:T(8,128)(2,1)S(1)}, u32[]{:S(2)}, u32[]{:S(2)}) %all-to-all-start.2) | async-done | bytes 524320 | tf_op jit(solution)/shard_map/all_to_all | solution.py:722
  71.9 6.5 %shard_map.125 = (bf16[2048,256]{1,0:T(8,128)(2,1)}, bf16[2048,256]{1,0:T(8,128)(2,1)}, bf16[2048,256]{1,0:T(8,128)(2,1)}, bf16[1024,256]{1,0:T(8,128)(2,1)}) custom-call(s32[8,1024]{1,0:T(8,128)} %get-tuple-element.47.refs_0_, bf16[1024,256]{1,0:T(8,128)(2,1)S(1)} %bitcast.28, f32[2048,256]{1,0:T(8,128)} %get-tuple-element.49.refs_2_, ...), custom_call_target="tpu_custom_call" | custom-call | flops 3000000000 | bytes 4194304 | tf_op jit(solution)/shard_map/pallas_call | solution.py:143
  78.5 3.7 %all-to-all-start.3 = ((bf16[128,8,256]{2,1,0:T(8,128)(2,1)}), bf16[128,8,256]{2,1,0:T(8,128)(2,1)S(1)}, u32[]{:S(2)}, u32[]{:S(2)}) async-start(bf16[128,8,256]{2,1,0:T(8,128)(2,1)} %bitcast.32), calls=%async_computation.3 | async-start | bytes 1048576 | tf_op jit(solution)/shard_map/all_to_all | solution.py:722
  82.2 9.8 %shard_map.126.refs_3_.refs_4_ = f32[20,256,128]{2,1,0:T(8,128)} custom-call(s32[20]{0:T(128)} %refs_0_.7, s32[16,20]{1,0:T(8,128)} %bitcast.38, bf16[20,16,128,128]{3,2,1,0:T(8,128)(2,1)} %refs_2_.6, bf16[2048,256]{1,0:T(8,128)(2,1)} %get-tuple-element.53.refs_3_), custom_call_target="tpu_custom_call" | custom-call | flops 5000000000 | bytes 4194304 | tf_op jit(solution)/shard_map/pallas_call | solution.py:143
  92.0 4.5 %all-to-all-done.3 = bf16[128,8,256]{2,1,0:T(8,128)(2,1)S(1)} async-done(((bf16[128,8,256]{2,1,0:T(8,128)(2,1)}), bf16[128,8,256]{2,1,0:T(8,128)(2,1)S(1)}, u32[]{:S(2)}, u32[]{:S(2)}) %all-to-all-start.3) | async-done | bytes 524320 | tf_op jit(solution)/shard_map/all_to_all | solution.py:722
  96.5 3.6 %shard_map.127 = (bf16[1024,256]{1,0:T(8,128)(2,1)}, bf16[256,512]{1,0:T(8,128)(2,1)}) custom-call(bf16[1024,256]{1,0:T(8,128)(2,1)S(1)} %bitcast.29, s32[512,128]{1,0:T(8,128)} %get-tuple-element.38.refs_1_, bf16[20,4,128,128]{3,2,1,0:T(8,128)(2,1)} %get-tuple-element.41.refs_3_.refs_2_, f32[20,256,128]{2,1,0:T(8,128)} %shard_map.126.refs_3_.refs_4_, ...), custom_call_target="tpu_custom_call" | custom-call | flops 2000000000 | bytes 4194304 | tf_op jit(solution)/shard_map/pallas_call | solution.py:143
  100.1 5.4 %all-to-all-start.4 = ((bf16[128,8,256]{2,1,0:T(8,128)(2,1)}), bf16[128,8,256]{2,1,0:T(8,128)(2,1)S(1)}, u32[]{:S(2)}, u32[]{:S(2)}) async-start(bf16[128,8,256]{2,1,0:T(8,128)(2,1)} %bitcast.34), calls=%async_computation.4 | async-start | bytes 1048576 | tf_op jit(solution)/shard_map/all_to_all | solution.py:722
  105.5 4.0 %fusion.refs_5_ = bf16[768,256]{1,0:T(8,128)(2,1)} fusion(bf16[2048,256]{1,0:T(8,128)(2,1)S(1)} %copy-done.3, bf16[2048,768]{1,0:T(8,128)(2,1)} %refs_4_.3), kind=kOutput, calls=%fused_computation.2 | convolution fusion | flops 805502976 | bytes 4587520 | tf_op jit(solution)/shard_map/dot_general | solution.py:769
  109.4 5.6 %shard_map.128.refs_3_ = f32[16,256,128]{2,1,0:T(8,128)} custom-call(s32[20]{0:T(128)} %refs_0_.7, s32[16,20]{1,0:T(8,128)} %bitcast.39, bf16[20,16,128,128]{3,2,1,0:T(8,128)(2,1)} %refs_2_.6, bf16[256,512]{1,0:T(8,128)(2,1)} %get-tuple-element.55.refs_3_, f32[20,256,128]{2,1,0:T(8,128)} %shard_map.126.refs_3_.refs_4_), custom_call_target="tpu_custom_call" | custom-call | flops 3000000000 | bytes 4194304 | tf_op jit(solution)/shard_map/pallas_call | solution.py:143
  115.1 4.5 %all-to-all-done.4 = bf16[128,8,256]{2,1,0:T(8,128)(2,1)S(1)} async-done(((bf16[128,8,256]{2,1,0:T(8,128)(2,1)}), bf16[128,8,256]{2,1,0:T(8,128)(2,1)S(1)}, u32[]{:S(2)}, u32[]{:S(2)}) %all-to-all-start.4) | async-done | bytes 524320 | tf_op jit(solution)/shard_map/all_to_all | solution.py:722
  119.6 6.8 %shard_map.129 = (bf16[256,2048]{1,0:T(8,128)(2,1)}, f32[1536,128]{1,0:T(8,128)}, bf16[1536,128]{1,0:T(8,128)(2,1)}) custom-call(s32[1]{0:T(128)} %bitcast.10.refs_0_.core, bf16[1024,256]{1,0:T(8,128)(2,1)S(1)} %bitcast.30, s32[1024,128]{1,0:T(8,128)} %get-tuple-element.44.refs_2_.refs_5_, f32[16,256,128]{2,1,0:T(8,128)} %shard_map.128.refs_3_, ...), custom_call_target="tpu_custom_call" | custom-call | flops 3000000000 | bytes 4194304 | tf_op jit(solution)/shard_map/pallas_call | solution.py:143
  126.8 1.7 collective-permute-done
  128.4 2.0 %add_convert_fusion = bf16[1536,128]{1,0:T(8,128)(2,1)} fusion(f32[1536,128]{1,0:T(8,128)} %get-tuple-element.57, bf16[1536,128]{1,0:T(8,128)(2,1)S(1)} %collective-permute-done), kind=kLoop, calls=%fused_computation.3 | loop fusion | flops 589824 | bytes 1572864 | tf_op jit(solution)/shard_map/convert_element_type | solution.py:776
  130.4 6.1 %all-to-all-start.5 = ((bf16[64,24,128]{2,1,0:T(8,128)(2,1)}), bf16[64,24,128]{2,1,0:T(8,128)(2,1)S(1)}, u32[]{:S(2)}, u32[]{:S(2)}) async-start(bf16[64,24,128]{2,1,0:T(8,128)(2,1)} %bitcast.16), calls=%async_computation.5 | async-start | bytes 786432 | tf_op jit(solution)/shard_map/all_to_all | solution.py:722
  136.5 4.8 %shard_map.130 = bf16[2048,768]{1,0:T(8,128)(2,1)} custom-call(bf16[2048,256]{1,0:T(8,128)(2,1)} %get-tuple-element.56.refs_0_, bf16[256,2048]{1,0:T(8,128)(2,1)} %get-tuple-element.59.refs_1_, bf16[768,256]{1,0:T(8,128)(2,1)} %refs_2_.7, bf16[768,256]{1,0:T(8,128)(2,1)} %refs_3_.3), custom_call_target="tpu_custom_call" | custom-call | flops 3000000000 | bytes 4194304 | tf_op jit(solution)/shard_map/pallas_call | solution.py:143
  141.3 6.0 %all-to-all-done.5.parts = bf16[64,24,128]{2,1,0:T(8,128)(2,1)S(1)} async-done(((bf16[64,24,128]{2,1,0:T(8,128)(2,1)}), bf16[64,24,128]{2,1,0:T(8,128)(2,1)S(1)}, u32[]{:S(2)}, u32[]{:S(2)}) %all-to-all-start.5) | async-done | bytes 393248 | tf_op jit(solution)/shard_map/all_to_all | solution.py:722
  147.4 14.8 %all_to_all.35 = bf16[64,24,128]{2,1,0:T(8,128)(2,1)S(1)} all-to-all(bf16[64,24,128]{2,1,0:T(8,128)(2,1)S(1)} %shard_map.131), channel_id=1, replica_groups=mesh['chip'=16,'core'=2,'local'=4] {'chip','local'}, dimensions={0} | all-to-all | bytes 786432 | tf_op jit(solution)/shard_map/all_to_all | solution.py:722
  162.2 2.9 %collective-permute-start.1 = (bf16[1536,128]{1,0:T(8,128)(2,1)S(1)}, bf16[1536,128]{1,0:T(8,128)(2,1)S(1)}, u32[]{:S(2)}, u32[]{:S(2)}) collective-permute-start(bf16[1536,128]{1,0:T(8,128)(2,1)S(1)} %bitcast.26), channel_id=1, source_target_pairs={{0,4},{4,0},{1,5},{5,1},{2,6},{6,2},{3,7},{7,3},{8,12},{12,8},{9,1... | collective-permute-start | bytes 1179656 | tf_op jit(solution)/shard_map/ppermute | solution.py:733
  165.2 1.3 collective-permute-done.1.other
  166.5 1.3 shard_map.132
  (10 shorter events, 0.5 us)
Async XLA Ops:
  0.6 16.3 %copy-start = (bf16[2048,768]{1,0:T(8,128)(2,1)S(1)}, bf16[2048,768]{1,0:T(8,128)(2,1)}, u32[]{:S(2)}) copy-start(bf16[2048,768]{1,0:T(8,128)(2,1)} %refs_4_.3) | copy-start | bytes 9437188
  0.6 16.3 %copy-start.1 = (bf16[768,256]{1,0:T(8,128)(2,1)S(1)}, bf16[768,256]{1,0:T(8,128)(2,1)}, u32[]{:S(2)}) copy-start(bf16[768,256]{1,0:T(8,128)(2,1)} %refs_2_.7) | copy-start | bytes 1179652
  5.0 21.7 %all-to-all-start = ((f32[128,1,128]{2,1,0:T(1,128)}), f32[128,1,128]{2,1,0:T(1,128)}, u32[]{:S(2)}, u32[]{:S(2)}) async-start(f32[128,1,128]{2,1,0:T(1,128)} %bitcast.36), calls=%async_computation | async-start | bytes 131072 | tf_op jit(solution)/shard_map/all_to_all | solution.py:722
  17.0 2.4 %copy-start.2 = (bf16[768,256]{1,0:T(8,128)(2,1)S(1)}, bf16[768,256]{1,0:T(8,128)(2,1)}, u32[]{:S(2)}) copy-start(bf16[768,256]{1,0:T(8,128)(2,1)} %refs_3_.3) | copy-start | bytes 1179652
  30.1 18.5 %all-to-all-start.1 = ((bf16[128,8,256]{2,1,0:T(8,128)(2,1)}), bf16[128,8,256]{2,1,0:T(8,128)(2,1)S(1)}, u32[]{:S(2)}, u32[]{:S(2)}) async-start(bf16[128,8,256]{2,1,0:T(8,128)(2,1)} %bitcast.35), calls=%async_computation.1 | async-start | bytes 1048576 | tf_op jit(solution)/shard_map/all_to_all | solution.py:722
  51.9 20.1 %all-to-all-start.2 = ((bf16[128,8,256]{2,1,0:T(8,128)(2,1)}), bf16[128,8,256]{2,1,0:T(8,128)(2,1)S(1)}, u32[]{:S(2)}, u32[]{:S(2)}) async-start(bf16[128,8,256]{2,1,0:T(8,128)(2,1)} %bitcast.33), calls=%async_computation.2 | async-start | bytes 1048576 | tf_op jit(solution)/shard_map/all_to_all | solution.py:722
  78.5 18.0 %all-to-all-start.3 = ((bf16[128,8,256]{2,1,0:T(8,128)(2,1)}), bf16[128,8,256]{2,1,0:T(8,128)(2,1)S(1)}, u32[]{:S(2)}, u32[]{:S(2)}) async-start(bf16[128,8,256]{2,1,0:T(8,128)(2,1)} %bitcast.32), calls=%async_computation.3 | async-start | bytes 1048576 | tf_op jit(solution)/shard_map/all_to_all | solution.py:722
  96.5 9.0 %copy-start.3 = (bf16[2048,256]{1,0:T(8,128)(2,1)S(1)}, bf16[2048,256]{1,0:T(8,128)(2,1)}, u32[]{:S(2)}) copy-start(bf16[2048,256]{1,0:T(8,128)(2,1)} %get-tuple-element.56.refs_0_) | copy-start | bytes 3145732
  100.1 19.5 %all-to-all-start.4 = ((bf16[128,8,256]{2,1,0:T(8,128)(2,1)}), bf16[128,8,256]{2,1,0:T(8,128)(2,1)S(1)}, u32[]{:S(2)}, u32[]{:S(2)}) async-start(bf16[128,8,256]{2,1,0:T(8,128)(2,1)} %bitcast.34), calls=%async_computation.4 | async-start | bytes 1048576 | tf_op jit(solution)/shard_map/all_to_all | solution.py:722
  126.4 2.0 %collective-permute-start = (bf16[1536,128]{1,0:T(8,128)(2,1)}, bf16[1536,128]{1,0:T(8,128)(2,1)S(1)}, u32[]{:S(2)}, u32[]{:S(2)}) collective-permute-start(bf16[1536,128]{1,0:T(8,128)(2,1)} %get-tuple-element.58), channel_id=1, source_target_pairs={{0,4},{4,0},{1,5},{5,1},{2,6},{6,2},{3,7},{7,3},{8,12},{12,8},{9,1... | collective-permute-start | bytes 1179656 | tf_op jit(solution)/shard_map/ppermute | solution.py:733
  130.4 16.9 %all-to-all-start.5 = ((bf16[64,24,128]{2,1,0:T(8,128)(2,1)}), bf16[64,24,128]{2,1,0:T(8,128)(2,1)S(1)}, u32[]{:S(2)}, u32[]{:S(2)}) async-start(bf16[64,24,128]{2,1,0:T(8,128)(2,1)} %bitcast.16), calls=%async_computation.5 | async-start | bytes 786432 | tf_op jit(solution)/shard_map/all_to_all | solution.py:722
  162.2 4.3 %collective-permute-start.1 = (bf16[1536,128]{1,0:T(8,128)(2,1)S(1)}, bf16[1536,128]{1,0:T(8,128)(2,1)S(1)}, u32[]{:S(2)}, u32[]{:S(2)}) collective-permute-start(bf16[1536,128]{1,0:T(8,128)(2,1)S(1)} %bitcast.26), channel_id=1, source_target_pairs={{0,4},{4,0},{1,5},{5,1},{2,6},{6,2},{3,7},{7,3},{8,12},{12,8},{9,1... | collective-permute-start | bytes 1179656 | tf_op jit(solution)/shard_map/ppermute | solution.py:733

commit v8 on v7

--- a/solution.py
+++ b/solution.py
@@ -599,7 +599,7 @@
         back_far_kernel,
         (tile_count, tile_column),
         ((tiles, groups(tiles)), (turned, 1), (partial, groups(partial))),
-        ((struct(masters, width, EDGE, dtype=F32), masters // GROUP, 0),),
+        ((inner(struct(masters, width, EDGE, dtype=F32)), masters // GROUP, 0),),
         (pltpu.VMEM((mirrors // EDGE, row_blocks + 1, EDGE, EDGE), BF16),),
         flops=3e9,
     )
@@ -642,9 +642,9 @@
         finish_kernel,
         (core,),
         (
-            (inner(back), 1),
+            (back, 1),
             (asked_column, 1),
-            (partial, 1),
+            (inner(partial), 1),
             (features, 1),
             (grad_self, 1),
         ),
@@ -770,7 +770,7 @@
         features, low, (((0,), (0,)), ((), ())), preferred_element_type=F32
     ).astype(BF16)
     send, turned = mirror_back(arrived, slot_column, slot_row, partial, far_tiles)
-    back = exchange(send)
+    back = pltpu.with_memory_space_constraint(exchange(send), pltpu.HBM)
     partial = back_far(tile_count, tile_column, tile_weight, turned, partial)
     d_projected, keep, give = finish(core, partial, back, asked_column, features, grad_self)
     pair = (keep + to_other_core(give).astype(F32)).astype(BF16)

time: 169 us -> 167 us (0.988)
  Pallas kernels: 66.8 us -> 63.1 us
  waiting for transfers between devices: 34.4 us -> 36.8 us
    pallas_call x11, Pallas kernels: 65.5 us -> 61.7 us  [run(): pl.pallas_call(body, in_specs=[smem] * len(scalars) + specs[:n], out_spec...]
    all_to_all x6, waiting for transfers between devices: 31.4 us -> 33.7 us  [exchange(): lax.all_to_all(buffer.reshape(parts, buffer.shape[0] // parts, buffer.sha...]
  transfers between devices with their start and end apart: 8 -> 8, of which waited for: 8 -> 8; matrix products, arithmetic and copies ran while one was open for 5% -> 5% of each run, Pallas kernels for 22% -> 21%
where the time goes in v8:
time: 167 us; the launch traced here: 166 us
  Pallas kernels  63.1 us (38%)
  starting transfers between devices  39.4 us (24%)
  waiting for transfers between devices  36.8 us (22%)
  blocking collectives  14.6 us (9%)
  matrix products  8.27 us (5%)
  other arithmetic  1.96 us (1%)
    pallas_call x11, Pallas kernels, run(): pl.pallas_call(body, in_specs=[smem] * len(scalars) + specs[:n], out_spec...  61.7 us
    all_to_all x6, starting transfers between devices, exchange(): lax.all_to_all(buffer.reshape(parts, buffer.shape[0] // parts, buffer.sha...  35.9 us
    all_to_all x6, waiting for transfers between devices, exchange(): lax.all_to_all(buffer.reshape(parts, buffer.shape[0] // parts, buffer.sha...  33.7 us
    all_to_all x1, blocking collectives, exchange(): lax.all_to_all(buffer.reshape(parts, buffer.shape[0] // parts, buffer.sha...  14.6 us
    dot_general x1, matrix products, on_device(): lax.dot_general(features, low, (((0,), (0,)), ((), ())), preferred_elemen...  3.97 us
    ppermute x2, starting transfers between devices, to_other_core(): return lax.ppermute(value, 'core', [(0, 1), (1, 0)])  3.53 us
  transfers between devices with their start and end apart: 8, of which 8 were waited for; matrix products, arithmetic and copies ran while one was open for 5% of the time, Pallas kernels for 21%

profile of v8, /device:TPU:1, one launch (start us, length us, event | category | flops | bytes accessed | tf_op | source)
XLA Modules:
  0.0 165.8 jit_solution(1674208593409815230)
XLA Ops:
  0.7 4.3 %shard_map.120 = (f32[128,128]{1,0:T(8,128)}, s32[1,512]{1,0:T(1,128)}, s32[512,128]{1,0:T(8,128)}) custom-call(s32[20]{0:T(128)} %refs_0_.7, s32[1,512]{1,0:T(1,128)} %bitcast.40, s32[1,512]{1,0:T(1,128)} %bitcast.41, bf16[20,16,128,128]{3,2,1,0:T(8,128)(2,1)} %refs_2_.6), custom_call_target="tpu_custom_call" | custom-call | flops 1000000000 | bytes 4194304 | tf_op jit(solution)/shard_map/pallas_call | solution.py:143
  5.0 12.0 %all-to-all-start = ((f32[128,1,128]{2,1,0:T(1,128)}), f32[128,1,128]{2,1,0:T(1,128)}, u32[]{:S(2)}, u32[]{:S(2)}) async-start(f32[128,1,128]{2,1,0:T(1,128)} %bitcast.36), calls=%async_computation | async-start | bytes 131072 | tf_op jit(solution)/shard_map/all_to_all | solution.py:722
  17.0 2.3 %fusion.1.refs_5_ = f32[2048,256]{1,0:T(8,128)} fusion(bf16[2048,768]{1,0:T(8,128)(2,1)S(1)} %copy-done, bf16[768,256]{1,0:T(8,128)(2,1)S(1)} %copy-done.2), kind=kOutput, calls=%fused_computation.4 | convolution fusion | flops 805306368 | bytes 5636096 | tf_op jit(solution)/shard_map/dot_general | solution.py:756
  19.3 2.0 %convolution_convert_fusion.refs_1_.refs_3_ = bf16[2048,256]{1,0:T(8,128)(2,1)} fusion(bf16[2048,768]{1,0:T(8,128)(2,1)S(1)} %copy-done, bf16[768,256]{1,0:T(8,128)(2,1)S(1)} %copy-done.3), kind=kOutput, calls=%fused_computation | convolution fusion | flops 805830656 | bytes 4587520 | tf_op jit(solution)/shard_map/dot_general | solution.py:755
  21.3 5.6 %all-to-all-done = f32[128,1,128]{2,1,0:T(1,128)} async-done(((f32[128,1,128]{2,1,0:T(1,128)}), f32[128,1,128]{2,1,0:T(1,128)}, u32[]{:S(2)}, u32[]{:S(2)}) %all-to-all-start) | async-done | bytes 65568 | tf_op jit(solution)/shard_map/all_to_all | solution.py:722
  26.9 3.3 %shard_map.121 = (bf16[1024,256]{1,0:T(8,128)(2,1)}, s32[1024,128]{1,0:T(8,128)}) custom-call(f32[128,128]{1,0:T(8,128)} %bitcast.4.refs_0_.refs_1_, bf16[2048,256]{1,0:T(8,128)(2,1)} %convolution_convert_fusion.refs_1_.refs_3_), custom_call_target="tpu_custom_call" | custom-call | flops 2000000000 | bytes 4194304 | tf_op jit(solution)/shard_map/pallas_call | solution.py:143
  30.2 4.2 %all-to-all-start.1 = ((bf16[128,8,256]{2,1,0:T(8,128)(2,1)}), bf16[128,8,256]{2,1,0:T(8,128)(2,1)S(1)}, u32[]{:S(2)}, u32[]{:S(2)}) async-start(bf16[128,8,256]{2,1,0:T(8,128)(2,1)} %bitcast.35), calls=%async_computation.1 | async-start | bytes 1048576 | tf_op jit(solution)/shard_map/all_to_all | solution.py:722
  34.4 9.5 %shard_map.122 = (f32[2560,256]{1,0:T(8,128)}, f32[2048,128]{1,0:T(8,128)}, bf16[20,4,128,128]{3,2,1,0:T(8,128)(2,1)}) custom-call(s32[20]{0:T(128)} %refs_0_.7, s32[16,20]{1,0:T(8,128)} %bitcast.37, bf16[20,16,128,128]{3,2,1,0:T(8,128)(2,1)} %refs_2_.6, bf16[2048,256]{1,0:T(8,128)(2,1)} %convolution_convert_fusion.refs_1_.refs_3_), custom_call_target="tpu_custom_call" | custom-call | flops 5000000000 | bytes 4194304 | tf_op jit(solution)/shard_map/pallas_call | solution.py:143
  43.9 4.6 %all-to-all-done.1 = bf16[128,8,256]{2,1,0:T(8,128)(2,1)S(1)} async-done(((bf16[128,8,256]{2,1,0:T(8,128)(2,1)}), bf16[128,8,256]{2,1,0:T(8,128)(2,1)S(1)}, u32[]{:S(2)}, u32[]{:S(2)}) %all-to-all-start.1) | async-done | bytes 524320 | tf_op jit(solution)/shard_map/all_to_all | solution.py:722
  48.5 3.3 %shard_map.123 = (bf16[1024,256]{1,0:T(8,128)(2,1)}, bf16[512,256]{1,0:T(8,128)(2,1)}) custom-call(bf16[1024,256]{1,0:T(8,128)(2,1)S(1)} %bitcast.30, s32[512,128]{1,0:T(8,128)} %get-tuple-element.38.refs_1_, f32[2560,256]{1,0:T(8,128)} %get-tuple-element.40.refs_2_.refs_4_, bf16[20,4,128,128]{3,2,1,0:T(8,128)(2,1)} %get-tuple-element.41.refs_3_.refs_2_, ...), custom_call_target="tpu_custom_call" | custom-call | flops 2000000000 | bytes 4194304 | tf_op jit(solution)/shard_map/pallas_call | solution.py:143
  51.9 5.6 %all-to-all-start.2 = ((bf16[128,8,256]{2,1,0:T(8,128)(2,1)}), bf16[128,8,256]{2,1,0:T(8,128)(2,1)S(1)}, u32[]{:S(2)}, u32[]{:S(2)}) async-start(bf16[128,8,256]{2,1,0:T(8,128)(2,1)} %bitcast.33), calls=%async_computation.2 | async-start | bytes 1048576 | tf_op jit(solution)/shard_map/all_to_all | solution.py:722
  57.5 6.9 %shard_map.124 = (f32[2048,256]{1,0:T(8,128)}, f32[2048,128]{1,0:T(8,128)}, s32[8,1024]{1,0:T(8,128)}) custom-call(bf16[512,256]{1,0:T(8,128)(2,1)} %get-tuple-element.43.refs_0_, f32[128,128]{1,0:T(8,128)} %bitcast.4.refs_0_.refs_1_, s32[1024,128]{1,0:T(8,128)} %get-tuple-element.44.refs_2_.refs_5_, ...), custom_call_target="tpu_custom_call" | custom-call | flops 5000000000 | bytes 4194304 | tf_op jit(solution)/shard_map/pallas_call | solution.py:143
  64.4 7.2 %all-to-all-done.2 = bf16[128,8,256]{2,1,0:T(8,128)(2,1)S(1)} async-done(((bf16[128,8,256]{2,1,0:T(8,128)(2,1)}), bf16[128,8,256]{2,1,0:T(8,128)(2,1)S(1)}, u32[]{:S(2)}, u32[]{:S(2)}) %all-to-all-start.2) | async-done | bytes 524320 | tf_op jit(solution)/shard_map/all_to_all | solution.py:722
  71.6 6.5 %shard_map.125 = (bf16[2048,256]{1,0:T(8,128)(2,1)}, bf16[2048,256]{1,0:T(8,128)(2,1)}, bf16[2048,256]{1,0:T(8,128)(2,1)}, bf16[1024,256]{1,0:T(8,128)(2,1)}) custom-call(s32[8,1024]{1,0:T(8,128)} %get-tuple-element.47.refs_0_, bf16[1024,256]{1,0:T(8,128)(2,1)S(1)} %bitcast.28, f32[2048,256]{1,0:T(8,128)} %get-tuple-element.49.refs_2_, ...), custom_call_target="tpu_custom_call" | custom-call | flops 3000000000 | bytes 4194304 | tf_op jit(solution)/shard_map/pallas_call | solution.py:143
  78.2 3.7 %all-to-all-start.3 = ((bf16[128,8,256]{2,1,0:T(8,128)(2,1)}), bf16[128,8,256]{2,1,0:T(8,128)(2,1)S(1)}, u32[]{:S(2)}, u32[]{:S(2)}) async-start(bf16[128,8,256]{2,1,0:T(8,128)(2,1)} %bitcast.31), calls=%async_computation.3 | async-start | bytes 1048576 | tf_op jit(solution)/shard_map/all_to_all | solution.py:722
  81.8 9.5 %shard_map.126.refs_3_.refs_4_ = f32[20,256,128]{2,1,0:T(8,128)} custom-call(s32[20]{0:T(128)} %refs_0_.7, s32[16,20]{1,0:T(8,128)} %bitcast.38, bf16[20,16,128,128]{3,2,1,0:T(8,128)(2,1)} %refs_2_.6, bf16[2048,256]{1,0:T(8,128)(2,1)} %get-tuple-element.53.refs_3_), custom_call_target="tpu_custom_call" | custom-call | flops 5000000000 | bytes 4194304 | tf_op jit(solution)/shard_map/pallas_call | solution.py:143
  91.3 4.8 %all-to-all-done.3 = bf16[128,8,256]{2,1,0:T(8,128)(2,1)S(1)} async-done(((bf16[128,8,256]{2,1,0:T(8,128)(2,1)}), bf16[128,8,256]{2,1,0:T(8,128)(2,1)S(1)}, u32[]{:S(2)}, u32[]{:S(2)}) %all-to-all-start.3) | async-done | bytes 524320 | tf_op jit(solution)/shard_map/all_to_all | solution.py:722
  96.1 3.6 %shard_map.127 = (bf16[1024,256]{1,0:T(8,128)(2,1)}, bf16[256,512]{1,0:T(8,128)(2,1)}) custom-call(bf16[1024,256]{1,0:T(8,128)(2,1)S(1)} %bitcast.29, s32[512,128]{1,0:T(8,128)} %get-tuple-element.38.refs_1_, bf16[20,4,128,128]{3,2,1,0:T(8,128)(2,1)} %get-tuple-element.41.refs_3_.refs_2_, f32[20,256,128]{2,1,0:T(8,128)} %shard_map.126.refs_3_.refs_4_, ...), custom_call_target="tpu_custom_call" | custom-call | flops 2000000000 | bytes 4194304 | tf_op jit(solution)/shard_map/pallas_call | solution.py:143
  99.7 5.2 %all-to-all-start.4 = ((bf16[128,8,256]{2,1,0:T(8,128)(2,1)}), bf16[128,8,256]{2,1,0:T(8,128)(2,1)S(1)}, u32[]{:S(2)}, u32[]{:S(2)}) async-start(bf16[128,8,256]{2,1,0:T(8,128)(2,1)} %bitcast.34), calls=%async_computation.4 | async-start | bytes 1048576 | tf_op jit(solution)/shard_map/all_to_all | solution.py:722
  105.0 4.0 %fusion.refs_5_ = bf16[768,256]{1,0:T(8,128)(2,1)} fusion(bf16[2048,256]{1,0:T(8,128)(2,1)S(1)} %copy-done.4, bf16[2048,768]{1,0:T(8,128)(2,1)} %refs_4_.3), kind=kOutput, calls=%fused_computation.2 | convolution fusion | flops 805502976 | bytes 4587520 | tf_op jit(solution)/shard_map/dot_general | solution.py:769
  108.9 4.6 %shard_map.128.refs_3_ = f32[16,256,128]{2,1,0:T(8,128)S(1)} custom-call(s32[20]{0:T(128)} %refs_0_.7, s32[16,20]{1,0:T(8,128)} %bitcast.39, bf16[20,16,128,128]{3,2,1,0:T(8,128)(2,1)} %refs_2_.6, bf16[256,512]{1,0:T(8,128)(2,1)} %get-tuple-element.55.refs_3_, f32[20,256,128]{2,1,0:T(8,128)} %shard_map.126.refs_3_.refs_4_), custom_call_target="tpu_custom_call" | custom-call | flops 3000000000 | bytes 4194304 | tf_op jit(solution)/shard_map/pallas_call | solution.py:143
  113.5 5.6 %all-to-all-done.4 = bf16[128,8,256]{2,1,0:T(8,128)(2,1)S(1)} async-done(((bf16[128,8,256]{2,1,0:T(8,128)(2,1)}), bf16[128,8,256]{2,1,0:T(8,128)(2,1)S(1)}, u32[]{:S(2)}, u32[]{:S(2)}) %all-to-all-start.4) | async-done | bytes 524320 | tf_op jit(solution)/shard_map/all_to_all | solution.py:722
  119.9 5.3 %shard_map.129 = (bf16[256,2048]{1,0:T(8,128)(2,1)}, f32[1536,128]{1,0:T(8,128)}, bf16[1536,128]{1,0:T(8,128)(2,1)}) custom-call(s32[1]{0:T(128)} %bitcast.10.refs_0_.core, bf16[1024,256]{1,0:T(8,128)(2,1)} %bitcast.32, s32[1024,128]{1,0:T(8,128)} %get-tuple-element.44.refs_2_.refs_5_, f32[16,256,128]{2,1,0:T(8,128)S(1)} %shard_map.128.refs_3_, ...), custom_call_target="tpu_custom_call" | custom-call | flops 3000000000 | bytes 4194304 | tf_op jit(solution)/shard_map/pallas_call | solution.py:143
  125.6 1.7 %collective-permute-done = bf16[1536,128]{1,0:T(8,128)(2,1)S(1)} collective-permute-done((bf16[1536,128]{1,0:T(8,128)(2,1)}, bf16[1536,128]{1,0:T(8,128)(2,1)S(1)}, u32[]{:S(2)}, u32[]{:S(2)}) %collective-permute-start) | collective-permute-done | bytes 393248 | tf_op jit(solution)/shard_map/ppermute | solution.py:733
  127.2 2.0 %add_convert_fusion = bf16[1536,128]{1,0:T(8,128)(2,1)} fusion(f32[1536,128]{1,0:T(8,128)} %get-tuple-element.57, bf16[1536,128]{1,0:T(8,128)(2,1)S(1)} %collective-permute-done), kind=kLoop, calls=%fused_computation.3 | loop fusion | flops 589824 | bytes 1572864 | tf_op jit(solution)/shard_map/convert_element_type | solution.py:776
  129.2 5.3 %all-to-all-start.5 = ((bf16[64,24,128]{2,1,0:T(8,128)(2,1)}), bf16[64,24,128]{2,1,0:T(8,128)(2,1)S(1)}, u32[]{:S(2)}, u32[]{:S(2)}) async-start(bf16[64,24,128]{2,1,0:T(8,128)(2,1)} %bitcast.16), calls=%async_computation.5 | async-start | bytes 786432 | tf_op jit(solution)/shard_map/all_to_all | solution.py:722
  134.5 4.8 %shard_map.130 = bf16[2048,768]{1,0:T(8,128)(2,1)} custom-call(bf16[2048,256]{1,0:T(8,128)(2,1)} %get-tuple-element.56.refs_0_, bf16[256,2048]{1,0:T(8,128)(2,1)} %get-tuple-element.59.refs_1_, bf16[768,256]{1,0:T(8,128)(2,1)} %refs_2_.7, bf16[768,256]{1,0:T(8,128)(2,1)} %refs_3_.3), custom_call_target="tpu_custom_call" | custom-call | flops 3000000000 | bytes 4194304 | tf_op jit(solution)/shard_map/pallas_call | solution.py:143
  139.3 5.9 %all-to-all-done.5.parts = bf16[64,24,128]{2,1,0:T(8,128)(2,1)S(1)} async-done(((bf16[64,24,128]{2,1,0:T(8,128)(2,1)}), bf16[64,24,128]{2,1,0:T(8,128)(2,1)S(1)}, u32[]{:S(2)}, u32[]{:S(2)}) %all-to-all-start.5) | async-done | bytes 393248 | tf_op jit(solution)/shard_map/all_to_all | solution.py:722
  145.3 14.6 %all_to_all.35 = bf16[64,24,128]{2,1,0:T(8,128)(2,1)S(1)} all-to-all(bf16[64,24,128]{2,1,0:T(8,128)(2,1)S(1)} %shard_map.131), channel_id=1, replica_groups=mesh['chip'=16,'core'=2,'local'=4] {'chip','local'}, dimensions={0} | all-to-all | bytes 786432 | tf_op jit(solution)/shard_map/all_to_all | solution.py:722
  159.9 3.2 %collective-permute-start.1 = (bf16[1536,128]{1,0:T(8,128)(2,1)S(1)}, bf16[1536,128]{1,0:T(8,128)(2,1)S(1)}, u32[]{:S(2)}, u32[]{:S(2)}) collective-permute-start(bf16[1536,128]{1,0:T(8,128)(2,1)S(1)} %bitcast.26), channel_id=1, source_target_pairs={{0,4},{4,0},{1,5},{5,1},{2,6},{6,2},{3,7},{7,3},{8,12},{12,8},{9,1... | collective-permute-start | bytes 1179656 | tf_op jit(solution)/shard_map/ppermute | solution.py:733
  163.1 1.3 collective-permute-done.1.other
  164.5 1.3 shard_map.132
  (12 shorter events, 1.2 us)
Async XLA Ops:
  0.6 16.3 %copy-start = (bf16[2048,768]{1,0:T(8,128)(2,1)S(1)}, bf16[2048,768]{1,0:T(8,128)(2,1)}, u32[]{:S(2)}) copy-start(bf16[2048,768]{1,0:T(8,128)(2,1)} %refs_4_.3) | copy-start | bytes 9437188
  0.6 16.3 %copy-start.2 = (bf16[768,256]{1,0:T(8,128)(2,1)S(1)}, bf16[768,256]{1,0:T(8,128)(2,1)}, u32[]{:S(2)}) copy-start(bf16[768,256]{1,0:T(8,128)(2,1)} %refs_2_.7) | copy-start | bytes 1179652
  5.0 21.9 %all-to-all-start = ((f32[128,1,128]{2,1,0:T(1,128)}), f32[128,1,128]{2,1,0:T(1,128)}, u32[]{:S(2)}, u32[]{:S(2)}) async-start(f32[128,1,128]{2,1,0:T(1,128)} %bitcast.36), calls=%async_computation | async-start | bytes 131072 | tf_op jit(solution)/shard_map/all_to_all | solution.py:722
  17.0 2.4 %copy-start.3 = (bf16[768,256]{1,0:T(8,128)(2,1)S(1)}, bf16[768,256]{1,0:T(8,128)(2,1)}, u32[]{:S(2)}) copy-start(bf16[768,256]{1,0:T(8,128)(2,1)} %refs_3_.3) | copy-start | bytes 1179652
  30.2 18.3 %all-to-all-start.1 = ((bf16[128,8,256]{2,1,0:T(8,128)(2,1)}), bf16[128,8,256]{2,1,0:T(8,128)(2,1)S(1)}, u32[]{:S(2)}, u32[]{:S(2)}) async-start(bf16[128,8,256]{2,1,0:T(8,128)(2,1)} %bitcast.35), calls=%async_computation.1 | async-start | bytes 1048576 | tf_op jit(solution)/shard_map/all_to_all | solution.py:722
  51.9 19.7 %all-to-all-start.2 = ((bf16[128,8,256]{2,1,0:T(8,128)(2,1)}), bf16[128,8,256]{2,1,0:T(8,128)(2,1)S(1)}, u32[]{:S(2)}, u32[]{:S(2)}) async-start(bf16[128,8,256]{2,1,0:T(8,128)(2,1)} %bitcast.33), calls=%async_computation.2 | async-start | bytes 1048576 | tf_op jit(solution)/shard_map/all_to_all | solution.py:722
  78.2 18.0 %all-to-all-start.3 = ((bf16[128,8,256]{2,1,0:T(8,128)(2,1)}), bf16[128,8,256]{2,1,0:T(8,128)(2,1)S(1)}, u32[]{:S(2)}, u32[]{:S(2)}) async-start(bf16[128,8,256]{2,1,0:T(8,128)(2,1)} %bitcast.31), calls=%async_computation.3 | async-start | bytes 1048576 | tf_op jit(solution)/shard_map/all_to_all | solution.py:722
  96.1 8.8 %copy-start.4 = (bf16[2048,256]{1,0:T(8,128)(2,1)S(1)}, bf16[2048,256]{1,0:T(8,128)(2,1)}, u32[]{:S(2)}) copy-start(bf16[2048,256]{1,0:T(8,128)(2,1)} %get-tuple-element.56.refs_0_) | copy-start | bytes 3145732
  99.7 19.4 %all-to-all-start.4 = ((bf16[128,8,256]{2,1,0:T(8,128)(2,1)}), bf16[128,8,256]{2,1,0:T(8,128)(2,1)S(1)}, u32[]{:S(2)}, u32[]{:S(2)}) async-start(bf16[128,8,256]{2,1,0:T(8,128)(2,1)} %bitcast.34), calls=%async_computation.4 | async-start | bytes 1048576 | tf_op jit(solution)/shard_map/all_to_all | solution.py:722
  119.1 0.8 copy-start.1
  125.2 2.0 %collective-permute-start = (bf16[1536,128]{1,0:T(8,128)(2,1)}, bf16[1536,128]{1,0:T(8,128)(2,1)S(1)}, u32[]{:S(2)}, u32[]{:S(2)}) collective-permute-start(bf16[1536,128]{1,0:T(8,128)(2,1)} %get-tuple-element.58), channel_id=1, source_target_pairs={{0,4},{4,0},{1,5},{5,1},{2,6},{6,2},{3,7},{7,3},{8,12},{12,8},{9,1... | collective-permute-start | bytes 1179656 | tf_op jit(solution)/shard_map/ppermute | solution.py:733
  129.2 16.0 %all-to-all-start.5 = ((bf16[64,24,128]{2,1,0:T(8,128)(2,1)}), bf16[64,24,128]{2,1,0:T(8,128)(2,1)S(1)}, u32[]{:S(2)}, u32[]{:S(2)}) async-start(bf16[64,24,128]{2,1,0:T(8,128)(2,1)} %bitcast.16), calls=%async_computation.5 | async-start | bytes 786432 | tf_op jit(solution)/shard_map/all_to_all | solution.py:722
  159.9 4.5 %collective-permute-start.1 = (bf16[1536,128]{1,0:T(8,128)(2,1)S(1)}, bf16[1536,128]{1,0:T(8,128)(2,1)S(1)}, u32[]{:S(2)}, u32[]{:S(2)}) collective-permute-start(bf16[1536,128]{1,0:T(8,128)(2,1)S(1)} %bitcast.26), channel_id=1, source_target_pairs={{0,4},{4,0},{1,5},{5,1},{2,6},{6,2},{3,7},{7,3},{8,12},{12,8},{9,1... | collective-permute-start | bytes 1179656 | tf_op jit(solution)/shard_map/ppermute | solution.py:733
